TPU v7x, 32 devices: a whole 2x2x4 slice. The times are simulated.
32 devices in a mesh: scene: 2 (over y), aper: 8 (over z, x), range: 2 (over core).
Axes of the slice: x: 2, y: 2, z: 4, core: 2. Of those that a mesh axis runs over, the one named last changes fastest.
Arguments:
- images: bfloat16 [16, 2, 512, 256], P(('scene', 'aper'), None, None, 'range'), parts along dimension 0, may hold values from -6 to 6
- interp_matrix: bfloat16 [1024, 512], replicated, may hold values from -0.25 to 0.25
- offsets: int32 [3, 2, 1024], replicated, may hold values from -28 to 28, as said below
- tap_index: int32 [3, 2, 1024], replicated, may hold values from 0 to 15
- tap_table: float32 [16, 8], replicated, may hold values from -1.5 to 1.5
- phase_base: float32 [3, 2, 1024], replicated, may hold values from -3.140625 to 3.140625
- phase_slope: float32 [3, 2, 1024], replicated, may hold values from -0.5 to 0.5
Outputs:
- merged: bfloat16 [16, 2, 512, 256], P(('scene', 'aper'), None, None, 'range'), parts along dimension 0
There are 2 independent parts, one for each index of `scene`. A program takes and returns all parts, laid end to end along the dimension named above; an argument that names none is the same for every part. Nothing has to cross between parts.
Inputs may be any that keep to these rules, and one draw needn't show every extreme that they name: `offsets`: for every level and role both -28 and 28 occur.
All inputs are finite; a program needn't handle non-finite values.
Results may differ from a plain program's by a relative error of at most 0.0085.
Values may be sent and summed in bfloat16 or wider, within the bound.
No kernel may reach another device: no remote copies, remote signals or barrier semaphores. Data moves between devices by JAX's collectives and lax.ppermute only.
A program may use at most 64 MiB of HBM per device.

v0:
```python
import jax
import jax.numpy as jnp
from jax import lax
from jax.sharding import PartitionSpec as P

HALO = 32


def padded(cells, sides, width):
    for axis, dim in sides:
        count = lax.axis_size(axis)
        ends = count - 1
        head = lax.slice_in_dim(cells, 0, width, axis=dim)
        tail = lax.slice_in_dim(cells, cells.shape[dim] - width, cells.shape[dim], axis=dim)
        cells = jnp.concatenate(
            [
                lax.ppermute(tail, axis, [(i, (i + 1) % count) for i in range(ends)]),
                cells,
                lax.ppermute(head, axis, [((i + 1) % count, i) for i in range(ends)]),
            ],
            axis=dim,
        )
    return cells


def from_partner(value, axis, distance):
    mask = 2**distance
    pairs = [(source, source ^ mask) for source in range(lax.axis_size(axis))]
    return lax.ppermute(value, axis, pairs)


def interpolate(matrix_rows, image):
    return jnp.einsum("pa,can->cpn", matrix_rows, image, preferred_element_type=jnp.float32).astype(
        jnp.bfloat16
    )


def shifted(inter, shift_rows, tap_rows, first_col, out_width):
    taps_count = tap_rows.shape[1]
    needed = out_width + taps_count - 1
    total_width = inter.shape[2]
    start_cols = first_col - 3 + shift_rows
    moved = inter
    for bit_number in range((total_width - needed).bit_length()):
        stride_len = 1 << bit_number
        rolled = jnp.concatenate(
            [moved[:, :, stride_len:], jnp.zeros_like(moved[:, :, :stride_len])], axis=2
        )
        chosen_bits = start_cols >> bit_number & 1 == 1
        moved = jnp.where(chosen_bits[None, :, None], rolled, moved)
    window = moved[:, :, :needed]
    summed = jnp.zeros(window.shape[:2] + (out_width,), jnp.float32)
    for tap_number in range(taps_count):
        summed = summed + tap_rows[None, :, tap_number, None] * window[
            :, :, tap_number : tap_number + out_width
        ].astype(jnp.float32)
    return summed


def pick_rows(table, merge_level, child_role, own_half, angle_count):
    chosen = lax.dynamic_index_in_dim(table[merge_level], child_role, 0, keepdims=False)
    return lax.dynamic_slice_in_dim(chosen, own_half * angle_count, angle_count, 0)


def contribution(
    inter,
    merge_level,
    child_role,
    own_half,
    offsets,
    tap_index,
    tap_table,
    phase_base,
    phase_slope,
    out_width,
    anchor,
):
    angle_count = inter.shape[1]
    shift_rows = pick_rows(offsets, merge_level, child_role, own_half, angle_count)
    index_rows = pick_rows(tap_index, merge_level, child_role, own_half, angle_count)
    onehot = (
        index_rows[:, None] == jnp.arange(tap_table.shape[0], dtype=jnp.int32)[None, :]
    ).astype(jnp.float32)
    tap_rows = jnp.dot(
        onehot, tap_table, precision=lax.Precision.HIGHEST, preferred_element_type=jnp.float32
    )
    summed = shifted(inter, shift_rows, tap_rows, HALO, out_width)
    positions = (anchor + jnp.arange(out_width, dtype=jnp.int32)).astype(jnp.float32)
    base_rows = pick_rows(phase_base, merge_level, child_role, own_half, angle_count)
    slope_rows = pick_rows(phase_slope, merge_level, child_role, own_half, angle_count)
    phase_angle = base_rows[:, None] + slope_rows[:, None] * positions[None, :]
    cosine = jnp.cos(phase_angle)
    sine_part = jnp.sin(phase_angle)
    real_part = summed[0]
    imag_part = summed[1]
    return jnp.stack(
        [real_part * cosine - imag_part * sine_part, real_part * sine_part + imag_part * cosine]
    )


def body(images, interp_matrix, offsets, tap_index, tap_table, phase_base, phase_slope):
    current = images[0]
    angle_count = current.shape[1]
    shard_span = current.shape[2]
    levels = offsets.shape[0]
    aper_index = lax.axis_index("aper")
    range_index = lax.axis_index("range")
    scene_span = shard_span * lax.axis_size("range")
    current = padded(current, (("range", 2),), levels * HALO)
    for merge_level in range(levels):
        own_half = aper_index >> merge_level & 1
        margin = (levels - merge_level) * HALO
        extended = current
        out_width = extended.shape[2] - 2 * HALO
        anchor = range_index * shard_span - (margin - HALO)
        own_rows = lax.dynamic_slice_in_dim(interp_matrix, own_half * angle_count, angle_count, 0)
        partner = from_partner(extended, "aper", merge_level)
        own_inter = interpolate(own_rows, extended)
        received = interpolate(own_rows, partner)
        summed = contribution(
            own_inter,
            merge_level,
            own_half,
            own_half,
            offsets,
            tap_index,
            tap_table,
            phase_base,
            phase_slope,
            out_width,
            anchor,
        )
        summed = summed + contribution(
            received,
            merge_level,
            1 - own_half,
            own_half,
            offsets,
            tap_index,
            tap_table,
            phase_base,
            phase_slope,
            out_width,
            anchor,
        )
        if margin > HALO:
            positions = anchor + jnp.arange(out_width, dtype=jnp.int32)
            inside = (positions >= 0) & (positions < scene_span)
            summed = jnp.where(inside[None, None, :], summed, 0.0)
        current = summed.astype(jnp.bfloat16)
    return current[None]


def solution(mesh):
    return jax.shard_map(
        body,
        mesh=mesh,
        in_specs=(P(("scene", "aper"), None, None, "range"), P(), P(), P(), P(), P(), P()),
        out_specs=P(("scene", "aper"), None, None, "range"),
        check_vma=False,
    )
```

profile of v0, /device:TPU:0, one launch (start us, length us, event | category | flops | bytes accessed | tf_op | source)
XLA Modules:
  0.0 82.6 jit_solution(4897862011869639215)
XLA Ops:
  0.0 1.2 %copy.8 = bf16[1,2,512,128]{2,3,1,0:T(8,128)(2,1)S(1)} copy(bf16[1,2,512,128]{3,2,1,0:T(8,128)(2,1)} %param.7) | data formatting | bytes 524288 | tf_op args[0]
  1.2 2.4 %collective-permute-start = (bf16[2,512,96]{1,2,0:T(8,128)(2,1)S(1)}, bf16[2,512,96]{1,2,0:T(8,128)(2,1)S(1)}, u32[]{:S(2)}, u32[]{:S(2)}) collective-permute-start(bf16[2,512,96]{1,2,0:T(8,128)(2,1)S(1)} %get-tuple-element.53), channel_id=1, source_target_pairs={{0,1},{2,3},{4,5},{6,7},{8,9},{10,11},{12,13},{14,15},{16,17},{18,... | collective-permute-start | bytes 589832 | tf_op jit(solution)/shard_map/ppermute | solution.py:17
  3.6 1.3 %collective-permute-start.1 = (bf16[2,512,96]{1,2,0:T(8,128)(2,1)S(1)}, bf16[2,512,96]{1,2,0:T(8,128)(2,1)S(1)}, u32[]{:S(2)}, u32[]{:S(2)}) collective-permute-start(bf16[2,512,96]{1,2,0:T(8,128)(2,1)S(1)} %get-tuple-element.54), channel_id=1, source_target_pairs={{1,0},{3,2},{5,4},{7,6},{9,8},{11,10},{13,12},{15,14},{17,16},{19,... | collective-permute-start | bytes 589832 | tf_op jit(solution)/shard_map/ppermute | solution.py:19
  5.3 0.3 fusion.37
  5.7 0.3 fusion.38
  6.2 0.3 fusion.36
  6.6 0.3 fusion.39
  7.2 0.3 fusion.35
  7.6 0.3 fusion.40
  8.3 0.5 fusion
  9.1 0.2 pad_select_fusion.11
  9.4 0.2 pad_select_fusion.10
  9.6 0.2 slice.705
  9.7 0.2 pad_select_fusion.9
  10.0 0.2 pad_select_fusion.8
  10.2 0.2 pad_select_fusion.7
  10.5 2.4 %collective-permute-start.2 = (bf16[2,512,320]{1,2,0:T(8,128)(2,1)S(1)}, bf16[2,512,320]{1,2,0:T(8,128)(2,1)S(1)}, u32[]{:S(2)}, u32[]{:S(2)}) collective-permute-start(bf16[2,512,320]{1,2,0:T(8,128)(2,1)S(1)} %pad_maximum_fusion), channel_id=1, source_target_pairs={{0,2},{2,0},{4,6},{6,4},{8,10},{10,8},{12,14},{14,12},{1,3},{3,1},... | collective-permute-start | bytes 1966088 | tf_op jit(solution)/shard_map/ppermute | solution.py:29
  12.9 0.2 pad_select_fusion.6
  13.0 1.0 %multiply_add_fusion.1 = f32[2,512,256]{1,2,0:T(8,128)S(1)} fusion(bf16[2,512,320]{1,2,0:T(8,128)(2,1)S(1)} %pad_select_fusion.6, f32[512]{0:T(512)S(1)} %bitcast.125, f32[512]{0:T(512)S(1)} %bitcast.126, f32[512]{0:T(512)S(1)} %bitcast.127, f32[512]{0:T(512)S(1)} %bitcast.128, f32[512]{0:T(512)S(1)} %bitcast.129, f32[512]{0:T(512)S(1)} %bitcast.130, ...), kind=kLoop, calls=%fused_computation.16 | loop fusion | flops 6029312 | bytes 5259264 | tf_op jit(solution)/shard_map/add | solution.py:54
  14.1 14.0 %collective-permute-done.2 = bf16[2,512,320]{1,2,0:T(8,128)(2,1)S(1)} collective-permute-done((bf16[2,512,320]{1,2,0:T(8,128)(2,1)S(1)}, bf16[2,512,320]{1,2,0:T(8,128)(2,1)S(1)}, u32[]{:S(2)}, u32[]{:S(2)}) %collective-permute-start.2) | collective-permute-done | bytes 655392 | tf_op jit(solution)/shard_map/ppermute | solution.py:29
  28.1 0.5 fusion.1
  28.6 0.2 slice.727
  28.8 0.2 pad_select_fusion.5
  29.0 0.2 slice.728
  29.1 0.2 pad_select_fusion.4
  29.5 0.2 pad_select_fusion.3
  29.7 0.2 pad_select_fusion.2
  30.0 0.2 pad_select_fusion.1
  30.2 0.2 pad_select_fusion
  30.4 1.0 %multiply_add_fusion = f32[2,512,256]{1,2,0:T(8,128)S(1)} fusion(bf16[2,512,320]{1,2,0:T(8,128)(2,1)S(1)} %pad_select_fusion, f32[512]{0:T(512)S(1)} %bitcast.117, f32[512]{0:T(512)S(1)} %bitcast.118, f32[512]{0:T(512)S(1)} %bitcast.119, f32[512]{0:T(512)S(1)} %bitcast.120, f32[512]{0:T(512)S(1)} %bitcast.121, f32[512]{0:T(512)S(1)} %bitcast.122, ...), kind=kLoop, calls=%fused_computation.15 | loop fusion | flops 6029312 | bytes 5259264 | tf_op jit(solution)/shard_map/add | solution.py:54
  31.4 4.4 %multiply_subtract_fusion = (f32[1,512,256]{1,2,0:T(8,128)S(1)}, f32[1,512,256]{1,2,0:T(8,128)S(1)}, f32[1,512,256]{1,2,0:T(8,128)S(1)}, f32[1,512,256]{1,2,0:T(8,128)S(1)}) fusion(f32[2,512,256]{1,2,0:T(8,128)S(1)} %multiply_add_fusion, f32[512]{0:T(512)S(1)} %bitcast.168, f32[512]{0:T(512)S(1)} %bitcast.171, f32[256]{0:T(256)S(1)} %fusion.59, ...), kind=kLoop, calls=%fused_computation.58 | loop fusion | flops 2097152 | bytes 4203520 | tf_op jit(solution)/shard_map/sub | solution.py:97
  35.8 0.2 fusion.7
  36.0 0.5 fusion.2
  36.5 2.4 %collective-permute-start.3 = (bf16[2,512,256]{1,2,0:T(8,128)(2,1)S(1)}, bf16[2,512,256]{1,2,0:T(8,128)(2,1)S(1)}, u32[]{:S(2)}, u32[]{:S(2)}) collective-permute-start(bf16[2,512,256]{1,2,0:T(8,128)(2,1)S(1)} %fusion.7), channel_id=1, source_target_pairs={{0,4},{2,6},{4,0},{6,2},{8,12},{10,14},{12,8},{14,10},{1,5},{3,7},... | collective-permute-start | bytes 1572872 | tf_op jit(solution)/shard_map/ppermute | solution.py:29
  40.3 0.8 multiply_add_fusion.3
  41.0 10.1 %collective-permute-done.3 = bf16[2,512,256]{1,2,0:T(8,128)(2,1)S(1)} collective-permute-done((bf16[2,512,256]{1,2,0:T(8,128)(2,1)S(1)}, bf16[2,512,256]{1,2,0:T(8,128)(2,1)S(1)}, u32[]{:S(2)}, u32[]{:S(2)}) %collective-permute-start.3) | collective-permute-done | bytes 524320 | tf_op jit(solution)/shard_map/ppermute | solution.py:29
  51.1 0.5 fusion.3
  52.9 0.8 multiply_add_fusion.2
  53.7 3.2 %multiply_subtract_fusion.2 = (f32[1,512,192]{1,2,0:T(8,128)S(1)}, f32[1,512,192]{1,2,0:T(8,128)S(1)}, f32[1,512,192]{1,2,0:T(8,128)S(1)}, f32[1,512,192]{1,2,0:T(8,128)S(1)}) fusion(f32[2,512,192]{1,2,0:T(8,128)S(1)} %multiply_add_fusion.2, f32[512]{0:T(512)S(1)} %bitcast.172, f32[512]{0:T(512)S(1)} %bitcast.175, f32[192]{0:T(256)S(1)} %fusion.60, ...), kind=kLoop, calls=%fused_computation.86 | loop fusion | flops 1572864 | bytes 3154688 | tf_op jit(solution)/shard_map/sub | solution.py:97
  56.9 0.2 fusion.9
  57.1 0.4 fusion.4
  57.5 2.8 %collective-permute-start.4 = (bf16[2,512,192]{1,2,0:T(8,128)(2,1)S(1)}, bf16[2,512,192]{1,2,0:T(8,128)(2,1)S(1)}, u32[]{:S(2)}, u32[]{:S(2)}) collective-permute-start(bf16[2,512,192]{1,2,0:T(8,128)(2,1)S(1)} %fusion.9), channel_id=1, source_target_pairs={{0,8},{2,10},{4,12},{6,14},{8,0},{10,2},{12,4},{14,6},{1,9},{3,11}... | collective-permute-start | bytes 1179656 | tf_op jit(solution)/shard_map/ppermute | solution.py:29
  61.4 0.5 multiply_add_fusion.5
  61.9 15.6 %collective-permute-done.4 = bf16[2,512,192]{1,2,0:T(8,128)(2,1)S(1)} collective-permute-done((bf16[2,512,192]{1,2,0:T(8,128)(2,1)S(1)}, bf16[2,512,192]{1,2,0:T(8,128)(2,1)S(1)}, u32[]{:S(2)}, u32[]{:S(2)}) %collective-permute-start.4) | collective-permute-done | bytes 393248 | tf_op jit(solution)/shard_map/ppermute | solution.py:29
  77.5 0.4 fusion.5
  79.0 0.5 multiply_add_fusion.4
  79.5 2.1 %subtract_bitcast_fusion = (f32[1,1,512,128]{2,3,1,0:T(8,128)S(1)}, f32[1,1,512,128]{2,3,1,0:T(8,128)S(1)}, f32[1,1,512,128]{2,3,1,0:T(8,128)S(1)}, f32[1,1,512,128]{2,3,1,0:T(8,128)S(1)}) fusion(f32[2,512,128]{1,2,0:T(8,128)S(1)} %multiply_add_fusion.4, f32[512]{0:T(512)S(1)} %bitcast.132, f32[512]{0:T(512)S(1)} %bitcast.135, f32[128]{0:T(128)S(1)} %add_convert_fusion, ...), kind=kLoop, calls=%fused_computation.96 | loop fusion | flops 1048576 | bytes 2105856 | tf_op jit(solution)/shard_map/stack | solution.py:96
  81.7 0.8 %copy.9 = bf16[1,2,512,128]{3,2,1,0:T(8,128)(2,1)} copy(bf16[1,2,512,128]{2,3,1,0:T(8,128)(2,1)S(1)} %fusion.10) | data formatting | bytes 524288 | tf_op jit(solution)/shard_map/convert_element_type | solution.py:150
  (102 shorter events, 6.6 us)
Async XLA Ops:
  0.0 8.3 %copy-start = (bf16[1024,512]{1,0:T(8,128)(2,1)S(1)}, bf16[1024,512]{1,0:T(8,128)(2,1)}, u32[]{:S(2)}) copy-start(bf16[1024,512]{1,0:T(8,128)(2,1)} %param.8) | copy-start | bytes 3145732
  0.0 5.0 %copy-start.1 = (s32[3,2,1024]{2,1,0:T(2,128)S(1)}, s32[3,2,1024]{2,1,0:T(2,128)}, u32[]{:S(2)}) copy-start(s32[3,2,1024]{2,1,0:T(2,128)} %param.10) | copy-start | bytes 73732
  0.0 5.1 %copy-start.2 = (s32[3,2,1024]{2,1,0:T(2,128)S(1)}, s32[3,2,1024]{2,1,0:T(2,128)}, u32[]{:S(2)}) copy-start(s32[3,2,1024]{2,1,0:T(2,128)} %param.9) | copy-start | bytes 73732
  0.0 5.2 %copy-start.5 = (f32[16,8]{0,1:T(8,128)S(1)}, f32[16,8]{0,1:T(8,128)}, u32[]{:S(2)}) copy-start(f32[16,8]{0,1:T(8,128)} %param.11) | copy-start | bytes 1540
  0.0 6.0 %copy-start.3 = (f32[3,2,1024]{2,1,0:T(2,128)S(1)}, f32[3,2,1024]{2,1,0:T(2,128)}, u32[]{:S(2)}) copy-start(f32[3,2,1024]{2,1,0:T(2,128)} %param.12) | copy-start | bytes 73732
  0.0 6.0 %copy-start.4 = (f32[3,2,1024]{2,1,0:T(2,128)S(1)}, f32[3,2,1024]{2,1,0:T(2,128)}, u32[]{:S(2)}) copy-start(f32[3,2,1024]{2,1,0:T(2,128)} %param.13) | copy-start | bytes 73732
  1.2 7.1 %collective-permute-start = (bf16[2,512,96]{1,2,0:T(8,128)(2,1)S(1)}, bf16[2,512,96]{1,2,0:T(8,128)(2,1)S(1)}, u32[]{:S(2)}, u32[]{:S(2)}) collective-permute-start(bf16[2,512,96]{1,2,0:T(8,128)(2,1)S(1)} %get-tuple-element.53), channel_id=1, source_target_pairs={{0,1},{2,3},{4,5},{6,7},{8,9},{10,11},{12,13},{14,15},{16,17},{18,... | collective-permute-start | bytes 589832 | tf_op jit(solution)/shard_map/ppermute | solution.py:17
  3.6 4.7 %collective-permute-start.1 = (bf16[2,512,96]{1,2,0:T(8,128)(2,1)S(1)}, bf16[2,512,96]{1,2,0:T(8,128)(2,1)S(1)}, u32[]{:S(2)}, u32[]{:S(2)}) collective-permute-start(bf16[2,512,96]{1,2,0:T(8,128)(2,1)S(1)} %get-tuple-element.54), channel_id=1, source_target_pairs={{1,0},{3,2},{5,4},{7,6},{9,8},{11,10},{13,12},{15,14},{17,16},{19,... | collective-permute-start | bytes 589832 | tf_op jit(solution)/shard_map/ppermute | solution.py:19
  10.5 17.6 %collective-permute-start.2 = (bf16[2,512,320]{1,2,0:T(8,128)(2,1)S(1)}, bf16[2,512,320]{1,2,0:T(8,128)(2,1)S(1)}, u32[]{:S(2)}, u32[]{:S(2)}) collective-permute-start(bf16[2,512,320]{1,2,0:T(8,128)(2,1)S(1)} %pad_maximum_fusion), channel_id=1, source_target_pairs={{0,2},{2,0},{4,6},{6,4},{8,10},{10,8},{12,14},{14,12},{1,3},{3,1},... | collective-permute-start | bytes 1966088 | tf_op jit(solution)/shard_map/ppermute | solution.py:29
  36.5 14.6 %collective-permute-start.3 = (bf16[2,512,256]{1,2,0:T(8,128)(2,1)S(1)}, bf16[2,512,256]{1,2,0:T(8,128)(2,1)S(1)}, u32[]{:S(2)}, u32[]{:S(2)}) collective-permute-start(bf16[2,512,256]{1,2,0:T(8,128)(2,1)S(1)} %fusion.7), channel_id=1, source_target_pairs={{0,4},{2,6},{4,0},{6,2},{8,12},{10,14},{12,8},{14,10},{1,5},{3,7},... | collective-permute-start | bytes 1572872 | tf_op jit(solution)/shard_map/ppermute | solution.py:29
  57.5 20.0 %collective-permute-start.4 = (bf16[2,512,192]{1,2,0:T(8,128)(2,1)S(1)}, bf16[2,512,192]{1,2,0:T(8,128)(2,1)S(1)}, u32[]{:S(2)}, u32[]{:S(2)}) collective-permute-start(bf16[2,512,192]{1,2,0:T(8,128)(2,1)S(1)} %fusion.9), channel_id=1, source_target_pairs={{0,8},{2,10},{4,12},{6,14},{8,0},{10,2},{12,4},{14,6},{1,9},{3,11}... | collective-permute-start | bytes 1179656 | tf_op jit(solution)/shard_map/ppermute | solution.py:29
where the time goes:
time: 82.8 us; the launch traced here: 82.6 us
  waiting for transfers between devices  39.7 us (48%)
  other arithmetic  20.4 us (25%)
  starting transfers between devices  11.2 us (14%)
  local copies, waits for them, and re-layouts  5.49 us (7%)
  matrix products  4.69 us (6%)
  between operations  1 us (1%)
    ppermute x3, waiting for transfers between devices, from_partner(): return lax.ppermute(value, axis, pairs)  39.7 us
    sub x2, other arithmetic, contribution(): real_part * cosine - imag_part * sine_part  7.62 us
    ppermute x3, starting transfers between devices, from_partner(): return lax.ppermute(value, axis, pairs)  7.58 us
    select_n x36, other arithmetic, shifted(): moved = jnp.where(chosen_bits[None, :, None], rolled, moved)  4.95 us
    add x6, other arithmetic, shifted(): summed + tap_rows[None, :, tap_number, None] * window[:, :, tap_number:ta...  4.62 us
    dot_general x6, matrix products, interpolate(): jnp.einsum('pa,can->cpn', matrix_rows, image, preferred_element_type=jnp....  2.82 us
    slice x36, local copies, waits for them, and re-layouts, shifted(): moved[:, :, stride_len:]  2.81 us
    ppermute x1, starting transfers between devices, padded(): lax.ppermute(tail, axis, [(i, (i + 1) % count) for i in range(ends)])  2.38 us
  transfers between devices with their start and end apart: 5, of which 3 were waited for; matrix products, arithmetic and copies ran while one was open for 9% of the time, Pallas kernels for 0%

commit v1 on v0

v1 whole, which is shorter than its diff:
```python
import functools

import jax
import jax.numpy as jnp
from jax import lax
from jax.experimental import pallas as pl
from jax.experimental.pallas import tpu as pltpu
from jax.sharding import PartitionSpec as P

HALO = 32
LANES = 128
ROWS = 8
KERNEL_VMEM = 8 << 20
VMEM = pl.BlockSpec(memory_space=pltpu.VMEM)


def run(kernel, outs, args, scratch=(), flops=0):
    size = sum(o.size * o.dtype.itemsize for o in outs)
    return pl.pallas_call(
        kernel,
        out_shape=outs,
        in_specs=[VMEM] * len(args),
        out_specs=[VMEM] * len(outs),
        scratch_shapes=scratch,
        compiler_params=pltpu.CompilerParams(vmem_limit_bytes=KERNEL_VMEM),
        cost_estimate=pl.CostEstimate(flops=flops, bytes_accessed=size, transcendentals=0),
    )(*args)


def from_partner(value, axis, mask):
    pairs = [(source, source ^ mask) for source in range(lax.axis_size(axis))]
    return lax.ppermute(value, axis, pairs)


def inner_start(width):
    return pl.multiple_of((1 - lax.axis_index("range")) * (width - HALO), HALO)


def tables_kernel(level, span, off, idx, base, slope, table, shift_ref, taps_ref, phase_ref):
    angles = off.shape[2] // 2
    half = lax.axis_index("aper") >> level & 1
    start = lax.axis_index("range") * span
    taps_count = table.shape[0]
    for order in range(2):
        role = half if order == 0 else 1 - half
        for j in range(angles // LANES):
            lane = pl.ds(pl.multiple_of(half * angles + j * LANES, LANES), LANES)

            def row(ref):
                both = ref[level, :, lane]
                return jnp.broadcast_to(jnp.where(role == 0, both[0:1], both[1:2]), (ROWS, LANES))

            shift = row(off) + (HALO - 3)
            shift_ref[order, j] = shift
            which = row(idx)
            taps = jnp.zeros((taps_count, LANES), jnp.float32)
            for k in range(table.shape[1]):
                taps = jnp.where(which == k, table[:, k : k + 1], taps)
            odd = shift & 1
            zero = jnp.zeros((ROWS, LANES), jnp.float32)
            rows = [jnp.broadcast_to(taps[t : t + 1], (ROWS, LANES)) for t in range(taps_count)]
            for t in range(taps_count + 1):
                even_tap = rows[t] if t < taps_count else zero
                odd_tap = rows[t - 1] if t > 0 else zero
                taps_ref[order, j, t] = jnp.where(odd == 1, odd_tap, even_tap)
            s = row(slope)
            ramp = lax.broadcasted_iota(jnp.int32, (ROWS, LANES), 0)
            near = row(base) + s * (ramp + start).astype(jnp.float32)
            c0, s0 = jnp.cos(near), jnp.sin(near)
            steps = span // ROWS
            far_at = lax.broadcasted_iota(jnp.int32, (steps, LANES), 0) * ROWS
            far = jnp.broadcast_to(s[0:1], (steps, LANES)) * far_at.astype(jnp.float32)
            c1, s1 = jnp.cos(far), jnp.sin(far)
            for u in range(steps):
                cu, su = c1[u : u + 1], s1[u : u + 1]
                at = pl.ds(u * ROWS, ROWS)
                phase_ref[order, 0, j, at, :] = c0 * cu - s0 * su
                phase_ref[order, 1, j, at, :] = s0 * cu + c0 * su


def turn_kernel(image, turned, edge):
    for part in range(image.shape[0]):
        turned[part] = image[part].T
    edge[...] = turned[:, pl.ds(inner_start(turned.shape[1]), HALO), :]


def shift_filter(slab, part, j, shift, taps, tmp, count):
    v = slab[part, j, 0 : count + 64, :]
    pick = lambda bit, a, b: jnp.where(
        jnp.broadcast_to((shift >> bit & 1 == 1)[None], (a.shape[0] // ROWS, ROWS, LANES)).reshape(a.shape), a, b
    )
    v = jnp.concatenate([pick(5, v[32 : count + 64], v[: count + 32]), v[count + 32 : count + 40]], 0)
    v = pick(4, v[16 : count + 40], v[: count + 24])
    v = pick(3, v[8 : count + 24], v[: count + 16])
    tmp[0, 0 : count + 16] = v
    v = pick(2, tmp[0, 4 : count + 20], v)
    tmp[1, 0 : count + 16] = v
    v = pick(1, tmp[1, 2 : count + 18], v)
    tmp[2, 0 : count + 16] = v
    total = None
    for t in range(taps.shape[0]):
        tap = jnp.broadcast_to(taps[t][None], (count // ROWS, ROWS, LANES)).reshape(count, LANES)
        term = tap * (v[:count] if t == 0 else tmp[2, t : t + count])
        total = term if total is None else total + term
    return total


def level_kernel(level, final, own, own_edge, other, other_edge, matrix, shift_ref, taps_ref, phase_ref, *rest):
    if final:
        out, slab, tmp, merged = rest
    else:
        merged, edge, slab, tmp = rest
    parts, span, angles = own.shape
    half = lax.axis_index("aper") >> level & 1
    place = lax.axis_index("range")
    rows = matrix[pl.ds(pl.multiple_of(half * angles, angles), angles), :]
    dims = (((1,), (1,)), ((), ()))
    for order, (image, image_edge) in enumerate(((own, own_edge), (other, other_edge))):
        for part in range(parts):
            inter = lax.dot_general(image[part], rows, dims, preferred_element_type=jnp.float32)
            inter = inter.astype(jnp.bfloat16).astype(jnp.float32)
            at_edge = lax.dot_general(image_edge[part], rows, dims, preferred_element_type=jnp.float32)
            at_edge = at_edge.astype(jnp.bfloat16).astype(jnp.float32)
            for j in range(angles // LANES):
                cut = slice(j * LANES, (j + 1) * LANES)
                slab[order * parts + part, j, HALO : HALO + span, :] = inter[:, cut]
                far = pl.multiple_of((1 - place) * (span + HALO), HALO)
                slab[order * parts + part, j, pl.ds(far, HALO), :] = at_edge[:, cut]
                none = pl.multiple_of(place * (span + HALO), HALO)
                slab[order * parts + part, j, pl.ds(none, HALO), :] = jnp.zeros((HALO, LANES), jnp.float32)

    def tile(j, carry):
        lane = pl.ds(pl.multiple_of(j * LANES, LANES), LANES)
        real = imag = None
        for order in range(2):
            shift = shift_ref[order, j]
            taps = taps_ref[order, j]
            re = shift_filter(slab, order * parts, j, shift, taps, tmp.at[0], span)
            im = shift_filter(slab, order * parts + 1, j, shift, taps, tmp.at[1], span)
            c, s = phase_ref[order, 0, j], phase_ref[order, 1, j]
            new_re, new_im = re * c - im * s, re * s + im * c
            real = new_re if real is None else real + new_re
            imag = new_im if imag is None else imag + new_im
        merged[0, :, lane] = real.astype(jnp.bfloat16)
        merged[1, :, lane] = imag.astype(jnp.bfloat16)
        return carry

    lax.fori_loop(0, angles // LANES, tile, 0)
    if final:
        for part in range(parts):
            out[part] = merged[part].T
    else:
        edge[...] = merged[:, pl.ds(inner_start(span), HALO), :]


def body(images, interp_matrix, offsets, tap_index, tap_table, phase_base, phase_slope):
    image = images[0]
    parts, angles, span = image.shape
    levels = offsets.shape[0]
    tiles = angles // LANES
    taps_count = tap_table.shape[1]
    f32, bf16 = jnp.float32, jnp.bfloat16
    like = jax.ShapeDtypeStruct
    turned_shape = [like((parts, span, angles), bf16), like((parts, HALO, angles), bf16)]
    work = [
        pltpu.VMEM((2 * parts, tiles, span + 2 * HALO, LANES), f32),
        pltpu.VMEM((parts, 3, span + 24, LANES), f32),
    ]

    received = from_partner(image, "aper", 1)
    current, edge = run(turn_kernel, turned_shape, [image])
    table = tap_table.T
    tables = [
        run(
            functools.partial(tables_kernel, level, span),
            [
                like((2, tiles, ROWS, LANES), jnp.int32),
                like((2, tiles, taps_count + 1, ROWS, LANES), f32),
                like((2, 2, tiles, span, LANES), f32),
            ],
            [offsets, tap_index, phase_base, phase_slope, table],
        )
        for level in range(levels)
    ]
    for level in range(levels):
        own_edge = from_partner(edge, "range", 1)
        if level == 0:
            other, other_edge = run(turn_kernel, turned_shape, [received])
        else:
            other = from_partner(current, "aper", 2**level)
            start = (1 - lax.axis_index("range")) * (span - HALO)
            other_edge = lax.dynamic_slice_in_dim(other, start, HALO, 1)
        other_edge = from_partner(other_edge, "range", 1)
        final = level == levels - 1
        outs = [like(image.shape, bf16)] if final else turned_shape
        result = run(
            functools.partial(level_kernel, level, final),
            outs,
            [current, own_edge, other, other_edge, interp_matrix, *tables[level]],
            work + ([pltpu.VMEM((parts, span, angles), bf16)] if final else []),
        )
        if final:
            return result[0][None]
        current, edge = result


def solution(mesh):
    return jax.shard_map(
        body,
        mesh=mesh,
        in_specs=(P(("scene", "aper"), None, None, "range"), P(), P(), P(), P(), P(), P()),
        out_specs=P(("scene", "aper"), None, None, "range"),
        check_vma=False,
    )
```

time: 82.8 us -> 47.4 us (0.57)
  other arithmetic: 20.4 us -> 0 us
  waiting for transfers between devices: 39.7 us -> 25.5 us
  Pallas kernels: 0 us -> 11 us
  matrix products: 4.69 us -> 0 us
  starting transfers between devices: 11.2 us -> 7.8 us
  local copies, waits for them, and re-layouts: 5.49 us -> 2.68 us
  between operations: 1 us -> 0.17 us
    ppermute x3 -> x9, waiting for transfers between devices: 39.7 us -> 25.5 us  [from_partner(): return lax.ppermute(value, axis, pairs)]
    pallas_call x0 -> x8, Pallas kernels: none -> 11 us  [run(): pl.pallas_call(kernel, out_shape=outs, in_specs=[VMEM] * len(args), out_s...]
    sub x2 -> x0, other arithmetic: 7.62 us -> none  [contribution(): real_part * cosine - imag_part * sine_part]
    select_n x36 -> x0, other arithmetic: 4.95 us -> none  [shifted(): moved = jnp.where(chosen_bits[None, :, None], rolled, moved)]
    add x8 -> x0, other arithmetic: 4.8 us -> none  [the longest x6 4.62 us: shifted(): summed + tap_rows[None, :, tap_number, None] * window[:, :, tap_number:ta...]
    dot_general x12 -> x0, matrix products: 4.69 us -> none  [the longest x6 2.82 us: interpolate(): jnp.einsum('pa,can->cpn', matrix_rows, image, preferred_element_type=jnp....]
    ppermute x2 -> x0, starting transfers between devices: 3.67 us -> none  [the longest x1 2.38 us: padded(): lax.ppermute(tail, axis, [(i, (i + 1) % count) for i in range(ends)])]
    slice x47 -> x0, local copies, waits for them, and re-layouts: 3.01 us -> none  [the longest x36 2.81 us: shifted(): moved[:, :, stride_len:]]
  transfers between devices with their start and end apart: 5 -> 9, of which waited for: 3 -> 6; matrix products, arithmetic and copies ran while one was open for 9% -> 0% of each run, Pallas kernels for 0% -> 4%
where the time goes in v1:
time: 47.4 us; the launch traced here: 47.2 us
  waiting for transfers between devices  25.5 us (54%)
  Pallas kernels  11 us (23%)
  starting transfers between devices  7.8 us (16%)
  local copies, waits for them, and re-layouts  2.68 us (6%)
    ppermute x9, waiting for transfers between devices, from_partner(): return lax.ppermute(value, axis, pairs)  25.5 us
    pallas_call x8, Pallas kernels, run(): pl.pallas_call(kernel, out_shape=outs, in_specs=[VMEM] * len(args), out_s...  11 us
    ppermute x9, starting transfers between devices, from_partner(): return lax.ppermute(value, axis, pairs)  7.8 us
    unnamed x16, local copies, waits for them, and re-layouts  2.67 us
  transfers between devices with their start and end apart: 9, of which 6 were waited for; matrix products, arithmetic and copies ran while one was open for 0% of the time, Pallas kernels for 4%

profile of v1, /device:TPU:0, one launch (start us, length us, event | category | flops | bytes accessed | tf_op | source)
XLA Modules:
  0.0 47.2 jit_solution(15089802824506534538)
XLA Ops:
  0.0 2.9 %collective-permute-start.1 = (bf16[2,512,128]{2,1,0:T(8,128)(2,1)}, bf16[2,512,128]{2,1,0:T(8,128)(2,1)S(1)}, u32[]{:S(2)}, u32[]{:S(2)}) collective-permute-start(bf16[2,512,128]{2,1,0:T(8,128)(2,1)} %bitcast.3), channel_id=1, source_target_pairs={{0,2},{2,0},{4,6},{6,4},{8,10},{10,8},{12,14},{14,12},{1,3},{3,1},... | collective-permute-start | bytes 786440 | tf_op jit(solution)/shard_map/ppermute | solution.py:32
  2.9 0.0 copy-start.2
  2.9 1.0 %copy-done.2 = bf16[1,2,512,128]{3,2,1,0:T(8,128)(2,1)S(1)} copy-done((bf16[1,2,512,128]{3,2,1,0:T(8,128)(2,1)S(1)}, bf16[1,2,512,128]{3,2,1,0:T(8,128)(2,1)}, u32[]{:S(2)}) %copy-start.2) | copy-done | bytes 262168
  3.9 0.1 shard_map.73
  4.1 0.0 copy-start.3
  4.1 0.0 copy-start.4
  4.1 0.0 copy-start.5
  4.1 0.0 copy-start.6
  4.1 0.1 collective-permute-start
  4.2 5.3 %collective-permute-done.1.image = bf16[2,512,128]{2,1,0:T(8,128)(2,1)S(1)} collective-permute-done((bf16[2,512,128]{2,1,0:T(8,128)(2,1)}, bf16[2,512,128]{2,1,0:T(8,128)(2,1)S(1)}, u32[]{:S(2)}, u32[]{:S(2)}) %collective-permute-start.1) | collective-permute-done | bytes 262176 | tf_op jit(solution)/shard_map/ppermute | solution.py:32
  9.5 0.0 copy-start.7
  9.5 0.1 shard_map.74
  9.6 0.1 collective-permute-start.2
  9.7 0.0 copy-done.3
  9.7 0.0 copy-done.4
  9.7 0.0 copy-done.5
  9.7 0.0 copy-done.6
  9.7 0.4 copy-done.7
  10.1 0.6 %shard_map.75 = (s32[2,4,8,128]{3,2,1,0:T(8,128)S(1)}, f32[2,4,9,8,128]{4,3,2,1,0:T(8,128)S(1)}, f32[2,2,4,128,128]{4,3,2,1,0:T(8,128)S(1)}) custom-call(s32[3,2,1024]{2,1,0:T(2,128)S(1)} %copy-done.3, s32[3,2,1024]{2,1,0:T(2,128)S(1)} %copy-done.4, f32[3,2,1024]{2,1,0:T(2,128)S(1)} %copy-done.5, f32[3,2,1024]{2,1,0:T(2,128)S(1)} %copy-done.6, ...), custom_call_target="tpu_custom_call" | custom-call | bytes 1376256 | tf_op jit(solution)/shard_map/pallas_call | solution.py:19
  10.8 0.0 collective-permute-done.own_edge
  10.8 0.1 collective-permute-done.2.other_edge
  10.9 0.0 copy-start
  10.9 1.2 %copy-done = bf16[1024,512]{1,0:T(8,128)(2,1)S(1)} copy-done((bf16[1024,512]{1,0:T(8,128)(2,1)S(1)}, bf16[1024,512]{1,0:T(8,128)(2,1)}, u32[]{:S(2)}) %copy-start) | copy-done | bytes 1048600
  12.1 0.0 copy-start.1
  12.1 2.7 %shard_map.76 = (bf16[2,128,512]{2,1,0:T(8,128)(2,1)S(1)}, bf16[2,32,512]{2,1,0:T(8,128)(2,1)S(1)}) custom-call(bf16[2,128,512]{2,1,0:T(8,128)(2,1)S(1)} %get-tuple-element.22.own, bf16[2,32,512]{2,1,0:T(8,128)(2,1)S(1)} %collective-permute-done.own_edge, bf16[2,128,512]{2,1,0:T(8,128)(2,1)S(1)} %get-tuple-element.24.other, ...), custom_call_target="tpu_custom_call" | custom-call | bytes 327680 | tf_op jit(solution)/shard_map/pallas_call | solution.py:19
  14.9 1.9 %collective-permute-start.4 = (bf16[2,128,512]{2,1,0:T(8,128)(2,1)S(1)}, bf16[2,128,512]{2,1,0:T(8,128)(2,1)S(1)}, u32[]{:S(2)}, u32[]{:S(2)}) collective-permute-start(bf16[2,128,512]{2,1,0:T(8,128)(2,1)S(1)} %get-tuple-element.29.own), channel_id=1, source_target_pairs={{0,4},{2,6},{4,0},{6,2},{8,12},{10,14},{12,8},{14,10},{1,5},{3,7},... | collective-permute-start | bytes 786440 | tf_op jit(solution)/shard_map/ppermute | solution.py:32
  16.7 0.0 collective-permute-start.3
  16.8 6.6 %collective-permute-done.4.other = bf16[2,128,512]{2,1,0:T(8,128)(2,1)S(1)} collective-permute-done((bf16[2,128,512]{2,1,0:T(8,128)(2,1)S(1)}, bf16[2,128,512]{2,1,0:T(8,128)(2,1)S(1)}, u32[]{:S(2)}, u32[]{:S(2)}) %collective-permute-start.4) | collective-permute-done | bytes 262176 | tf_op jit(solution)/shard_map/ppermute | solution.py:32
  23.4 0.0 collective-permute-start.5
  23.4 0.6 %shard_map.77 = (s32[2,4,8,128]{3,2,1,0:T(8,128)S(1)}, f32[2,4,9,8,128]{4,3,2,1,0:T(8,128)S(1)}, f32[2,2,4,128,128]{4,3,2,1,0:T(8,128)S(1)}) custom-call(s32[3,2,1024]{2,1,0:T(2,128)S(1)} %copy-done.3, s32[3,2,1024]{2,1,0:T(2,128)S(1)} %copy-done.4, f32[3,2,1024]{2,1,0:T(2,128)S(1)} %copy-done.5, f32[3,2,1024]{2,1,0:T(2,128)S(1)} %copy-done.6, ...), custom_call_target="tpu_custom_call" | custom-call | bytes 1376256 | tf_op jit(solution)/shard_map/pallas_call | solution.py:19
  24.0 0.0 collective-permute-done.3.own_edge
  24.0 0.6 %collective-permute-done.5.other_edge = bf16[2,32,512]{2,1,0:T(8,128)(2,1)S(1)} collective-permute-done((bf16[2,32,512]{2,1,0:T(8,128)(2,1)S(1)}, bf16[2,32,512]{2,1,0:T(8,128)(2,1)S(1)}, u32[]{:S(2)}, u32[]{:S(2)}) %collective-permute-start.5) | collective-permute-done | bytes 65568 | tf_op jit(solution)/shard_map/ppermute | solution.py:32
  24.6 0.0 copy-done.1
  24.6 2.7 %shard_map.78 = (bf16[2,128,512]{2,1,0:T(8,128)(2,1)S(1)}, bf16[2,32,512]{2,1,0:T(8,128)(2,1)S(1)}) custom-call(bf16[2,128,512]{2,1,0:T(8,128)(2,1)S(1)} %get-tuple-element.29.own, bf16[2,32,512]{2,1,0:T(8,128)(2,1)S(1)} %collective-permute-done.3.own_edge, bf16[2,128,512]{2,1,0:T(8,128)(2,1)S(1)} %collective-permute-done.4.other, ...), custom_call_target="tpu_custom_call" | custom-call | bytes 327680 | tf_op jit(solution)/shard_map/pallas_call | solution.py:19
  27.4 2.8 %collective-permute-start.7 = (bf16[2,128,512]{2,1,0:T(8,128)(2,1)S(1)}, bf16[2,128,512]{2,1,0:T(8,128)(2,1)S(1)}, u32[]{:S(2)}, u32[]{:S(2)}) collective-permute-start(bf16[2,128,512]{2,1,0:T(8,128)(2,1)S(1)} %get-tuple-element.34.own), channel_id=1, source_target_pairs={{0,8},{2,10},{4,12},{6,14},{8,0},{10,2},{12,4},{14,6},{1,9},{3,11}... | collective-permute-start | bytes 786440 | tf_op jit(solution)/shard_map/ppermute | solution.py:32
  30.2 0.0 collective-permute-start.6
  30.2 12.2 %collective-permute-done.7.other = bf16[2,128,512]{2,1,0:T(8,128)(2,1)S(1)} collective-permute-done((bf16[2,128,512]{2,1,0:T(8,128)(2,1)S(1)}, bf16[2,128,512]{2,1,0:T(8,128)(2,1)S(1)}, u32[]{:S(2)}, u32[]{:S(2)}) %collective-permute-start.7) | collective-permute-done | bytes 262176 | tf_op jit(solution)/shard_map/ppermute | solution.py:32
  42.4 0.0 collective-permute-start.8
  42.4 0.6 %shard_map.79 = (s32[2,4,8,128]{3,2,1,0:T(8,128)S(1)}, f32[2,4,9,8,128]{4,3,2,1,0:T(8,128)S(1)}, f32[2,2,4,128,128]{4,3,2,1,0:T(8,128)S(1)}) custom-call(s32[3,2,1024]{2,1,0:T(2,128)S(1)} %copy-done.3, s32[3,2,1024]{2,1,0:T(2,128)S(1)} %copy-done.4, f32[3,2,1024]{2,1,0:T(2,128)S(1)} %copy-done.5, f32[3,2,1024]{2,1,0:T(2,128)S(1)} %copy-done.6, ...), custom_call_target="tpu_custom_call" | custom-call | bytes 1376256 | tf_op jit(solution)/shard_map/pallas_call | solution.py:19
  43.0 0.0 collective-permute-done.6.own_edge
  43.1 0.6 %collective-permute-done.8.other_edge = bf16[2,32,512]{2,1,0:T(8,128)(2,1)S(1)} collective-permute-done((bf16[2,32,512]{2,1,0:T(8,128)(2,1)S(1)}, bf16[2,32,512]{2,1,0:T(8,128)(2,1)S(1)}, u32[]{:S(2)}, u32[]{:S(2)}) %collective-permute-start.8) | collective-permute-done | bytes 65568 | tf_op jit(solution)/shard_map/ppermute | solution.py:32
  43.7 3.5 %shard_map.80 = bf16[2,512,128]{2,1,0:T(8,128)(2,1)} custom-call(bf16[2,128,512]{2,1,0:T(8,128)(2,1)S(1)} %get-tuple-element.34.own, bf16[2,32,512]{2,1,0:T(8,128)(2,1)S(1)} %collective-permute-done.6.own_edge, bf16[2,128,512]{2,1,0:T(8,128)(2,1)S(1)} %collective-permute-done.7.other, bf16[2,32,512]{2,1,0:T(8,128)(2,1)S(1)} %collective-permute-done.8.other_edge, ...), custom_call_target="tpu_custom_call" | custom-call | bytes 262144 | tf_op jit(solution)/shard_map/pallas_call | solution.py:19
  (2 shorter events, 0.0 us)
Async XLA Ops:
  0.0 9.5 %collective-permute-start.1 = (bf16[2,512,128]{2,1,0:T(8,128)(2,1)}, bf16[2,512,128]{2,1,0:T(8,128)(2,1)S(1)}, u32[]{:S(2)}, u32[]{:S(2)}) collective-permute-start(bf16[2,512,128]{2,1,0:T(8,128)(2,1)} %bitcast.3), channel_id=1, source_target_pairs={{0,2},{2,0},{4,6},{6,4},{8,10},{10,8},{12,14},{14,12},{1,3},{3,1},... | collective-permute-start | bytes 786440 | tf_op jit(solution)/shard_map/ppermute | solution.py:32
  2.9 1.0 %copy-start.2 = (bf16[1,2,512,128]{3,2,1,0:T(8,128)(2,1)S(1)}, bf16[1,2,512,128]{3,2,1,0:T(8,128)(2,1)}, u32[]{:S(2)}) copy-start(bf16[1,2,512,128]{3,2,1,0:T(8,128)(2,1)} %param.7) | copy-start | bytes 786436
  4.1 5.6 %copy-start.3 = (s32[3,2,1024]{2,1,0:T(2,128)S(1)}, s32[3,2,1024]{2,1,0:T(2,128)}, u32[]{:S(2)}) copy-start(s32[3,2,1024]{2,1,0:T(2,128)} %off.5) | copy-start | bytes 73732
  4.1 5.6 %copy-start.4 = (s32[3,2,1024]{2,1,0:T(2,128)S(1)}, s32[3,2,1024]{2,1,0:T(2,128)}, u32[]{:S(2)}) copy-start(s32[3,2,1024]{2,1,0:T(2,128)} %idx.5) | copy-start | bytes 73732
  4.1 5.6 %copy-start.5 = (f32[3,2,1024]{2,1,0:T(2,128)S(1)}, f32[3,2,1024]{2,1,0:T(2,128)}, u32[]{:S(2)}) copy-start(f32[3,2,1024]{2,1,0:T(2,128)} %base.5) | copy-start | bytes 73732
  4.1 5.6 %copy-start.6 = (f32[3,2,1024]{2,1,0:T(2,128)S(1)}, f32[3,2,1024]{2,1,0:T(2,128)}, u32[]{:S(2)}) copy-start(f32[3,2,1024]{2,1,0:T(2,128)} %slope.5) | copy-start | bytes 73732
  4.1 6.7 %collective-permute-start = (bf16[2,32,512]{2,1,0:T(8,128)(2,1)S(1)}, bf16[2,32,512]{2,1,0:T(8,128)(2,1)S(1)}, u32[]{:S(2)}, u32[]{:S(2)}) collective-permute-start(bf16[2,32,512]{2,1,0:T(8,128)(2,1)S(1)} %get-tuple-element.23), channel_id=1, source_target_pairs={{0,1},{1,0},{2,3},{3,2},{4,5},{5,4},{6,7},{7,6},{8,9},{9,8},{10,11... | collective-permute-start | bytes 196616 | tf_op jit(solution)/shard_map/ppermute | solution.py:32
  9.5 0.7 %copy-start.7 = (f32[16,8]{0,1:T(8,128)S(1)}, f32[16,8]{0,1:T(8,128)}, u32[]{:S(2)}) copy-start(f32[16,8]{0,1:T(8,128)} %param.11) | copy-start | bytes 1540
  9.6 1.3 %collective-permute-start.2 = (bf16[2,32,512]{2,1,0:T(8,128)(2,1)S(1)}, bf16[2,32,512]{2,1,0:T(8,128)(2,1)S(1)}, u32[]{:S(2)}, u32[]{:S(2)}) collective-permute-start(bf16[2,32,512]{2,1,0:T(8,128)(2,1)S(1)} %get-tuple-element.25), channel_id=1, source_target_pairs={{0,1},{1,0},{2,3},{3,2},{4,5},{5,4},{6,7},{7,6},{8,9},{9,8},{10,11... | collective-permute-start | bytes 196616 | tf_op jit(solution)/shard_map/ppermute | solution.py:32
  10.9 1.2 %copy-start = (bf16[1024,512]{1,0:T(8,128)(2,1)S(1)}, bf16[1024,512]{1,0:T(8,128)(2,1)}, u32[]{:S(2)}) copy-start(bf16[1024,512]{1,0:T(8,128)(2,1)} %matrix.5) | copy-start | bytes 3145732
  12.1 12.5 %copy-start.1 = (bf16[1024,512]{1,0:T(8,128)(2,1)S(1)}, bf16[1024,512]{1,0:T(8,128)(2,1)}, u32[]{:S(2)}) copy-start(bf16[1024,512]{1,0:T(8,128)(2,1)} %matrix.5) | copy-start | bytes 3145732
  14.9 8.5 %collective-permute-start.4 = (bf16[2,128,512]{2,1,0:T(8,128)(2,1)S(1)}, bf16[2,128,512]{2,1,0:T(8,128)(2,1)S(1)}, u32[]{:S(2)}, u32[]{:S(2)}) collective-permute-start(bf16[2,128,512]{2,1,0:T(8,128)(2,1)S(1)} %get-tuple-element.29.own), channel_id=1, source_target_pairs={{0,4},{2,6},{4,0},{6,2},{8,12},{10,14},{12,8},{14,10},{1,5},{3,7},... | collective-permute-start | bytes 786440 | tf_op jit(solution)/shard_map/ppermute | solution.py:32
  16.7 7.3 %collective-permute-start.3 = (bf16[2,32,512]{2,1,0:T(8,128)(2,1)S(1)}, bf16[2,32,512]{2,1,0:T(8,128)(2,1)S(1)}, u32[]{:S(2)}, u32[]{:S(2)}) collective-permute-start(bf16[2,32,512]{2,1,0:T(8,128)(2,1)S(1)} %get-tuple-element.30), channel_id=1, source_target_pairs={{0,1},{1,0},{2,3},{3,2},{4,5},{5,4},{6,7},{7,6},{8,9},{9,8},{10,11... | collective-permute-start | bytes 196616 | tf_op jit(solution)/shard_map/ppermute | solution.py:32
  23.4 1.3 %collective-permute-start.5 = (bf16[2,32,512]{2,1,0:T(8,128)(2,1)S(1)}, bf16[2,32,512]{2,1,0:T(8,128)(2,1)S(1)}, u32[]{:S(2)}, u32[]{:S(2)}) collective-permute-start(bf16[2,32,512]{2,1,0:T(8,128)(2,1)S(1)} %constant_dynamic-slice_fusion.1), channel_id=1, source_target_pairs={{0,1},{1,0},{2,3},{3,2},{4,5},{5,4},{6,7},{7,6},{8,9},{9,8},{10,11... | collective-permute-start | bytes 196616 | tf_op jit(solution)/shard_map/ppermute | solution.py:32
  27.4 15.1 %collective-permute-start.7 = (bf16[2,128,512]{2,1,0:T(8,128)(2,1)S(1)}, bf16[2,128,512]{2,1,0:T(8,128)(2,1)S(1)}, u32[]{:S(2)}, u32[]{:S(2)}) collective-permute-start(bf16[2,128,512]{2,1,0:T(8,128)(2,1)S(1)} %get-tuple-element.34.own), channel_id=1, source_target_pairs={{0,8},{2,10},{4,12},{6,14},{8,0},{10,2},{12,4},{14,6},{1,9},{3,11}... | collective-permute-start | bytes 786440 | tf_op jit(solution)/shard_map/ppermute | solution.py:32
  30.2 12.9 %collective-permute-start.6 = (bf16[2,32,512]{2,1,0:T(8,128)(2,1)S(1)}, bf16[2,32,512]{2,1,0:T(8,128)(2,1)S(1)}, u32[]{:S(2)}, u32[]{:S(2)}) collective-permute-start(bf16[2,32,512]{2,1,0:T(8,128)(2,1)S(1)} %get-tuple-element.35), channel_id=1, source_target_pairs={{0,1},{1,0},{2,3},{3,2},{4,5},{5,4},{6,7},{7,6},{8,9},{9,8},{10,11... | collective-permute-start | bytes 196616 | tf_op jit(solution)/shard_map/ppermute | solution.py:32
  42.4 1.3 %collective-permute-start.8 = (bf16[2,32,512]{2,1,0:T(8,128)(2,1)S(1)}, bf16[2,32,512]{2,1,0:T(8,128)(2,1)S(1)}, u32[]{:S(2)}, u32[]{:S(2)}) collective-permute-start(bf16[2,32,512]{2,1,0:T(8,128)(2,1)S(1)} %constant_dynamic-slice_fusion), channel_id=1, source_target_pairs={{0,1},{1,0},{2,3},{3,2},{4,5},{5,4},{6,7},{7,6},{8,9},{9,8},{10,11... | collective-permute-start | bytes 196616 | tf_op jit(solution)/shard_map/ppermute | solution.py:32

commit v2 on v1

v2 whole, which is shorter than its diff:
```python
import functools

import jax
import jax.numpy as jnp
from jax import lax
from jax.experimental import pallas as pl
from jax.experimental.pallas import tpu as pltpu
from jax.sharding import PartitionSpec as P

HALO = 32
LANES = 128
ROWS = 8
KERNEL_VMEM = 8 << 20
VMEM = pl.BlockSpec(memory_space=pltpu.VMEM)
like = jax.ShapeDtypeStruct
f32, bf16 = jnp.float32, jnp.bfloat16


def run(kernel, outs, args, scratch=(), flops=0):
    size = sum(o.size * o.dtype.itemsize for o in [*outs, *args])
    return pl.pallas_call(
        kernel,
        out_shape=outs,
        in_specs=[VMEM] * len(args),
        out_specs=[VMEM] * len(outs),
        scratch_shapes=scratch,
        compiler_params=pltpu.CompilerParams(vmem_limit_bytes=KERNEL_VMEM),
        cost_estimate=pl.CostEstimate(flops=flops, bytes_accessed=size, transcendentals=0),
    )(*args)


def from_partner(value, axis, mask):
    pairs = [(source, source ^ mask) for source in range(lax.axis_size(axis))]
    return lax.ppermute(value, axis, pairs)


def first_bin(span, near, far):
    return pl.multiple_of(jnp.where(lax.axis_index("range") == 0, near, span - far), HALO)


def own_half(level):
    return lax.axis_index("aper") >> level & 1


def turn_kernel(image, turned, edge):
    span = turned.shape[1]
    for part in range(image.shape[0]):
        turned[part] = image[part].T
    edge[...] = turned[:, pl.ds(first_bin(span, span - HALO, span), HALO), :]


def halves_kernel(matrix, halves):
    angles = matrix.shape[1]
    for half in range(halves.shape[0]):
        halves[half] = matrix[half * angles : (half + 1) * angles, :].T


def make_tables(level, span, order, params, shift_ref, taps_ref, phase_ref):
    off, idx, base, slope, table = params
    angles = off.shape[2] // 2
    half = own_half(level)
    start = lax.axis_index("range") * span
    taps_count = table.shape[0]
    role = half if order == 0 else 1 - half
    for j in range(angles // LANES):
        lane = pl.ds(pl.multiple_of(half * angles + j * LANES, LANES), LANES)

        def row(ref):
            both = ref[level, :, lane]
            return jnp.broadcast_to(jnp.where(role == 0, both[0:1], both[1:2]), (ROWS, LANES))

        shift = row(off) + (HALO - 3)
        shift_ref[j] = shift
        which = row(idx)
        taps = jnp.zeros((taps_count, LANES), f32)
        for k in range(table.shape[1]):
            taps = jnp.where(which == k, table[:, k : k + 1], taps)
        odd = shift & 1
        zero = jnp.zeros((ROWS, LANES), f32)
        rows = [jnp.broadcast_to(taps[t : t + 1], (ROWS, LANES)) for t in range(taps_count)]
        for t in range(taps_count + 1):
            even_tap = rows[t] if t < taps_count else zero
            odd_tap = rows[t - 1] if t > 0 else zero
            taps_ref[j, t] = jnp.where(odd == 1, odd_tap, even_tap)
        s = row(slope)
        ramp = lax.broadcasted_iota(jnp.int32, (ROWS, LANES), 0)
        near = row(base) + s * (ramp + start).astype(f32)
        c0, s0 = jnp.cos(near), jnp.sin(near)
        steps = span // ROWS
        far_at = lax.broadcasted_iota(jnp.int32, (steps, LANES), 0) * ROWS
        far = jnp.broadcast_to(s[0:1], (steps, LANES)) * far_at.astype(f32)
        c1, s1 = jnp.cos(far), jnp.sin(far)
        for u in range(steps):
            cu, su = c1[u : u + 1], s1[u : u + 1]
            at = pl.ds(u * ROWS, ROWS)
            phase_ref[0, j, at, :] = c0 * cu - s0 * su
            phase_ref[1, j, at, :] = s0 * cu + c0 * su


def interpolate(level, span, pieces, halves, slab):
    half = own_half(level)
    rows = jnp.concatenate([ref[part] for ref, _, _ in pieces for part in range(ref.shape[0])], 0)
    inter = jnp.dot(rows, halves[half], preferred_element_type=f32).astype(bf16).astype(f32)
    at = 0
    for ref, near, far in pieces:
        place = pl.ds(pl.multiple_of(first_bin(span, near, far) + HALO, HALO), far - near)
        for part in range(ref.shape[0]):
            for j in range(inter.shape[1] // LANES):
                slab[part, j, place, :] = inter[at : at + far - near, j * LANES : (j + 1) * LANES]
            at += far - near
    place = pl.ds(pl.multiple_of(first_bin(span, -HALO, 0) + HALO, HALO), HALO)
    slab[:, :, place, :] = jnp.zeros((slab.shape[0], slab.shape[1], HALO, LANES), f32)


def pick(shift, bit, a, b):
    count = a.shape[0]
    mask = jnp.broadcast_to((shift >> bit & 1 == 1)[None], (count // ROWS, ROWS, LANES))
    return jnp.where(mask.reshape(count, LANES), a, b)


def shift_filter(slab, part, j, start, shift, taps, tmp, count):
    v = slab[part, j, pl.ds(start, count + 64), :]
    v = jnp.concatenate([pick(shift, 5, v[32 : count + 64], v[: count + 32]), v[count + 32 : count + 40]], 0)
    v = pick(shift, 4, v[16 : count + 40], v[: count + 24])
    v = pick(shift, 3, v[8 : count + 24], v[: count + 16])
    tmp[0, 0 : count + 16] = v
    v = pick(shift, 2, tmp[0, 4 : count + 20], v)
    tmp[1, 0 : count + 16] = v
    v = pick(shift, 1, tmp[1, 2 : count + 18], v)
    tmp[2, 0 : count + 16] = v
    total = None
    for t in range(taps.shape[0]):
        tap = jnp.broadcast_to(taps[t][None], (count // ROWS, ROWS, LANES)).reshape(count, LANES)
        term = tap * (v[:count] if t == 0 else tmp[2, t : t + count])
        total = term if total is None else total + term
    return total


def terms(slab, j, start, count, tables, tmp):
    shift_ref, taps_ref, phase_ref = tables
    shift, taps = shift_ref[j], taps_ref[j]
    re = shift_filter(slab, 0, j, start, shift, taps, tmp.at[0], count)
    im = shift_filter(slab, 1, j, start, shift, taps, tmp.at[1], count)
    c = phase_ref[0, j, pl.ds(start, count), :]
    s = phase_ref[1, j, pl.ds(start, count), :]
    return re * c - im * s, re * s + im * c


def own_kernel(level, span, stretches, *refs):
    pieces = [(ref, *stretch) for ref, stretch in zip(refs, stretches)]
    refs = refs[len(stretches) :]
    halves, params, (acc, *others), (slab, tmp, *own) = refs[0], refs[1:6], refs[6:10], refs[10:]
    make_tables(level, span, 0, params, *own)
    make_tables(level, span, 1, params, *others)
    interpolate(level, span, pieces, halves, slab)

    def tile(j, carry):
        re, im = terms(slab, j, 0, span, own, tmp)
        acc[0, j], acc[1, j] = re, im
        return carry

    lax.fori_loop(0, acc.shape[1], tile, 0)


def merge_kernel(level, span, stretches, near, far, final, *refs):
    pieces = [(ref, *stretch) for ref, stretch in zip(refs, stretches)]
    refs = refs[len(stretches) :]
    halves, acc, tables, out, slab, tmp = refs[0], refs[1], refs[2:5], refs[5], refs[6], refs[7]
    merged = refs[8] if final else out
    interpolate(level, span, pieces, halves, slab)
    start, count = first_bin(span, near, far), far - near

    def tile(j, carry):
        lane = pl.ds(pl.multiple_of(j * LANES, LANES), LANES)
        re, im = terms(slab, j, start, count, tables, tmp)
        merged[0, :, lane] = (acc[0, j, pl.ds(start, count), :] + re).astype(bf16)
        merged[1, :, lane] = (acc[1, j, pl.ds(start, count), :] + im).astype(bf16)
        return carry

    lax.fori_loop(0, acc.shape[1], tile, 0)
    if final:
        for part in range(out.shape[0]):
            out[part] = merged[part].T


def body(images, interp_matrix, offsets, tap_index, tap_table, phase_base, phase_slope):
    image = images[0]
    parts, angles, span = image.shape
    levels = offsets.shape[0]
    tiles = angles // LANES
    taps_count = tap_table.shape[1]
    params = [offsets, tap_index, phase_base, phase_slope, tap_table.T]
    table_shapes = [((tiles, ROWS, LANES), jnp.int32), ((tiles, taps_count + 1, ROWS, LANES), f32), ((2, tiles, span, LANES), f32)]

    def work(count):
        return [pltpu.VMEM((parts, tiles, span + 2 * HALO, LANES), f32), pltpu.VMEM((parts, 3, count + 24, LANES), f32)]

    def turned(value):
        return run(turn_kernel, [like((parts, span, angles), bf16), like((parts, HALO, angles), bf16)], [value])

    def own(level, pieces):
        refs, stretches = zip(*pieces)
        return run(
            functools.partial(own_kernel, level, span, stretches),
            [like((parts, tiles, span, LANES), f32)] + [like(*shape) for shape in table_shapes],
            [*refs, halves, *params],
            work(span) + [pltpu.VMEM(*shape) for shape in table_shapes],
        )

    def merge(level, pieces, near, far, own_terms, final=False):
        refs, stretches = zip(*pieces)
        shape = image.shape if final else (parts, far - near, angles)
        return run(
            functools.partial(merge_kernel, level, span, stretches, near, far, final),
            [like(shape, bf16)],
            [*refs, halves, *own_terms],
            work(far - near) + ([pltpu.VMEM((parts, span, angles), bf16)] if final else []),
        )[0]

    def swap(value):
        return from_partner(value, "range", 1)

    received = from_partner(image, "aper", 1)
    (halves,) = run(halves_kernel, [like((2, angles, angles), bf16)], [interp_matrix])

    current, edge = turned(image)
    beyond = (span, span + HALO)
    own_terms = own(0, [(current, (0, span)), (swap(edge), beyond)])
    other, other_edge = turned(received)
    other_edge = swap(other_edge)
    cut = span - HALO
    outer = merge(0, [(other, (0, span))], 0, cut, own_terms)
    inner = merge(0, [(other, (0, span)), (other_edge, beyond)], cut, span, own_terms)

    other_outer = from_partner(outer, "aper", 2)
    other_inner = from_partner(inner, "aper", 2)
    own_terms = own(1, [(outer, (0, cut)), (inner, (cut, span)), (swap(inner), beyond)])
    middle = cut - HALO
    outer = merge(1, [(other_outer, (0, cut))], 0, middle, own_terms)
    inner = merge(
        1, [(other_outer, (0, cut)), (other_inner, (cut, span)), (swap(other_inner), beyond)], middle, span, own_terms
    )

    def last(value):
        start = jnp.where(lax.axis_index("range") == 0, span - middle - HALO, 0)
        return lax.dynamic_slice_in_dim(value, start, HALO, 1)

    other_outer = from_partner(outer, "aper", 4)
    other_inner = from_partner(inner, "aper", 4)
    own_terms = own(2, [(outer, (0, middle)), (inner, (middle, span)), (swap(last(inner)), beyond)])
    pieces = [(other_outer, (0, middle)), (other_inner, (middle, span)), (swap(last(other_inner)), beyond)]
    return merge(2, pieces, 0, span, own_terms, True)[None]


def solution(mesh):
    return jax.shard_map(
        body,
        mesh=mesh,
        in_specs=(P(("scene", "aper"), None, None, "range"), P(), P(), P(), P(), P(), P()),
        out_specs=P(("scene", "aper"), None, None, "range"),
        check_vma=False,
    )
```

time: 47.4 us -> 38.9 us (0.82)
  waiting for transfers between devices: 25.5 us -> 17.8 us
  Pallas kernels: 11 us -> 9.19 us
  starting transfers between devices: 7.8 us -> 8.89 us
    ppermute x9 -> x11, waiting for transfers between devices: 25.5 us -> 17.8 us  [from_partner(): return lax.ppermute(value, axis, pairs)]
    pallas_call x8 -> x11, Pallas kernels: 11 us -> 9.19 us  [run(): pl.pallas_call(kernel, out_shape=outs, in_specs=[VMEM] * len(args), out_s...]
    ppermute x9 -> x11, starting transfers between devices: 7.8 us -> 8.89 us  [from_partner(): return lax.ppermute(value, axis, pairs)]
    unnamed x16 -> x14, local copies, waits for them, and re-layouts: 2.67 us -> 2.64 us
  transfers between devices with their start and end apart: 9 -> 11, of which waited for: 6 -> 4; matrix products, arithmetic and copies ran while one was open for 0% -> 0% of each run, Pallas kernels for 4% -> 17%
where the time goes in v2:
time: 38.9 us; the launch traced here: 38.7 us
  waiting for transfers between devices  17.8 us (46%)
  Pallas kernels  9.19 us (24%)
  starting transfers between devices  8.89 us (23%)
  local copies, waits for them, and re-layouts  2.65 us (7%)
    ppermute x11, waiting for transfers between devices, from_partner(): return lax.ppermute(value, axis, pairs)  17.8 us
    pallas_call x11, Pallas kernels, run(): pl.pallas_call(kernel, out_shape=outs, in_specs=[VMEM] * len(args), out_s...  9.19 us
    ppermute x11, starting transfers between devices, from_partner(): return lax.ppermute(value, axis, pairs)  8.89 us
    unnamed x14, local copies, waits for them, and re-layouts  2.64 us
  transfers between devices with their start and end apart: 11, of which 4 were waited for; matrix products, arithmetic and copies ran while one was open for 0% of the time, Pallas kernels for 17%

profile of v2, /device:TPU:0, one launch (start us, length us, event | category | flops | bytes accessed | tf_op | source)
XLA Modules:
  0.0 38.7 jit_solution(8244420433963341692)
XLA Ops:
  0.0 2.9 %collective-permute-start = (bf16[2,512,128]{2,1,0:T(8,128)(2,1)}, bf16[2,512,128]{2,1,0:T(8,128)(2,1)S(1)}, u32[]{:S(2)}, u32[]{:S(2)}) collective-permute-start(bf16[2,512,128]{2,1,0:T(8,128)(2,1)} %bitcast.3), channel_id=1, source_target_pairs={{0,2},{2,0},{4,6},{6,4},{8,10},{10,8},{12,14},{14,12},{1,3},{3,1},... | collective-permute-start | bytes 786440 | tf_op jit(solution)/shard_map/ppermute | solution.py:34
  2.9 0.0 copy-start.1
  2.9 1.0 %copy-done.1 = bf16[1,2,512,128]{3,2,1,0:T(8,128)(2,1)S(1)} copy-done((bf16[1,2,512,128]{3,2,1,0:T(8,128)(2,1)S(1)}, bf16[1,2,512,128]{3,2,1,0:T(8,128)(2,1)}, u32[]{:S(2)}) %copy-start.1) | copy-done | bytes 262168
  3.9 0.1 shard_map.75
  4.0 0.1 collective-permute-start.1
  4.1 0.0 copy-start
  4.1 1.2 %copy-done = bf16[1024,512]{1,0:T(8,128)(2,1)S(1)} copy-done((bf16[1024,512]{1,0:T(8,128)(2,1)S(1)}, bf16[1024,512]{1,0:T(8,128)(2,1)}, u32[]{:S(2)}) %copy-start) | copy-done | bytes 1048600
  5.4 0.0 copy-start.2
  5.4 0.0 copy-start.3
  5.4 0.0 copy-start.4
  5.4 0.0 copy-start.5
  5.4 0.0 copy-start.6
  5.4 0.3 shard_map.74.refs_2_.refs_1_.refs_3_
  5.7 0.0 collective-permute-done.1.refs_1_
  5.7 0.4 copy-done.2
  6.1 0.0 copy-done.3
  6.1 0.0 copy-done.4
  6.1 0.0 copy-done.5
  6.1 0.0 copy-done.6
  6.1 1.4 %shard_map.76 = (f32[2,4,128,128]{3,2,1,0:T(8,128)S(1)}, s32[4,8,128]{2,1,0:T(8,128)S(1)}, f32[4,9,8,128]{3,2,1,0:T(8,128)S(1)}, f32[2,4,128,128]{3,2,1,0:T(8,128)S(1)}) custom-call(bf16[2,128,512]{2,1,0:T(8,128)(2,1)S(1)} %get-tuple-element.22.refs_0_, bf16[2,32,512]{2,1,0:T(8,128)(2,1)S(1)} %collective-permute-done.1.refs_1_, ...), custom_call_target="tpu_custom_call" | custom-call | bytes 2687488 | tf_op jit(solution)/shard_map/pallas_call | solution.py:21
  7.5 1.9 %collective-permute-done.image = bf16[2,512,128]{2,1,0:T(8,128)(2,1)S(1)} collective-permute-done((bf16[2,512,128]{2,1,0:T(8,128)(2,1)}, bf16[2,512,128]{2,1,0:T(8,128)(2,1)S(1)}, u32[]{:S(2)}, u32[]{:S(2)}) %collective-permute-start) | collective-permute-done | bytes 262176 | tf_op jit(solution)/shard_map/ppermute | solution.py:34
  9.5 0.1 shard_map.73
  9.6 0.1 collective-permute-start.3
  9.7 0.8 %shard_map.77.refs_0_ = bf16[2,96,512]{2,1,0:T(8,128)(2,1)S(1)} custom-call(bf16[2,128,512]{2,1,0:T(8,128)(2,1)S(1)} %get-tuple-element.21.refs_0_, bf16[2,512,512]{2,1,0:T(8,128)(2,1)S(1)} %shard_map.74.refs_2_.refs_1_.refs_3_, f32[2,4,128,128]{3,2,1,0:T(8,128)S(1)} %get-tuple-element.24.refs_2_.refs_3_, ...), custom_call_target="tpu_custom_call" | custom-call | bytes 2719744 | tf_op jit(solution)/shard_map/pallas_call | solution.py:21
  10.5 1.9 %collective-permute-start.2 = (bf16[2,96,512]{2,1,0:T(8,128)(2,1)S(1)}, bf16[2,96,512]{2,1,0:T(8,128)(2,1)S(1)}, u32[]{:S(2)}, u32[]{:S(2)}) collective-permute-start(bf16[2,96,512]{2,1,0:T(8,128)(2,1)S(1)} %shard_map.77.refs_0_), channel_id=1, source_target_pairs={{0,4},{2,6},{4,0},{6,2},{8,12},{10,14},{12,8},{14,10},{1,5},{3,7},... | collective-permute-start | bytes 589832 | tf_op jit(solution)/shard_map/ppermute | solution.py:34
  12.4 0.0 collective-permute-done.3.refs_1_
  12.4 0.5 %shard_map.78.refs_1_ = bf16[2,32,512]{2,1,0:T(8,128)(2,1)S(1)} custom-call(bf16[2,128,512]{2,1,0:T(8,128)(2,1)S(1)} %get-tuple-element.21.refs_0_, bf16[2,32,512]{2,1,0:T(8,128)(2,1)S(1)} %collective-permute-done.3.refs_1_, bf16[2,512,512]{2,1,0:T(8,128)(2,1)S(1)} %shard_map.74.refs_2_.refs_1_.refs_3_, ...), custom_call_target="tpu_custom_call" | custom-call | bytes 2654208 | tf_op jit(solution)/shard_map/pallas_call | solution.py:21
  12.9 0.4 %collective-permute-start.6 = (bf16[2,32,512]{2,1,0:T(8,128)(2,1)S(1)}, bf16[2,32,512]{2,1,0:T(8,128)(2,1)S(1)}, u32[]{:S(2)}, u32[]{:S(2)}) collective-permute-start(bf16[2,32,512]{2,1,0:T(8,128)(2,1)S(1)} %shard_map.78.refs_1_), channel_id=1, source_target_pairs={{0,4},{2,6},{4,0},{6,2},{8,12},{10,14},{12,8},{14,10},{1,5},{3,7},... | collective-permute-start | bytes 196616 | tf_op jit(solution)/shard_map/ppermute | solution.py:34
  13.3 0.0 collective-permute-start.4
  13.3 6.0 %collective-permute-done.6.refs_1_ = bf16[2,32,512]{2,1,0:T(8,128)(2,1)S(1)} collective-permute-done((bf16[2,32,512]{2,1,0:T(8,128)(2,1)S(1)}, bf16[2,32,512]{2,1,0:T(8,128)(2,1)S(1)}, u32[]{:S(2)}, u32[]{:S(2)}) %collective-permute-start.6) | collective-permute-done | bytes 65568 | tf_op jit(solution)/shard_map/ppermute | solution.py:34
  19.3 0.0 collective-permute-start.7
  19.3 0.0 collective-permute-done.4.refs_2_
  19.3 1.4 %shard_map.79 = (f32[2,4,128,128]{3,2,1,0:T(8,128)S(1)}, s32[4,8,128]{2,1,0:T(8,128)S(1)}, f32[4,9,8,128]{3,2,1,0:T(8,128)S(1)}, f32[2,4,128,128]{3,2,1,0:T(8,128)S(1)}) custom-call(bf16[2,96,512]{2,1,0:T(8,128)(2,1)S(1)} %shard_map.77.refs_0_, bf16[2,32,512]{2,1,0:T(8,128)(2,1)S(1)} %shard_map.78.refs_1_, ...), custom_call_target="tpu_custom_call" | custom-call | bytes 2687488 | tf_op jit(solution)/shard_map/pallas_call | solution.py:21
  20.7 0.0 collective-permute-done.7.refs_2_
  20.7 0.0 collective-permute-done.2.refs_0_
  20.7 0.7 %shard_map.81.refs_1_ = bf16[2,64,512]{2,1,0:T(8,128)(2,1)S(1)} custom-call(bf16[2,96,512]{2,1,0:T(8,128)(2,1)S(1)} %collective-permute-done.2.refs_0_, bf16[2,32,512]{2,1,0:T(8,128)(2,1)S(1)} %collective-permute-done.6.refs_1_, bf16[2,32,512]{2,1,0:T(8,128)(2,1)S(1)} %collective-permute-done.7.refs_2_, ...), custom_call_target="tpu_custom_call" | custom-call | bytes 2719744 | tf_op jit(solution)/shard_map/pallas_call | solution.py:21
  21.4 2.8 %collective-permute-start.8 = (bf16[2,64,512]{2,1,0:T(8,128)(2,1)S(1)}, bf16[2,64,512]{2,1,0:T(8,128)(2,1)S(1)}, u32[]{:S(2)}, u32[]{:S(2)}) collective-permute-start(bf16[2,64,512]{2,1,0:T(8,128)(2,1)S(1)} %shard_map.81.refs_1_), channel_id=1, source_target_pairs={{0,8},{2,10},{4,12},{6,14},{8,0},{10,2},{12,4},{14,6},{1,9},{3,11}... | collective-permute-start | bytes 393224 | tf_op jit(solution)/shard_map/ppermute | solution.py:34
  24.3 0.2 collective-permute-start.10
  24.5 0.6 %shard_map.80.refs_0_ = bf16[2,64,512]{2,1,0:T(8,128)(2,1)S(1)} custom-call(bf16[2,96,512]{2,1,0:T(8,128)(2,1)S(1)} %collective-permute-done.2.refs_0_, bf16[2,512,512]{2,1,0:T(8,128)(2,1)S(1)} %shard_map.74.refs_2_.refs_1_.refs_3_, f32[2,4,128,128]{3,2,1,0:T(8,128)S(1)} %get-tuple-element.29.refs_2_.refs_4_, ...), custom_call_target="tpu_custom_call" | custom-call | bytes 2588672 | tf_op jit(solution)/shard_map/pallas_call | solution.py:21
  25.1 0.4 %collective-permute-start.5 = (bf16[2,64,512]{2,1,0:T(8,128)(2,1)S(1)}, bf16[2,64,512]{2,1,0:T(8,128)(2,1)S(1)}, u32[]{:S(2)}, u32[]{:S(2)}) collective-permute-start(bf16[2,64,512]{2,1,0:T(8,128)(2,1)S(1)} %shard_map.80.refs_0_), channel_id=1, source_target_pairs={{0,8},{2,10},{4,12},{6,14},{8,0},{10,2},{12,4},{14,6},{1,9},{3,11}... | collective-permute-start | bytes 393224 | tf_op jit(solution)/shard_map/ppermute | solution.py:34
  25.5 8.8 %collective-permute-done.8.refs_1_ = bf16[2,64,512]{2,1,0:T(8,128)(2,1)S(1)} collective-permute-done((bf16[2,64,512]{2,1,0:T(8,128)(2,1)S(1)}, bf16[2,64,512]{2,1,0:T(8,128)(2,1)S(1)}, u32[]{:S(2)}, u32[]{:S(2)}) %collective-permute-start.8) | collective-permute-done | bytes 131104 | tf_op jit(solution)/shard_map/ppermute | solution.py:34
  34.3 0.0 collective-permute-start.9
  34.3 0.0 collective-permute-done.10.refs_2_
  34.3 1.4 %shard_map.82 = (f32[2,4,128,128]{3,2,1,0:T(8,128)S(1)}, s32[4,8,128]{2,1,0:T(8,128)S(1)}, f32[4,9,8,128]{3,2,1,0:T(8,128)S(1)}, f32[2,4,128,128]{3,2,1,0:T(8,128)S(1)}) custom-call(bf16[2,64,512]{2,1,0:T(8,128)(2,1)S(1)} %shard_map.80.refs_0_, bf16[2,64,512]{2,1,0:T(8,128)(2,1)S(1)} %shard_map.81.refs_1_, ...), custom_call_target="tpu_custom_call" | custom-call | bytes 2687488 | tf_op jit(solution)/shard_map/pallas_call | solution.py:21
  35.7 1.1 %collective-permute-done.5.refs_0_ = bf16[2,64,512]{2,1,0:T(8,128)(2,1)S(1)} collective-permute-done((bf16[2,64,512]{2,1,0:T(8,128)(2,1)S(1)}, bf16[2,64,512]{2,1,0:T(8,128)(2,1)S(1)}, u32[]{:S(2)}, u32[]{:S(2)}) %collective-permute-start.5) | collective-permute-done | bytes 131104 | tf_op jit(solution)/shard_map/ppermute | solution.py:34
  36.8 0.0 collective-permute-done.9.refs_2_
  36.9 1.8 %shard_map.83 = bf16[2,512,128]{2,1,0:T(8,128)(2,1)} custom-call(bf16[2,64,512]{2,1,0:T(8,128)(2,1)S(1)} %collective-permute-done.5.refs_0_, bf16[2,64,512]{2,1,0:T(8,128)(2,1)S(1)} %collective-permute-done.8.refs_1_, bf16[2,32,512]{2,1,0:T(8,128)(2,1)S(1)} %collective-permute-done.9.refs_2_, bf16[2,512,512]{2,1,0:T(8,128)(2,1)S(1)} %shard_map.74.refs_2_.refs_1_.refs_3_, ...), custom_call_target="tpu_custom_call" | custom-call | bytes 2850816 | tf_op jit(solution)/shard_map/pallas_call | solution.py:21
  (2 shorter events, 0.0 us)
Async XLA Ops:
  0.0 9.5 %collective-permute-start = (bf16[2,512,128]{2,1,0:T(8,128)(2,1)}, bf16[2,512,128]{2,1,0:T(8,128)(2,1)S(1)}, u32[]{:S(2)}, u32[]{:S(2)}) collective-permute-start(bf16[2,512,128]{2,1,0:T(8,128)(2,1)} %bitcast.3), channel_id=1, source_target_pairs={{0,2},{2,0},{4,6},{6,4},{8,10},{10,8},{12,14},{14,12},{1,3},{3,1},... | collective-permute-start | bytes 786440 | tf_op jit(solution)/shard_map/ppermute | solution.py:34
  2.9 1.0 %copy-start.1 = (bf16[1,2,512,128]{3,2,1,0:T(8,128)(2,1)S(1)}, bf16[1,2,512,128]{3,2,1,0:T(8,128)(2,1)}, u32[]{:S(2)}) copy-start(bf16[1,2,512,128]{3,2,1,0:T(8,128)(2,1)} %param.7) | copy-start | bytes 786436
  4.0 1.7 %collective-permute-start.1 = (bf16[2,32,512]{2,1,0:T(8,128)(2,1)S(1)}, bf16[2,32,512]{2,1,0:T(8,128)(2,1)S(1)}, u32[]{:S(2)}, u32[]{:S(2)}) collective-permute-start(bf16[2,32,512]{2,1,0:T(8,128)(2,1)S(1)} %get-tuple-element.23), channel_id=1, source_target_pairs={{0,1},{1,0},{2,3},{3,2},{4,5},{5,4},{6,7},{7,6},{8,9},{9,8},{10,11... | collective-permute-start | bytes 196616 | tf_op jit(solution)/shard_map/ppermute | solution.py:34
  4.1 1.2 %copy-start = (bf16[1024,512]{1,0:T(8,128)(2,1)S(1)}, bf16[1024,512]{1,0:T(8,128)(2,1)}, u32[]{:S(2)}) copy-start(bf16[1024,512]{1,0:T(8,128)(2,1)} %matrix.1) | copy-start | bytes 3145732
  5.4 0.7 %copy-start.2 = (s32[3,2,1024]{2,1,0:T(2,128)S(1)}, s32[3,2,1024]{2,1,0:T(2,128)}, u32[]{:S(2)}) copy-start(s32[3,2,1024]{2,1,0:T(2,128)} %refs_4_.5) | copy-start | bytes 73732
  5.4 0.8 %copy-start.3 = (s32[3,2,1024]{2,1,0:T(2,128)S(1)}, s32[3,2,1024]{2,1,0:T(2,128)}, u32[]{:S(2)}) copy-start(s32[3,2,1024]{2,1,0:T(2,128)} %refs_5_.5) | copy-start | bytes 73732
  5.4 0.8 %copy-start.4 = (f32[3,2,1024]{2,1,0:T(2,128)S(1)}, f32[3,2,1024]{2,1,0:T(2,128)}, u32[]{:S(2)}) copy-start(f32[3,2,1024]{2,1,0:T(2,128)} %refs_6_.5) | copy-start | bytes 73732
  5.4 0.8 %copy-start.5 = (f32[3,2,1024]{2,1,0:T(2,128)S(1)}, f32[3,2,1024]{2,1,0:T(2,128)}, u32[]{:S(2)}) copy-start(f32[3,2,1024]{2,1,0:T(2,128)} %refs_7_.3) | copy-start | bytes 73732
  5.4 0.8 %copy-start.6 = (f32[16,8]{0,1:T(8,128)S(1)}, f32[16,8]{0,1:T(8,128)}, u32[]{:S(2)}) copy-start(f32[16,8]{0,1:T(8,128)} %param.11) | copy-start | bytes 1540
  9.6 2.8 %collective-permute-start.3 = (bf16[2,32,512]{2,1,0:T(8,128)(2,1)S(1)}, bf16[2,32,512]{2,1,0:T(8,128)(2,1)S(1)}, u32[]{:S(2)}, u32[]{:S(2)}) collective-permute-start(bf16[2,32,512]{2,1,0:T(8,128)(2,1)S(1)} %get-tuple-element.28), channel_id=1, source_target_pairs={{0,1},{1,0},{2,3},{3,2},{4,5},{5,4},{6,7},{7,6},{8,9},{9,8},{10,11... | collective-permute-start | bytes 196616 | tf_op jit(solution)/shard_map/ppermute | solution.py:34
  10.5 10.3 %collective-permute-start.2 = (bf16[2,96,512]{2,1,0:T(8,128)(2,1)S(1)}, bf16[2,96,512]{2,1,0:T(8,128)(2,1)S(1)}, u32[]{:S(2)}, u32[]{:S(2)}) collective-permute-start(bf16[2,96,512]{2,1,0:T(8,128)(2,1)S(1)} %shard_map.77.refs_0_), channel_id=1, source_target_pairs={{0,4},{2,6},{4,0},{6,2},{8,12},{10,14},{12,8},{14,10},{1,5},{3,7},... | collective-permute-start | bytes 589832 | tf_op jit(solution)/shard_map/ppermute | solution.py:34
  12.9 6.4 %collective-permute-start.6 = (bf16[2,32,512]{2,1,0:T(8,128)(2,1)S(1)}, bf16[2,32,512]{2,1,0:T(8,128)(2,1)S(1)}, u32[]{:S(2)}, u32[]{:S(2)}) collective-permute-start(bf16[2,32,512]{2,1,0:T(8,128)(2,1)S(1)} %shard_map.78.refs_1_), channel_id=1, source_target_pairs={{0,4},{2,6},{4,0},{6,2},{8,12},{10,14},{12,8},{14,10},{1,5},{3,7},... | collective-permute-start | bytes 196616 | tf_op jit(solution)/shard_map/ppermute | solution.py:34
  13.3 6.0 %collective-permute-start.4 = (bf16[2,32,512]{2,1,0:T(8,128)(2,1)S(1)}, bf16[2,32,512]{2,1,0:T(8,128)(2,1)S(1)}, u32[]{:S(2)}, u32[]{:S(2)}) collective-permute-start(bf16[2,32,512]{2,1,0:T(8,128)(2,1)S(1)} %shard_map.78.refs_1_), channel_id=1, source_target_pairs={{0,1},{1,0},{2,3},{3,2},{4,5},{5,4},{6,7},{7,6},{8,9},{9,8},{10,11... | collective-permute-start | bytes 196616 | tf_op jit(solution)/shard_map/ppermute | solution.py:34
  19.3 1.4 %collective-permute-start.7 = (bf16[2,32,512]{2,1,0:T(8,128)(2,1)S(1)}, bf16[2,32,512]{2,1,0:T(8,128)(2,1)S(1)}, u32[]{:S(2)}, u32[]{:S(2)}) collective-permute-start(bf16[2,32,512]{2,1,0:T(8,128)(2,1)S(1)} %collective-permute-done.6.refs_1_), channel_id=1, source_target_pairs={{0,1},{1,0},{2,3},{3,2},{4,5},{5,4},{6,7},{7,6},{8,9},{9,8},{10,11... | collective-permute-start | bytes 196616 | tf_op jit(solution)/shard_map/ppermute | solution.py:34
  21.4 12.9 %collective-permute-start.8 = (bf16[2,64,512]{2,1,0:T(8,128)(2,1)S(1)}, bf16[2,64,512]{2,1,0:T(8,128)(2,1)S(1)}, u32[]{:S(2)}, u32[]{:S(2)}) collective-permute-start(bf16[2,64,512]{2,1,0:T(8,128)(2,1)S(1)} %shard_map.81.refs_1_), channel_id=1, source_target_pairs={{0,8},{2,10},{4,12},{6,14},{8,0},{10,2},{12,4},{14,6},{1,9},{3,11}... | collective-permute-start | bytes 393224 | tf_op jit(solution)/shard_map/ppermute | solution.py:34
  24.3 10.1 %collective-permute-start.10 = (bf16[2,32,512]{2,1,0:T(8,128)(2,1)S(1)}, bf16[2,32,512]{2,1,0:T(8,128)(2,1)S(1)}, u32[]{:S(2)}, u32[]{:S(2)}) collective-permute-start(bf16[2,32,512]{2,1,0:T(8,128)(2,1)S(1)} %constant_dynamic-slice_fusion), channel_id=1, source_target_pairs={{0,1},{1,0},{2,3},{3,2},{4,5},{5,4},{6,7},{7,6},{8,9},{9,8},{10,11... | collective-permute-start | bytes 196616 | tf_op jit(solution)/shard_map/ppermute | solution.py:34
  25.1 11.8 %collective-permute-start.5 = (bf16[2,64,512]{2,1,0:T(8,128)(2,1)S(1)}, bf16[2,64,512]{2,1,0:T(8,128)(2,1)S(1)}, u32[]{:S(2)}, u32[]{:S(2)}) collective-permute-start(bf16[2,64,512]{2,1,0:T(8,128)(2,1)S(1)} %shard_map.80.refs_0_), channel_id=1, source_target_pairs={{0,8},{2,10},{4,12},{6,14},{8,0},{10,2},{12,4},{14,6},{1,9},{3,11}... | collective-permute-start | bytes 393224 | tf_op jit(solution)/shard_map/ppermute | solution.py:34
  34.3 2.6 %collective-permute-start.9 = (bf16[2,32,512]{2,1,0:T(8,128)(2,1)S(1)}, bf16[2,32,512]{2,1,0:T(8,128)(2,1)S(1)}, u32[]{:S(2)}, u32[]{:S(2)}) collective-permute-start(bf16[2,32,512]{2,1,0:T(8,128)(2,1)S(1)} %constant_dynamic-slice_fusion.1), channel_id=1, source_target_pairs={{0,1},{1,0},{2,3},{3,2},{4,5},{5,4},{6,7},{7,6},{8,9},{9,8},{10,11... | collective-permute-start | bytes 196616 | tf_op jit(solution)/shard_map/ppermute | solution.py:34

commit v3 on v2

--- a/solution.py
+++ b/solution.py
@@ -10,6 +10,7 @@
 HALO = 32
 LANES = 128
 ROWS = 8
+STEP = 16
 KERNEL_VMEM = 8 << 20
 VMEM = pl.BlockSpec(memory_space=pltpu.VMEM)
 like = jax.ShapeDtypeStruct
@@ -29,13 +30,44 @@
     )(*args)
 
 
+def edge_kernel(value, after, edge):
+    width = value.shape[1]
+    edge[...] = value[:, pl.ds(first_bin(width, width - HALO, width), HALO), :]
+
+
+def inner_edge(value, after):
+    return pl.pallas_call(
+        edge_kernel,
+        out_shape=like((value.shape[0], HALO, value.shape[2]), value.dtype),
+        in_specs=[VMEM, pl.BlockSpec(memory_space=pl.ANY)],
+        out_specs=VMEM,
+        compiler_params=pltpu.CompilerParams(vmem_limit_bytes=KERNEL_VMEM),
+        cost_estimate=pl.CostEstimate(flops=0, bytes_accessed=0, transcendentals=0),
+    )(value, after)
+
+
+def after_kernel(value, token, out):
+    out[...] = value[...]
+
+
+def after(value, token):
+    return pl.pallas_call(
+        after_kernel,
+        out_shape=like(value.shape, value.dtype),
+        in_specs=[VMEM, pl.BlockSpec(memory_space=pl.ANY)],
+        out_specs=VMEM,
+        compiler_params=pltpu.CompilerParams(vmem_limit_bytes=KERNEL_VMEM),
+        cost_estimate=pl.CostEstimate(flops=0, bytes_accessed=0, transcendentals=0),
+    )(value, token)
+
+
 def from_partner(value, axis, mask):
     pairs = [(source, source ^ mask) for source in range(lax.axis_size(axis))]
     return lax.ppermute(value, axis, pairs)
 
 
 def first_bin(span, near, far):
-    return pl.multiple_of(jnp.where(lax.axis_index("range") == 0, near, span - far), HALO)
+    return pl.multiple_of(jnp.where(lax.axis_index("range") == 0, near, span - far), STEP)
 
 
 def own_half(level):
@@ -103,7 +135,7 @@
     inter = jnp.dot(rows, halves[half], preferred_element_type=f32).astype(bf16).astype(f32)
     at = 0
     for ref, near, far in pieces:
-        place = pl.ds(pl.multiple_of(first_bin(span, near, far) + HALO, HALO), far - near)
+        place = pl.ds(pl.multiple_of(first_bin(span, near, far) + HALO, STEP), far - near)
         for part in range(ref.shape[0]):
             for j in range(inter.shape[1] // LANES):
                 slab[part, j, place, :] = inter[at : at + far - near, j * LANES : (j + 1) * LANES]
@@ -165,16 +197,23 @@
 def merge_kernel(level, span, stretches, near, far, final, *refs):
     pieces = [(ref, *stretch) for ref, stretch in zip(refs, stretches)]
     refs = refs[len(stretches) :]
-    halves, acc, tables, out, slab, tmp = refs[0], refs[1], refs[2:5], refs[5], refs[6], refs[7]
-    merged = refs[8] if final else out
+    halves, acc, tables = refs[0], refs[1], refs[2:5]
+    start, count = first_bin(span, near, far), far - near
+    if final:
+        out, slab, tmp, merged = refs[-4:]
+        if near > 0:
+            merged[:, pl.ds(first_bin(span, 0, near), near), :] = refs[5][...]
+        into = start
+    else:
+        merged, slab, tmp = refs[5:]
+        into = 0
     interpolate(level, span, pieces, halves, slab)
-    start, count = first_bin(span, near, far), far - near
 
     def tile(j, carry):
         lane = pl.ds(pl.multiple_of(j * LANES, LANES), LANES)
         re, im = terms(slab, j, start, count, tables, tmp)
-        merged[0, :, lane] = (acc[0, j, pl.ds(start, count), :] + re).astype(bf16)
-        merged[1, :, lane] = (acc[1, j, pl.ds(start, count), :] + im).astype(bf16)
+        merged[0, pl.ds(into, count), lane] = (acc[0, j, pl.ds(start, count), :] + re).astype(bf16)
+        merged[1, pl.ds(into, count), lane] = (acc[1, j, pl.ds(start, count), :] + im).astype(bf16)
         return carry
 
     lax.fori_loop(0, acc.shape[1], tile, 0)
@@ -207,13 +246,13 @@
             work(span) + [pltpu.VMEM(*shape) for shape in table_shapes],
         )
 
-    def merge(level, pieces, near, far, own_terms, final=False):
+    def merge(level, pieces, near, far, own_terms, ready=None, final=False):
         refs, stretches = zip(*pieces)
         shape = image.shape if final else (parts, far - near, angles)
         return run(
             functools.partial(merge_kernel, level, span, stretches, near, far, final),
             [like(shape, bf16)],
-            [*refs, halves, *own_terms],
+            [*refs, halves, *own_terms] + ([ready] if ready is not None else []),
             work(far - near) + ([pltpu.VMEM((parts, span, angles), bf16)] if final else []),
         )[0]
 
@@ -228,28 +267,36 @@
     own_terms = own(0, [(current, (0, span)), (swap(edge), beyond)])
     other, other_edge = turned(received)
     other_edge = swap(other_edge)
-    cut = span - HALO
+    cut = 96
     outer = merge(0, [(other, (0, span))], 0, cut, own_terms)
-    inner = merge(0, [(other, (0, span)), (other_edge, beyond)], cut, span, own_terms)
+    pieces = [(other, (0, span)), (other_edge, beyond)]
+    inner = merge(0, pieces, cut, span, own_terms)
 
     other_outer = from_partner(outer, "aper", 2)
     other_inner = from_partner(inner, "aper", 2)
-    own_terms = own(1, [(outer, (0, cut)), (inner, (cut, span)), (swap(inner), beyond)])
-    middle = cut - HALO
+    own_edge = swap(inner_edge(inner, outer))
+    own_terms = own(1, [(outer, (0, cut)), (inner, (cut, span)), (own_edge, beyond)])
+    middle = 64
+    last = span - HALO
     outer = merge(1, [(other_outer, (0, cut))], 0, middle, own_terms)
-    inner = merge(
-        1, [(other_outer, (0, cut)), (other_inner, (cut, span)), (swap(other_inner), beyond)], middle, span, own_terms
-    )
-
-    def last(value):
-        start = jnp.where(lax.axis_index("range") == 0, span - middle - HALO, 0)
-        return lax.dynamic_slice_in_dim(value, start, HALO, 1)
+    other_edge = swap(inner_edge(other_inner, outer))
+    pieces = [(other_outer, (0, cut)), (other_inner, (cut, span)), (other_edge, beyond)]
+    edge = merge(1, pieces, last, span, own_terms)
+    inner = merge(1, pieces, middle, last, own_terms)
 
     other_outer = from_partner(outer, "aper", 4)
+    other_edge = from_partner(edge, "aper", 4)
     other_inner = from_partner(inner, "aper", 4)
-    own_terms = own(2, [(outer, (0, middle)), (inner, (middle, span)), (swap(last(inner)), beyond)])
-    pieces = [(other_outer, (0, middle)), (other_inner, (middle, span)), (swap(last(other_inner)), beyond)]
-    return merge(2, pieces, 0, span, own_terms, True)[None]
+    own_edge = swap(edge)
+    own_terms = own(2, [(outer, (0, middle)), (inner, (middle, last)), (edge, (last, span)), (own_edge, beyond)])
+    pieces = [(other_outer, (0, middle)), (other_inner, (middle, last)), (other_edge, (last, span))]
+    pieces += [(swap(after(other_edge, own_terms[0])), beyond)]
+    first = middle - HALO
+    if first > 0:
+        outer = merge(2, [(other_outer, (0, middle))], 0, first, own_terms)
+    else:
+        outer = None
+    return merge(2, pieces, first, span, own_terms, outer, True)[None]
 
 
 def solution(mesh):

time: 38.9 us -> 36 us (0.925)
  waiting for transfers between devices: 17.8 us -> 11.9 us
  starting transfers between devices: 8.89 us -> 11.2 us
  Pallas kernels: 9.19 us -> 9.89 us
    ppermute x11 -> x12, waiting for transfers between devices: 17.8 us -> 11.9 us  [from_partner(): return lax.ppermute(value, axis, pairs)]
    ppermute x11 -> x12, starting transfers between devices: 8.89 us -> 11.2 us  [from_partner(): return lax.ppermute(value, axis, pairs)]
    pallas_call x11 -> x13, Pallas kernels: 9.19 us -> 9.87 us  [run(): pl.pallas_call(kernel, out_shape=outs, in_specs=[VMEM] * len(args), out_s...]
  transfers between devices with their start and end apart: 11 -> 12, of which waited for: 4 -> 7; matrix products, arithmetic and copies ran while one was open for 0% -> 0% of each run, Pallas kernels for 17% -> 20%
where the time goes in v3:
time: 36 us; the launch traced here: 35.8 us
  waiting for transfers between devices  11.9 us (33%)
  starting transfers between devices  11.2 us (31%)
  Pallas kernels  9.89 us (27%)
  local copies, waits for them, and re-layouts  2.64 us (7%)
    ppermute x12, waiting for transfers between devices, from_partner(): return lax.ppermute(value, axis, pairs)  11.9 us
    ppermute x12, starting transfers between devices, from_partner(): return lax.ppermute(value, axis, pairs)  11.2 us
    pallas_call x13, Pallas kernels, run(): pl.pallas_call(kernel, out_shape=outs, in_specs=[VMEM] * len(args), out_s...  9.87 us
    unnamed x14, local copies, waits for them, and re-layouts  2.64 us
  transfers between devices with their start and end apart: 12, of which 7 were waited for; matrix products, arithmetic and copies ran while one was open for 0% of the time, Pallas kernels for 20%

profile of v3, /device:TPU:0, one launch (start us, length us, event | category | flops | bytes accessed | tf_op | source)
XLA Modules:
  0.0 35.8 jit_solution(17393652838053468977)
XLA Ops:
  0.0 2.9 %collective-permute-start = (bf16[2,512,128]{2,1,0:T(8,128)(2,1)}, bf16[2,512,128]{2,1,0:T(8,128)(2,1)S(1)}, u32[]{:S(2)}, u32[]{:S(2)}) collective-permute-start(bf16[2,512,128]{2,1,0:T(8,128)(2,1)} %bitcast.3), channel_id=1, source_target_pairs={{0,2},{2,0},{4,6},{6,4},{8,10},{10,8},{12,14},{14,12},{1,3},{3,1},... | collective-permute-start | bytes 786440 | tf_op jit(solution)/shard_map/ppermute | solution.py:66
  2.9 0.0 copy-start.1
  2.9 1.0 %copy-done.1 = bf16[1,2,512,128]{3,2,1,0:T(8,128)(2,1)S(1)} copy-done((bf16[1,2,512,128]{3,2,1,0:T(8,128)(2,1)S(1)}, bf16[1,2,512,128]{3,2,1,0:T(8,128)(2,1)}, u32[]{:S(2)}) %copy-start.1) | copy-done | bytes 262168
  3.9 0.1 shard_map.75
  4.0 0.1 collective-permute-start.1
  4.1 0.0 copy-start
  4.1 1.2 %copy-done = bf16[1024,512]{1,0:T(8,128)(2,1)S(1)} copy-done((bf16[1024,512]{1,0:T(8,128)(2,1)S(1)}, bf16[1024,512]{1,0:T(8,128)(2,1)}, u32[]{:S(2)}) %copy-start) | copy-done | bytes 1048600
  5.4 0.0 copy-start.2
  5.4 0.0 copy-start.6
  5.4 0.3 shard_map.74.refs_2_.refs_1_.refs_3_.refs_4_
  5.7 0.0 collective-permute-done.1.refs_1_
  5.7 0.4 %copy-done.2 = s32[3,2,1024]{2,1,0:T(2,128)S(1)} copy-done((s32[3,2,1024]{2,1,0:T(2,128)S(1)}, s32[3,2,1024]{2,1,0:T(2,128)}, u32[]{:S(2)}) %copy-start.2) | copy-done | bytes 24600
  6.1 0.0 copy-done.3
  6.1 0.0 copy-done.4
  6.1 0.0 copy-done.5
  6.1 0.0 copy-done.6
  6.1 1.4 %shard_map.76 = (f32[2,4,128,128]{3,2,1,0:T(8,128)S(1)}, s32[4,8,128]{2,1,0:T(8,128)S(1)}, f32[4,9,8,128]{3,2,1,0:T(8,128)S(1)}, f32[2,4,128,128]{3,2,1,0:T(8,128)S(1)}) custom-call(bf16[2,128,512]{2,1,0:T(8,128)(2,1)S(1)} %get-tuple-element.22.refs_0_, bf16[2,32,512]{2,1,0:T(8,128)(2,1)S(1)} %collective-permute-done.1.refs_1_, ...), custom_call_target="tpu_custom_call" | custom-call | bytes 2687488 | tf_op jit(solution)/shard_map/pallas_call | solution.py:22
  7.5 1.9 %collective-permute-done.image = bf16[2,512,128]{2,1,0:T(8,128)(2,1)S(1)} collective-permute-done((bf16[2,512,128]{2,1,0:T(8,128)(2,1)}, bf16[2,512,128]{2,1,0:T(8,128)(2,1)S(1)}, u32[]{:S(2)}, u32[]{:S(2)}) %collective-permute-start) | collective-permute-done | bytes 262176 | tf_op jit(solution)/shard_map/ppermute | solution.py:66
  9.5 0.1 shard_map.73
  9.6 0.8 %shard_map.77.after.refs_0_ = bf16[2,96,512]{2,1,0:T(8,128)(2,1)S(1)} custom-call(bf16[2,128,512]{2,1,0:T(8,128)(2,1)S(1)} %get-tuple-element.21.refs_0_, bf16[2,512,512]{2,1,0:T(8,128)(2,1)S(1)} %shard_map.74.refs_2_.refs_1_.refs_3_.refs_4_, f32[2,4,128,128]{3,2,1,0:T(8,128)S(1)} %get-tuple-element.24.refs_2_.refs_3_, ...), custom_call_target="tpu_custom_call" | custom-call | bytes 2719744 | tf_op jit(solution)/shard_map/pallas_call | solution.py:22
  10.4 1.9 %collective-permute-start.2 = (bf16[2,96,512]{2,1,0:T(8,128)(2,1)S(1)}, bf16[2,96,512]{2,1,0:T(8,128)(2,1)S(1)}, u32[]{:S(2)}, u32[]{:S(2)}) collective-permute-start(bf16[2,96,512]{2,1,0:T(8,128)(2,1)S(1)} %shard_map.77.after.refs_0_), channel_id=1, source_target_pairs={{0,4},{2,6},{4,0},{6,2},{8,12},{10,14},{12,8},{14,10},{1,5},{3,7},... | collective-permute-start | bytes 589832 | tf_op jit(solution)/shard_map/ppermute | solution.py:66
  12.3 0.0 collective-permute-start.3
  12.3 1.3 %collective-permute-done.3.refs_1_ = bf16[2,32,512]{2,1,0:T(8,128)(2,1)S(1)} collective-permute-done((bf16[2,32,512]{2,1,0:T(8,128)(2,1)S(1)}, bf16[2,32,512]{2,1,0:T(8,128)(2,1)S(1)}, u32[]{:S(2)}, u32[]{:S(2)}) %collective-permute-start.3) | collective-permute-done | bytes 65568 | tf_op jit(solution)/shard_map/ppermute | solution.py:66
  13.5 0.5 %shard_map.78.value.refs_1_ = bf16[2,32,512]{2,1,0:T(8,128)(2,1)S(1)} custom-call(bf16[2,128,512]{2,1,0:T(8,128)(2,1)S(1)} %get-tuple-element.21.refs_0_, bf16[2,32,512]{2,1,0:T(8,128)(2,1)S(1)} %collective-permute-done.3.refs_1_, bf16[2,512,512]{2,1,0:T(8,128)(2,1)S(1)} %shard_map.74.refs_2_.refs_1_.refs_3_.refs_4_, ...), custom_call_target="tpu_custom_call" | custom-call | bytes 2654208 | tf_op jit(solution)/shard_map/pallas_call | solution.py:22
  14.1 0.2 collective-permute-start.4
  14.3 0.2 collective-permute-start.6
  14.5 0.9 %collective-permute-done.4.refs_2_ = bf16[2,32,512]{2,1,0:T(8,128)(2,1)S(1)} collective-permute-done((bf16[2,32,512]{2,1,0:T(8,128)(2,1)S(1)}, bf16[2,32,512]{2,1,0:T(8,128)(2,1)S(1)}, u32[]{:S(2)}, u32[]{:S(2)}) %collective-permute-start.4) | collective-permute-done | bytes 65568 | tf_op jit(solution)/shard_map/ppermute | solution.py:66
  15.4 1.4 %shard_map.80 = (f32[2,4,128,128]{3,2,1,0:T(8,128)S(1)}, s32[4,8,128]{2,1,0:T(8,128)S(1)}, f32[4,9,8,128]{3,2,1,0:T(8,128)S(1)}, f32[2,4,128,128]{3,2,1,0:T(8,128)S(1)}) custom-call(bf16[2,96,512]{2,1,0:T(8,128)(2,1)S(1)} %shard_map.77.after.refs_0_, bf16[2,32,512]{2,1,0:T(8,128)(2,1)S(1)} %shard_map.78.value.refs_1_, ...), custom_call_target="tpu_custom_call" | custom-call | bytes 2687488 | tf_op jit(solution)/shard_map/pallas_call | solution.py:22
  16.8 0.0 collective-permute-done.2.refs_0_
  16.8 0.6 %shard_map.81.after.refs_0_ = bf16[2,64,512]{2,1,0:T(8,128)(2,1)S(1)} custom-call(bf16[2,96,512]{2,1,0:T(8,128)(2,1)S(1)} %collective-permute-done.2.refs_0_, bf16[2,512,512]{2,1,0:T(8,128)(2,1)S(1)} %shard_map.74.refs_2_.refs_1_.refs_3_.refs_4_, f32[2,4,128,128]{3,2,1,0:T(8,128)S(1)} %get-tuple-element.29.refs_2_.refs_4_, ...), custom_call_target="tpu_custom_call" | custom-call | bytes 2588672 | tf_op jit(solution)/shard_map/pallas_call | solution.py:22
  17.5 1.2 %collective-permute-done.6.value.refs_1_ = bf16[2,32,512]{2,1,0:T(8,128)(2,1)S(1)} collective-permute-done((bf16[2,32,512]{2,1,0:T(8,128)(2,1)S(1)}, bf16[2,32,512]{2,1,0:T(8,128)(2,1)S(1)}, u32[]{:S(2)}, u32[]{:S(2)}) %collective-permute-start.6) | collective-permute-done | bytes 65568 | tf_op jit(solution)/shard_map/ppermute | solution.py:66
  18.7 0.0 collective-permute-start.7
  18.7 2.7 %collective-permute-start.5 = (bf16[2,64,512]{2,1,0:T(8,128)(2,1)S(1)}, bf16[2,64,512]{2,1,0:T(8,128)(2,1)S(1)}, u32[]{:S(2)}, u32[]{:S(2)}) collective-permute-start(bf16[2,64,512]{2,1,0:T(8,128)(2,1)S(1)} %shard_map.81.after.refs_0_), channel_id=1, source_target_pairs={{0,8},{2,10},{4,12},{6,14},{8,0},{10,2},{12,4},{14,6},{1,9},{3,11}... | collective-permute-start | bytes 393224 | tf_op jit(solution)/shard_map/ppermute | solution.py:66
  21.4 0.0 collective-permute-done.7.refs_2_
  21.4 0.5 %shard_map.84.refs_2_ = bf16[2,32,512]{2,1,0:T(8,128)(2,1)S(1)} custom-call(bf16[2,96,512]{2,1,0:T(8,128)(2,1)S(1)} %collective-permute-done.2.refs_0_, bf16[2,32,512]{2,1,0:T(8,128)(2,1)S(1)} %collective-permute-done.6.value.refs_1_, bf16[2,32,512]{2,1,0:T(8,128)(2,1)S(1)} %collective-permute-done.7.refs_2_, ...), custom_call_target="tpu_custom_call" | custom-call | bytes 2654208 | tf_op jit(solution)/shard_map/pallas_call | solution.py:22
  21.9 0.2 collective-permute-start.10
  22.1 1.2 %collective-permute-start.9 = (bf16[2,32,512]{2,1,0:T(8,128)(2,1)S(1)}, bf16[2,32,512]{2,1,0:T(8,128)(2,1)S(1)}, u32[]{:S(2)}, u32[]{:S(2)}) collective-permute-start(bf16[2,32,512]{2,1,0:T(8,128)(2,1)S(1)} %shard_map.84.refs_2_), channel_id=1, source_target_pairs={{0,8},{2,10},{4,12},{6,14},{8,0},{10,2},{12,4},{14,6},{1,9},{3,11}... | collective-permute-start | bytes 196616 | tf_op jit(solution)/shard_map/ppermute | solution.py:66
  23.3 0.5 %shard_map.83.refs_1_ = bf16[2,32,512]{2,1,0:T(8,128)(2,1)S(1)} custom-call(bf16[2,96,512]{2,1,0:T(8,128)(2,1)S(1)} %collective-permute-done.2.refs_0_, bf16[2,32,512]{2,1,0:T(8,128)(2,1)S(1)} %collective-permute-done.6.value.refs_1_, bf16[2,32,512]{2,1,0:T(8,128)(2,1)S(1)} %collective-permute-done.7.refs_2_, ...), custom_call_target="tpu_custom_call" | custom-call | bytes 2654208 | tf_op jit(solution)/shard_map/pallas_call | solution.py:22
  23.9 1.8 %collective-permute-start.8 = (bf16[2,32,512]{2,1,0:T(8,128)(2,1)S(1)}, bf16[2,32,512]{2,1,0:T(8,128)(2,1)S(1)}, u32[]{:S(2)}, u32[]{:S(2)}) collective-permute-start(bf16[2,32,512]{2,1,0:T(8,128)(2,1)S(1)} %shard_map.83.refs_1_), channel_id=1, source_target_pairs={{0,8},{2,10},{4,12},{6,14},{8,0},{10,2},{12,4},{14,6},{1,9},{3,11}... | collective-permute-start | bytes 196616 | tf_op jit(solution)/shard_map/ppermute | solution.py:66
  25.7 0.0 collective-permute-done.10.refs_3_
  25.7 1.4 %shard_map.85 = (f32[2,4,128,128]{3,2,1,0:T(8,128)S(1)}, s32[4,8,128]{2,1,0:T(8,128)S(1)}, f32[4,9,8,128]{3,2,1,0:T(8,128)S(1)}, f32[2,4,128,128]{3,2,1,0:T(8,128)S(1)}) custom-call(bf16[2,64,512]{2,1,0:T(8,128)(2,1)S(1)} %shard_map.81.after.refs_0_, bf16[2,32,512]{2,1,0:T(8,128)(2,1)S(1)} %shard_map.83.refs_1_, bf16[2,32,512]{2,1,0:T(8,128)(2,1)S(1)} %shard_map.84.refs_2_, ...), custom_call_target="tpu_custom_call" | custom-call | bytes 2687488 | tf_op jit(solution)/shard_map/pallas_call | solution.py:22
  27.1 5.8 %collective-permute-done.9.value.refs_2_ = bf16[2,32,512]{2,1,0:T(8,128)(2,1)S(1)} collective-permute-done((bf16[2,32,512]{2,1,0:T(8,128)(2,1)S(1)}, bf16[2,32,512]{2,1,0:T(8,128)(2,1)S(1)}, u32[]{:S(2)}, u32[]{:S(2)}) %collective-permute-start.9) | collective-permute-done | bytes 65568 | tf_op jit(solution)/shard_map/ppermute | solution.py:66
  32.8 0.0 collective-permute-start.11
  32.9 0.0 collective-permute-done.5.refs_0_
  32.9 0.5 %shard_map.87.refs_9_ = bf16[2,32,512]{2,1,0:T(8,128)(2,1)S(1)} custom-call(bf16[2,64,512]{2,1,0:T(8,128)(2,1)S(1)} %collective-permute-done.5.refs_0_, bf16[2,512,512]{2,1,0:T(8,128)(2,1)S(1)} %shard_map.74.refs_2_.refs_1_.refs_3_.refs_4_, f32[2,4,128,128]{3,2,1,0:T(8,128)S(1)} %get-tuple-element.33.token.refs_2_.refs_5_, ...), custom_call_target="tpu_custom_call" | custom-call | bytes 2457600 | tf_op jit(solution)/shard_map/pallas_call | solution.py:22
  33.3 0.6 %collective-permute-done.8.refs_1_ = bf16[2,32,512]{2,1,0:T(8,128)(2,1)S(1)} collective-permute-done((bf16[2,32,512]{2,1,0:T(8,128)(2,1)S(1)}, bf16[2,32,512]{2,1,0:T(8,128)(2,1)S(1)}, u32[]{:S(2)}, u32[]{:S(2)}) %collective-permute-start.8) | collective-permute-done | bytes 65568 | tf_op jit(solution)/shard_map/ppermute | solution.py:66
  33.9 0.2 collective-permute-done.11.refs_3_
  34.1 1.7 %shard_map.88 = bf16[2,512,128]{2,1,0:T(8,128)(2,1)} custom-call(bf16[2,64,512]{2,1,0:T(8,128)(2,1)S(1)} %collective-permute-done.5.refs_0_, bf16[2,32,512]{2,1,0:T(8,128)(2,1)S(1)} %collective-permute-done.8.refs_1_, bf16[2,32,512]{2,1,0:T(8,128)(2,1)S(1)} %collective-permute-done.9.value.refs_2_, bf16[2,32,512]{2,1,0:T(8,128)(2,1)S(1)} %collective-permute-done.11.refs_3_, ...), custom_call_target="tpu_custom_call" | custom-call | bytes 2916352 | tf_op jit(solution)/shard_map/pallas_call | solution.py:22
  (6 shorter events, 0.0 us)
Async XLA Ops:
  0.0 9.5 %collective-permute-start = (bf16[2,512,128]{2,1,0:T(8,128)(2,1)}, bf16[2,512,128]{2,1,0:T(8,128)(2,1)S(1)}, u32[]{:S(2)}, u32[]{:S(2)}) collective-permute-start(bf16[2,512,128]{2,1,0:T(8,128)(2,1)} %bitcast.3), channel_id=1, source_target_pairs={{0,2},{2,0},{4,6},{6,4},{8,10},{10,8},{12,14},{14,12},{1,3},{3,1},... | collective-permute-start | bytes 786440 | tf_op jit(solution)/shard_map/ppermute | solution.py:66
  2.9 1.0 %copy-start.1 = (bf16[1,2,512,128]{3,2,1,0:T(8,128)(2,1)S(1)}, bf16[1,2,512,128]{3,2,1,0:T(8,128)(2,1)}, u32[]{:S(2)}) copy-start(bf16[1,2,512,128]{3,2,1,0:T(8,128)(2,1)} %param.7) | copy-start | bytes 786436
  4.0 1.7 %collective-permute-start.1 = (bf16[2,32,512]{2,1,0:T(8,128)(2,1)S(1)}, bf16[2,32,512]{2,1,0:T(8,128)(2,1)S(1)}, u32[]{:S(2)}, u32[]{:S(2)}) collective-permute-start(bf16[2,32,512]{2,1,0:T(8,128)(2,1)S(1)} %get-tuple-element.23), channel_id=1, source_target_pairs={{0,1},{1,0},{2,3},{3,2},{4,5},{5,4},{6,7},{7,6},{8,9},{9,8},{10,11... | collective-permute-start | bytes 196616 | tf_op jit(solution)/shard_map/ppermute | solution.py:66
  4.1 1.2 %copy-start = (bf16[1024,512]{1,0:T(8,128)(2,1)S(1)}, bf16[1024,512]{1,0:T(8,128)(2,1)}, u32[]{:S(2)}) copy-start(bf16[1024,512]{1,0:T(8,128)(2,1)} %matrix.1) | copy-start | bytes 3145732
  5.4 0.7 %copy-start.2 = (s32[3,2,1024]{2,1,0:T(2,128)S(1)}, s32[3,2,1024]{2,1,0:T(2,128)}, u32[]{:S(2)}) copy-start(s32[3,2,1024]{2,1,0:T(2,128)} %refs_5_.5) | copy-start | bytes 73732
  5.4 0.8 %copy-start.3 = (s32[3,2,1024]{2,1,0:T(2,128)S(1)}, s32[3,2,1024]{2,1,0:T(2,128)}, u32[]{:S(2)}) copy-start(s32[3,2,1024]{2,1,0:T(2,128)} %refs_6_.5) | copy-start | bytes 73732
  5.4 0.8 %copy-start.4 = (f32[3,2,1024]{2,1,0:T(2,128)S(1)}, f32[3,2,1024]{2,1,0:T(2,128)}, u32[]{:S(2)}) copy-start(f32[3,2,1024]{2,1,0:T(2,128)} %refs_7_.3) | copy-start | bytes 73732
  5.4 0.8 %copy-start.5 = (f32[3,2,1024]{2,1,0:T(2,128)S(1)}, f32[3,2,1024]{2,1,0:T(2,128)}, u32[]{:S(2)}) copy-start(f32[3,2,1024]{2,1,0:T(2,128)} %refs_8_.1) | copy-start | bytes 73732
  5.4 0.8 %copy-start.6 = (f32[16,8]{0,1:T(8,128)S(1)}, f32[16,8]{0,1:T(8,128)}, u32[]{:S(2)}) copy-start(f32[16,8]{0,1:T(8,128)} %param.11) | copy-start | bytes 1540
  10.4 6.4 %collective-permute-start.2 = (bf16[2,96,512]{2,1,0:T(8,128)(2,1)S(1)}, bf16[2,96,512]{2,1,0:T(8,128)(2,1)S(1)}, u32[]{:S(2)}, u32[]{:S(2)}) collective-permute-start(bf16[2,96,512]{2,1,0:T(8,128)(2,1)S(1)} %shard_map.77.after.refs_0_), channel_id=1, source_target_pairs={{0,4},{2,6},{4,0},{6,2},{8,12},{10,14},{12,8},{14,10},{1,5},{3,7},... | collective-permute-start | bytes 589832 | tf_op jit(solution)/shard_map/ppermute | solution.py:66
  12.3 1.3 %collective-permute-start.3 = (bf16[2,32,512]{2,1,0:T(8,128)(2,1)S(1)}, bf16[2,32,512]{2,1,0:T(8,128)(2,1)S(1)}, u32[]{:S(2)}, u32[]{:S(2)}) collective-permute-start(bf16[2,32,512]{2,1,0:T(8,128)(2,1)S(1)} %get-tuple-element.28), channel_id=1, source_target_pairs={{0,1},{1,0},{2,3},{3,2},{4,5},{5,4},{6,7},{7,6},{8,9},{9,8},{10,11... | collective-permute-start | bytes 196616 | tf_op jit(solution)/shard_map/ppermute | solution.py:66
  14.1 1.3 %collective-permute-start.4 = (bf16[2,32,512]{2,1,0:T(8,128)(2,1)S(1)}, bf16[2,32,512]{2,1,0:T(8,128)(2,1)S(1)}, u32[]{:S(2)}, u32[]{:S(2)}) collective-permute-start(bf16[2,32,512]{2,1,0:T(8,128)(2,1)S(1)} %shard_map.79), channel_id=1, source_target_pairs={{0,1},{1,0},{2,3},{3,2},{4,5},{5,4},{6,7},{7,6},{8,9},{9,8},{10,11... | collective-permute-start | bytes 196616 | tf_op jit(solution)/shard_map/ppermute | solution.py:66
  14.3 4.4 %collective-permute-start.6 = (bf16[2,32,512]{2,1,0:T(8,128)(2,1)S(1)}, bf16[2,32,512]{2,1,0:T(8,128)(2,1)S(1)}, u32[]{:S(2)}, u32[]{:S(2)}) collective-permute-start(bf16[2,32,512]{2,1,0:T(8,128)(2,1)S(1)} %shard_map.78.value.refs_1_), channel_id=1, source_target_pairs={{0,4},{2,6},{4,0},{6,2},{8,12},{10,14},{12,8},{14,10},{1,5},{3,7},... | collective-permute-start | bytes 196616 | tf_op jit(solution)/shard_map/ppermute | solution.py:66
  18.7 2.7 %collective-permute-start.7 = (bf16[2,32,512]{2,1,0:T(8,128)(2,1)S(1)}, bf16[2,32,512]{2,1,0:T(8,128)(2,1)S(1)}, u32[]{:S(2)}, u32[]{:S(2)}) collective-permute-start(bf16[2,32,512]{2,1,0:T(8,128)(2,1)S(1)} %shard_map.82), channel_id=1, source_target_pairs={{0,1},{1,0},{2,3},{3,2},{4,5},{5,4},{6,7},{7,6},{8,9},{9,8},{10,11... | collective-permute-start | bytes 196616 | tf_op jit(solution)/shard_map/ppermute | solution.py:66
  18.7 14.2 %collective-permute-start.5 = (bf16[2,64,512]{2,1,0:T(8,128)(2,1)S(1)}, bf16[2,64,512]{2,1,0:T(8,128)(2,1)S(1)}, u32[]{:S(2)}, u32[]{:S(2)}) collective-permute-start(bf16[2,64,512]{2,1,0:T(8,128)(2,1)S(1)} %shard_map.81.after.refs_0_), channel_id=1, source_target_pairs={{0,8},{2,10},{4,12},{6,14},{8,0},{10,2},{12,4},{14,6},{1,9},{3,11}... | collective-permute-start | bytes 393224 | tf_op jit(solution)/shard_map/ppermute | solution.py:66
  21.9 3.8 %collective-permute-start.10 = (bf16[2,32,512]{2,1,0:T(8,128)(2,1)S(1)}, bf16[2,32,512]{2,1,0:T(8,128)(2,1)S(1)}, u32[]{:S(2)}, u32[]{:S(2)}) collective-permute-start(bf16[2,32,512]{2,1,0:T(8,128)(2,1)S(1)} %shard_map.84.refs_2_), channel_id=1, source_target_pairs={{0,1},{1,0},{2,3},{3,2},{4,5},{5,4},{6,7},{7,6},{8,9},{9,8},{10,11... | collective-permute-start | bytes 196616 | tf_op jit(solution)/shard_map/ppermute | solution.py:66
  22.1 10.7 %collective-permute-start.9 = (bf16[2,32,512]{2,1,0:T(8,128)(2,1)S(1)}, bf16[2,32,512]{2,1,0:T(8,128)(2,1)S(1)}, u32[]{:S(2)}, u32[]{:S(2)}) collective-permute-start(bf16[2,32,512]{2,1,0:T(8,128)(2,1)S(1)} %shard_map.84.refs_2_), channel_id=1, source_target_pairs={{0,8},{2,10},{4,12},{6,14},{8,0},{10,2},{12,4},{14,6},{1,9},{3,11}... | collective-permute-start | bytes 196616 | tf_op jit(solution)/shard_map/ppermute | solution.py:66
  23.9 10.1 %collective-permute-start.8 = (bf16[2,32,512]{2,1,0:T(8,128)(2,1)S(1)}, bf16[2,32,512]{2,1,0:T(8,128)(2,1)S(1)}, u32[]{:S(2)}, u32[]{:S(2)}) collective-permute-start(bf16[2,32,512]{2,1,0:T(8,128)(2,1)S(1)} %shard_map.83.refs_1_), channel_id=1, source_target_pairs={{0,8},{2,10},{4,12},{6,14},{8,0},{10,2},{12,4},{14,6},{1,9},{3,11}... | collective-permute-start | bytes 196616 | tf_op jit(solution)/shard_map/ppermute | solution.py:66
  32.8 1.3 %collective-permute-start.11 = (bf16[2,32,512]{2,1,0:T(8,128)(2,1)S(1)}, bf16[2,32,512]{2,1,0:T(8,128)(2,1)S(1)}, u32[]{:S(2)}, u32[]{:S(2)}) collective-permute-start(bf16[2,32,512]{2,1,0:T(8,128)(2,1)S(1)} %shard_map.86), channel_id=1, source_target_pairs={{0,1},{1,0},{2,3},{3,2},{4,5},{5,4},{6,7},{7,6},{8,9},{9,8},{10,11... | collective-permute-start | bytes 196616 | tf_op jit(solution)/shard_map/ppermute | solution.py:66

commit v4 on v3

--- a/solution.py
+++ b/solution.py
@@ -18,7 +18,6 @@
 
 
 def run(kernel, outs, args, scratch=(), flops=0):
-    size = sum(o.size * o.dtype.itemsize for o in [*outs, *args])
     return pl.pallas_call(
         kernel,
         out_shape=outs,
@@ -26,7 +25,7 @@
         out_specs=[VMEM] * len(outs),
         scratch_shapes=scratch,
         compiler_params=pltpu.CompilerParams(vmem_limit_bytes=KERNEL_VMEM),
-        cost_estimate=pl.CostEstimate(flops=flops, bytes_accessed=size, transcendentals=0),
+        cost_estimate=pl.CostEstimate(flops=flops, bytes_accessed=flops // 300, transcendentals=0),
     )(*args)
 
 
@@ -246,7 +245,7 @@
             work(span) + [pltpu.VMEM(*shape) for shape in table_shapes],
         )
 
-    def merge(level, pieces, near, far, own_terms, ready=None, final=False):
+    def merge(level, pieces, near, far, own_terms, ready=None, final=False, flops=0):
         refs, stretches = zip(*pieces)
         shape = image.shape if final else (parts, far - near, angles)
         return run(
@@ -254,6 +253,7 @@
             [like(shape, bf16)],
             [*refs, halves, *own_terms] + ([ready] if ready is not None else []),
             work(far - near) + ([pltpu.VMEM((parts, span, angles), bf16)] if final else []),
+            flops=flops,
         )[0]
 
     def swap(value):
@@ -268,21 +268,21 @@
     other, other_edge = turned(received)
     other_edge = swap(other_edge)
     cut = 96
-    outer = merge(0, [(other, (0, span))], 0, cut, own_terms)
+    outer = merge(0, [(other, (0, span))], 0, cut, own_terms, flops=0)
     pieces = [(other, (0, span)), (other_edge, beyond)]
-    inner = merge(0, pieces, cut, span, own_terms)
+    inner = merge(0, pieces, cut, span, own_terms, flops=0)
 
     other_outer = from_partner(outer, "aper", 2)
     other_inner = from_partner(inner, "aper", 2)
-    own_edge = swap(inner_edge(inner, outer))
+    own_edge = swap(inner)
+    other_edge = from_partner(own_edge, "aper", 2)
     own_terms = own(1, [(outer, (0, cut)), (inner, (cut, span)), (own_edge, beyond)])
     middle = 64
     last = span - HALO
-    outer = merge(1, [(other_outer, (0, cut))], 0, middle, own_terms)
-    other_edge = swap(inner_edge(other_inner, outer))
+    outer = merge(1, [(other_outer, (0, cut))], 0, middle, own_terms, flops=0)
     pieces = [(other_outer, (0, cut)), (other_inner, (cut, span)), (other_edge, beyond)]
-    edge = merge(1, pieces, last, span, own_terms)
-    inner = merge(1, pieces, middle, last, own_terms)
+    edge = merge(1, pieces, last, span, own_terms, flops=0)
+    inner = merge(1, pieces, middle, last, own_terms, flops=0)
 
     other_outer = from_partner(outer, "aper", 4)
     other_edge = from_partner(edge, "aper", 4)

time: 36 us -> 35.4 us (0.983)
  waiting for transfers between devices: 11.9 us -> 10.5 us
  starting transfers between devices: 11.2 us -> 12 us
    ppermute x12, waiting for transfers between devices: 11.9 us -> 10.5 us  [from_partner(): return lax.ppermute(value, axis, pairs)]
    ppermute x12, starting transfers between devices: 11.2 us -> 12 us  [from_partner(): return lax.ppermute(value, axis, pairs)]
  transfers between devices with their start and end apart: 12 -> 12, of which waited for: 7 -> 6; matrix products, arithmetic and copies ran while one was open for 0% -> 0% of each run, Pallas kernels for 20% -> 21%
where the time goes in v4:
time: 35.4 us; the launch traced here: 35.2 us
  starting transfers between devices  12 us (34%)
  waiting for transfers between devices  10.5 us (30%)
  Pallas kernels  9.87 us (28%)
  local copies, waits for them, and re-layouts  2.64 us (7%)
    ppermute x12, starting transfers between devices, from_partner(): return lax.ppermute(value, axis, pairs)  12 us
    ppermute x12, waiting for transfers between devices, from_partner(): return lax.ppermute(value, axis, pairs)  10.5 us
    pallas_call x13, Pallas kernels, run(): pl.pallas_call(kernel, out_shape=outs, in_specs=[VMEM] * len(args), out_s...  9.86 us
    unnamed x14, local copies, waits for them, and re-layouts  2.64 us
  transfers between devices with their start and end apart: 12, of which 6 were waited for; matrix products, arithmetic and copies ran while one was open for 0% of the time, Pallas kernels for 21%

profile of v4, /device:TPU:0, one launch (start us, length us, event | category | flops | bytes accessed | tf_op | source)
XLA Modules:
  0.0 35.2 jit_solution(12286748795061851030)
XLA Ops:
  0.0 2.9 %collective-permute-start = (bf16[2,512,128]{2,1,0:T(8,128)(2,1)}, bf16[2,512,128]{2,1,0:T(8,128)(2,1)S(1)}, u32[]{:S(2)}, u32[]{:S(2)}) collective-permute-start(bf16[2,512,128]{2,1,0:T(8,128)(2,1)} %bitcast.3), channel_id=1, source_target_pairs={{0,2},{2,0},{4,6},{6,4},{8,10},{10,8},{12,14},{14,12},{1,3},{3,1},... | collective-permute-start | bytes 786440 | tf_op jit(solution)/shard_map/ppermute | solution.py:65
  2.9 0.0 copy-start.1
  2.9 1.0 %copy-done.1 = bf16[1,2,512,128]{3,2,1,0:T(8,128)(2,1)S(1)} copy-done((bf16[1,2,512,128]{3,2,1,0:T(8,128)(2,1)S(1)}, bf16[1,2,512,128]{3,2,1,0:T(8,128)(2,1)}, u32[]{:S(2)}) %copy-start.1) | copy-done | bytes 262168
  3.9 0.1 shard_map.75
  4.0 0.1 collective-permute-start.1
  4.1 0.0 copy-start
  4.1 1.2 %copy-done = bf16[1024,512]{1,0:T(8,128)(2,1)S(1)} copy-done((bf16[1024,512]{1,0:T(8,128)(2,1)S(1)}, bf16[1024,512]{1,0:T(8,128)(2,1)}, u32[]{:S(2)}) %copy-start) | copy-done | bytes 1048600
  5.4 0.0 copy-start.2
  5.4 0.0 copy-start.6
  5.4 0.3 shard_map.74.refs_2_.refs_1_.refs_3_.refs_4_
  5.7 0.0 collective-permute-done.1.refs_1_
  5.7 0.4 %copy-done.2 = s32[3,2,1024]{2,1,0:T(2,128)S(1)} copy-done((s32[3,2,1024]{2,1,0:T(2,128)S(1)}, s32[3,2,1024]{2,1,0:T(2,128)}, u32[]{:S(2)}) %copy-start.2) | copy-done | bytes 24600
  6.1 0.0 copy-done.3
  6.1 0.0 copy-done.4
  6.1 0.0 copy-done.5
  6.1 0.0 copy-done.6
  6.1 1.4 %shard_map.76 = (f32[2,4,128,128]{3,2,1,0:T(8,128)S(1)}, s32[4,8,128]{2,1,0:T(8,128)S(1)}, f32[4,9,8,128]{3,2,1,0:T(8,128)S(1)}, f32[2,4,128,128]{3,2,1,0:T(8,128)S(1)}) custom-call(bf16[2,128,512]{2,1,0:T(8,128)(2,1)S(1)} %get-tuple-element.22.refs_0_, bf16[2,32,512]{2,1,0:T(8,128)(2,1)S(1)} %collective-permute-done.1.refs_1_, ...), custom_call_target="tpu_custom_call" | custom-call | tf_op jit(solution)/shard_map/pallas_call | solution.py:21
  7.5 1.9 %collective-permute-done.image = bf16[2,512,128]{2,1,0:T(8,128)(2,1)S(1)} collective-permute-done((bf16[2,512,128]{2,1,0:T(8,128)(2,1)}, bf16[2,512,128]{2,1,0:T(8,128)(2,1)S(1)}, u32[]{:S(2)}, u32[]{:S(2)}) %collective-permute-start) | collective-permute-done | bytes 262176 | tf_op jit(solution)/shard_map/ppermute | solution.py:65
  9.5 0.1 shard_map.73
  9.6 0.8 %shard_map.77.refs_0_ = bf16[2,96,512]{2,1,0:T(8,128)(2,1)S(1)} custom-call(bf16[2,128,512]{2,1,0:T(8,128)(2,1)S(1)} %get-tuple-element.21.refs_0_, bf16[2,512,512]{2,1,0:T(8,128)(2,1)S(1)} %shard_map.74.refs_2_.refs_1_.refs_3_.refs_4_, f32[2,4,128,128]{3,2,1,0:T(8,128)S(1)} %get-tuple-element.24.refs_2_.refs_3_, ...), custom_call_target="tpu_custom_call" | custom-call | tf_op jit(solution)/shard_map/pallas_call | solution.py:21
  10.4 1.9 %collective-permute-start.2 = (bf16[2,96,512]{2,1,0:T(8,128)(2,1)S(1)}, bf16[2,96,512]{2,1,0:T(8,128)(2,1)S(1)}, u32[]{:S(2)}, u32[]{:S(2)}) collective-permute-start(bf16[2,96,512]{2,1,0:T(8,128)(2,1)S(1)} %shard_map.77.refs_0_), channel_id=1, source_target_pairs={{0,4},{2,6},{4,0},{6,2},{8,12},{10,14},{12,8},{14,10},{1,5},{3,7},... | collective-permute-start | bytes 589832 | tf_op jit(solution)/shard_map/ppermute | solution.py:65
  12.3 0.0 collective-permute-start.3
  12.3 1.3 %collective-permute-done.3.refs_1_ = bf16[2,32,512]{2,1,0:T(8,128)(2,1)S(1)} collective-permute-done((bf16[2,32,512]{2,1,0:T(8,128)(2,1)S(1)}, bf16[2,32,512]{2,1,0:T(8,128)(2,1)S(1)}, u32[]{:S(2)}, u32[]{:S(2)}) %collective-permute-start.3) | collective-permute-done | bytes 65568 | tf_op jit(solution)/shard_map/ppermute | solution.py:65
  13.5 0.5 %shard_map.78.refs_1_ = bf16[2,32,512]{2,1,0:T(8,128)(2,1)S(1)} custom-call(bf16[2,128,512]{2,1,0:T(8,128)(2,1)S(1)} %get-tuple-element.21.refs_0_, bf16[2,32,512]{2,1,0:T(8,128)(2,1)S(1)} %collective-permute-done.3.refs_1_, bf16[2,512,512]{2,1,0:T(8,128)(2,1)S(1)} %shard_map.74.refs_2_.refs_1_.refs_3_.refs_4_, ...), custom_call_target="tpu_custom_call" | custom-call | tf_op jit(solution)/shard_map/pallas_call | solution.py:21
  14.1 0.2 collective-permute-start.4
  14.3 0.2 collective-permute-start.6
  14.5 0.9 %collective-permute-done.4.refs_2_ = bf16[2,32,512]{2,1,0:T(8,128)(2,1)S(1)} collective-permute-done((bf16[2,32,512]{2,1,0:T(8,128)(2,1)S(1)}, bf16[2,32,512]{2,1,0:T(8,128)(2,1)S(1)}, u32[]{:S(2)}, u32[]{:S(2)}) %collective-permute-start.4) | collective-permute-done | bytes 65568 | tf_op jit(solution)/shard_map/ppermute | solution.py:65
  15.4 0.9 %collective-permute-start.7 = (bf16[2,32,512]{2,1,0:T(8,128)(2,1)S(1)}, bf16[2,32,512]{2,1,0:T(8,128)(2,1)S(1)}, u32[]{:S(2)}, u32[]{:S(2)}) collective-permute-start(bf16[2,32,512]{2,1,0:T(8,128)(2,1)S(1)} %collective-permute-done.4.refs_2_), channel_id=1, source_target_pairs={{0,4},{2,6},{4,0},{6,2},{8,12},{10,14},{12,8},{14,10},{1,5},{3,7},... | collective-permute-start | bytes 196616 | tf_op jit(solution)/shard_map/ppermute | solution.py:65
  16.3 1.4 %shard_map.79 = (f32[2,4,128,128]{3,2,1,0:T(8,128)S(1)}, s32[4,8,128]{2,1,0:T(8,128)S(1)}, f32[4,9,8,128]{3,2,1,0:T(8,128)S(1)}, f32[2,4,128,128]{3,2,1,0:T(8,128)S(1)}) custom-call(bf16[2,96,512]{2,1,0:T(8,128)(2,1)S(1)} %shard_map.77.refs_0_, bf16[2,32,512]{2,1,0:T(8,128)(2,1)S(1)} %shard_map.78.refs_1_, ...), custom_call_target="tpu_custom_call" | custom-call | tf_op jit(solution)/shard_map/pallas_call | solution.py:21
  17.7 0.0 collective-permute-done.2.refs_0_
  17.7 0.6 %shard_map.80.refs_0_ = bf16[2,64,512]{2,1,0:T(8,128)(2,1)S(1)} custom-call(bf16[2,96,512]{2,1,0:T(8,128)(2,1)S(1)} %collective-permute-done.2.refs_0_, bf16[2,512,512]{2,1,0:T(8,128)(2,1)S(1)} %shard_map.74.refs_2_.refs_1_.refs_3_.refs_4_, f32[2,4,128,128]{3,2,1,0:T(8,128)S(1)} %get-tuple-element.29.refs_2_.refs_4_, ...), custom_call_target="tpu_custom_call" | custom-call | tf_op jit(solution)/shard_map/pallas_call | solution.py:21
  18.4 2.7 %collective-permute-start.5 = (bf16[2,64,512]{2,1,0:T(8,128)(2,1)S(1)}, bf16[2,64,512]{2,1,0:T(8,128)(2,1)S(1)}, u32[]{:S(2)}, u32[]{:S(2)}) collective-permute-start(bf16[2,64,512]{2,1,0:T(8,128)(2,1)S(1)} %shard_map.80.refs_0_), channel_id=1, source_target_pairs={{0,8},{2,10},{4,12},{6,14},{8,0},{10,2},{12,4},{14,6},{1,9},{3,11}... | collective-permute-start | bytes 393224 | tf_op jit(solution)/shard_map/ppermute | solution.py:65
  21.0 0.0 collective-permute-done.6.refs_1_
  21.0 0.0 collective-permute-done.7.refs_2_
  21.0 0.5 %shard_map.82.refs_2_ = bf16[2,32,512]{2,1,0:T(8,128)(2,1)S(1)} custom-call(bf16[2,96,512]{2,1,0:T(8,128)(2,1)S(1)} %collective-permute-done.2.refs_0_, bf16[2,32,512]{2,1,0:T(8,128)(2,1)S(1)} %collective-permute-done.6.refs_1_, bf16[2,32,512]{2,1,0:T(8,128)(2,1)S(1)} %collective-permute-done.7.refs_2_, ...), custom_call_target="tpu_custom_call" | custom-call | tf_op jit(solution)/shard_map/pallas_call | solution.py:21
  21.6 0.1 collective-permute-start.10
  21.7 1.7 %collective-permute-start.9 = (bf16[2,32,512]{2,1,0:T(8,128)(2,1)S(1)}, bf16[2,32,512]{2,1,0:T(8,128)(2,1)S(1)}, u32[]{:S(2)}, u32[]{:S(2)}) collective-permute-start(bf16[2,32,512]{2,1,0:T(8,128)(2,1)S(1)} %shard_map.82.refs_2_), channel_id=1, source_target_pairs={{0,8},{2,10},{4,12},{6,14},{8,0},{10,2},{12,4},{14,6},{1,9},{3,11}... | collective-permute-start | bytes 196616 | tf_op jit(solution)/shard_map/ppermute | solution.py:65
  23.4 0.5 %shard_map.81.refs_1_ = bf16[2,32,512]{2,1,0:T(8,128)(2,1)S(1)} custom-call(bf16[2,96,512]{2,1,0:T(8,128)(2,1)S(1)} %collective-permute-done.2.refs_0_, bf16[2,32,512]{2,1,0:T(8,128)(2,1)S(1)} %collective-permute-done.6.refs_1_, bf16[2,32,512]{2,1,0:T(8,128)(2,1)S(1)} %collective-permute-done.7.refs_2_, ...), custom_call_target="tpu_custom_call" | custom-call | tf_op jit(solution)/shard_map/pallas_call | solution.py:21
  23.9 1.4 %collective-permute-start.8 = (bf16[2,32,512]{2,1,0:T(8,128)(2,1)S(1)}, bf16[2,32,512]{2,1,0:T(8,128)(2,1)S(1)}, u32[]{:S(2)}, u32[]{:S(2)}) collective-permute-start(bf16[2,32,512]{2,1,0:T(8,128)(2,1)S(1)} %shard_map.81.refs_1_), channel_id=1, source_target_pairs={{0,8},{2,10},{4,12},{6,14},{8,0},{10,2},{12,4},{14,6},{1,9},{3,11}... | collective-permute-start | bytes 196616 | tf_op jit(solution)/shard_map/ppermute | solution.py:65
  25.3 0.0 collective-permute-done.10.refs_3_
  25.3 1.4 %shard_map.83 = (f32[2,4,128,128]{3,2,1,0:T(8,128)S(1)}, s32[4,8,128]{2,1,0:T(8,128)S(1)}, f32[4,9,8,128]{3,2,1,0:T(8,128)S(1)}, f32[2,4,128,128]{3,2,1,0:T(8,128)S(1)}) custom-call(bf16[2,64,512]{2,1,0:T(8,128)(2,1)S(1)} %shard_map.80.refs_0_, bf16[2,32,512]{2,1,0:T(8,128)(2,1)S(1)} %shard_map.81.refs_1_, bf16[2,32,512]{2,1,0:T(8,128)(2,1)S(1)} %shard_map.82.refs_2_, ...), custom_call_target="tpu_custom_call" | custom-call | tf_op jit(solution)/shard_map/pallas_call | solution.py:21
  26.6 5.6 %collective-permute-done.9.value.refs_2_ = bf16[2,32,512]{2,1,0:T(8,128)(2,1)S(1)} collective-permute-done((bf16[2,32,512]{2,1,0:T(8,128)(2,1)S(1)}, bf16[2,32,512]{2,1,0:T(8,128)(2,1)S(1)}, u32[]{:S(2)}, u32[]{:S(2)}) %collective-permute-start.9) | collective-permute-done | bytes 65568 | tf_op jit(solution)/shard_map/ppermute | solution.py:65
  32.3 0.0 collective-permute-start.11
  32.3 0.0 collective-permute-done.5.refs_0_
  32.3 0.4 %shard_map.85.refs_9_ = bf16[2,32,512]{2,1,0:T(8,128)(2,1)S(1)} custom-call(bf16[2,64,512]{2,1,0:T(8,128)(2,1)S(1)} %collective-permute-done.5.refs_0_, bf16[2,512,512]{2,1,0:T(8,128)(2,1)S(1)} %shard_map.74.refs_2_.refs_1_.refs_3_.refs_4_, f32[2,4,128,128]{3,2,1,0:T(8,128)S(1)} %get-tuple-element.33.token.refs_2_.refs_5_, ...), custom_call_target="tpu_custom_call" | custom-call | tf_op jit(solution)/shard_map/pallas_call | solution.py:21
  32.7 0.2 collective-permute-done.8.refs_1_
  33.0 0.6 %collective-permute-done.11.refs_3_ = bf16[2,32,512]{2,1,0:T(8,128)(2,1)S(1)} collective-permute-done((bf16[2,32,512]{2,1,0:T(8,128)(2,1)S(1)}, bf16[2,32,512]{2,1,0:T(8,128)(2,1)S(1)}, u32[]{:S(2)}, u32[]{:S(2)}) %collective-permute-start.11) | collective-permute-done | bytes 65568 | tf_op jit(solution)/shard_map/ppermute | solution.py:65
  33.5 1.7 %shard_map.86 = bf16[2,512,128]{2,1,0:T(8,128)(2,1)} custom-call(bf16[2,64,512]{2,1,0:T(8,128)(2,1)S(1)} %collective-permute-done.5.refs_0_, bf16[2,32,512]{2,1,0:T(8,128)(2,1)S(1)} %collective-permute-done.8.refs_1_, bf16[2,32,512]{2,1,0:T(8,128)(2,1)S(1)} %collective-permute-done.9.value.refs_2_, bf16[2,32,512]{2,1,0:T(8,128)(2,1)S(1)} %collective-permute-done.11.refs_3_, ...), custom_call_target="tpu_custom_call" | custom-call | tf_op jit(solution)/shard_map/pallas_call | solution.py:21
  (4 shorter events, 0.0 us)
Async XLA Ops:
  0.0 9.5 %collective-permute-start = (bf16[2,512,128]{2,1,0:T(8,128)(2,1)}, bf16[2,512,128]{2,1,0:T(8,128)(2,1)S(1)}, u32[]{:S(2)}, u32[]{:S(2)}) collective-permute-start(bf16[2,512,128]{2,1,0:T(8,128)(2,1)} %bitcast.3), channel_id=1, source_target_pairs={{0,2},{2,0},{4,6},{6,4},{8,10},{10,8},{12,14},{14,12},{1,3},{3,1},... | collective-permute-start | bytes 786440 | tf_op jit(solution)/shard_map/ppermute | solution.py:65
  2.9 1.0 %copy-start.1 = (bf16[1,2,512,128]{3,2,1,0:T(8,128)(2,1)S(1)}, bf16[1,2,512,128]{3,2,1,0:T(8,128)(2,1)}, u32[]{:S(2)}) copy-start(bf16[1,2,512,128]{3,2,1,0:T(8,128)(2,1)} %param.7) | copy-start | bytes 786436
  4.0 1.7 %collective-permute-start.1 = (bf16[2,32,512]{2,1,0:T(8,128)(2,1)S(1)}, bf16[2,32,512]{2,1,0:T(8,128)(2,1)S(1)}, u32[]{:S(2)}, u32[]{:S(2)}) collective-permute-start(bf16[2,32,512]{2,1,0:T(8,128)(2,1)S(1)} %get-tuple-element.23), channel_id=1, source_target_pairs={{0,1},{1,0},{2,3},{3,2},{4,5},{5,4},{6,7},{7,6},{8,9},{9,8},{10,11... | collective-permute-start | bytes 196616 | tf_op jit(solution)/shard_map/ppermute | solution.py:65
  4.1 1.2 %copy-start = (bf16[1024,512]{1,0:T(8,128)(2,1)S(1)}, bf16[1024,512]{1,0:T(8,128)(2,1)}, u32[]{:S(2)}) copy-start(bf16[1024,512]{1,0:T(8,128)(2,1)} %matrix.1) | copy-start | bytes 3145732
  5.4 0.7 %copy-start.2 = (s32[3,2,1024]{2,1,0:T(2,128)S(1)}, s32[3,2,1024]{2,1,0:T(2,128)}, u32[]{:S(2)}) copy-start(s32[3,2,1024]{2,1,0:T(2,128)} %refs_5_.5) | copy-start | bytes 73732
  5.4 0.8 %copy-start.3 = (s32[3,2,1024]{2,1,0:T(2,128)S(1)}, s32[3,2,1024]{2,1,0:T(2,128)}, u32[]{:S(2)}) copy-start(s32[3,2,1024]{2,1,0:T(2,128)} %refs_6_.5) | copy-start | bytes 73732
  5.4 0.8 %copy-start.4 = (f32[3,2,1024]{2,1,0:T(2,128)S(1)}, f32[3,2,1024]{2,1,0:T(2,128)}, u32[]{:S(2)}) copy-start(f32[3,2,1024]{2,1,0:T(2,128)} %refs_7_.3) | copy-start | bytes 73732
  5.4 0.8 %copy-start.5 = (f32[3,2,1024]{2,1,0:T(2,128)S(1)}, f32[3,2,1024]{2,1,0:T(2,128)}, u32[]{:S(2)}) copy-start(f32[3,2,1024]{2,1,0:T(2,128)} %refs_8_.1) | copy-start | bytes 73732
  5.4 0.8 %copy-start.6 = (f32[16,8]{0,1:T(8,128)S(1)}, f32[16,8]{0,1:T(8,128)}, u32[]{:S(2)}) copy-start(f32[16,8]{0,1:T(8,128)} %param.11) | copy-start | bytes 1540
  10.4 7.3 %collective-permute-start.2 = (bf16[2,96,512]{2,1,0:T(8,128)(2,1)S(1)}, bf16[2,96,512]{2,1,0:T(8,128)(2,1)S(1)}, u32[]{:S(2)}, u32[]{:S(2)}) collective-permute-start(bf16[2,96,512]{2,1,0:T(8,128)(2,1)S(1)} %shard_map.77.refs_0_), channel_id=1, source_target_pairs={{0,4},{2,6},{4,0},{6,2},{8,12},{10,14},{12,8},{14,10},{1,5},{3,7},... | collective-permute-start | bytes 589832 | tf_op jit(solution)/shard_map/ppermute | solution.py:65
  12.3 1.3 %collective-permute-start.3 = (bf16[2,32,512]{2,1,0:T(8,128)(2,1)S(1)}, bf16[2,32,512]{2,1,0:T(8,128)(2,1)S(1)}, u32[]{:S(2)}, u32[]{:S(2)}) collective-permute-start(bf16[2,32,512]{2,1,0:T(8,128)(2,1)S(1)} %get-tuple-element.28), channel_id=1, source_target_pairs={{0,1},{1,0},{2,3},{3,2},{4,5},{5,4},{6,7},{7,6},{8,9},{9,8},{10,11... | collective-permute-start | bytes 196616 | tf_op jit(solution)/shard_map/ppermute | solution.py:65
  14.1 1.3 %collective-permute-start.4 = (bf16[2,32,512]{2,1,0:T(8,128)(2,1)S(1)}, bf16[2,32,512]{2,1,0:T(8,128)(2,1)S(1)}, u32[]{:S(2)}, u32[]{:S(2)}) collective-permute-start(bf16[2,32,512]{2,1,0:T(8,128)(2,1)S(1)} %shard_map.78.refs_1_), channel_id=1, source_target_pairs={{0,1},{1,0},{2,3},{3,2},{4,5},{5,4},{6,7},{7,6},{8,9},{9,8},{10,11... | collective-permute-start | bytes 196616 | tf_op jit(solution)/shard_map/ppermute | solution.py:65
  14.3 6.7 %collective-permute-start.6 = (bf16[2,32,512]{2,1,0:T(8,128)(2,1)S(1)}, bf16[2,32,512]{2,1,0:T(8,128)(2,1)S(1)}, u32[]{:S(2)}, u32[]{:S(2)}) collective-permute-start(bf16[2,32,512]{2,1,0:T(8,128)(2,1)S(1)} %shard_map.78.refs_1_), channel_id=1, source_target_pairs={{0,4},{2,6},{4,0},{6,2},{8,12},{10,14},{12,8},{14,10},{1,5},{3,7},... | collective-permute-start | bytes 196616 | tf_op jit(solution)/shard_map/ppermute | solution.py:65
  15.4 5.6 %collective-permute-start.7 = (bf16[2,32,512]{2,1,0:T(8,128)(2,1)S(1)}, bf16[2,32,512]{2,1,0:T(8,128)(2,1)S(1)}, u32[]{:S(2)}, u32[]{:S(2)}) collective-permute-start(bf16[2,32,512]{2,1,0:T(8,128)(2,1)S(1)} %collective-permute-done.4.refs_2_), channel_id=1, source_target_pairs={{0,4},{2,6},{4,0},{6,2},{8,12},{10,14},{12,8},{14,10},{1,5},{3,7},... | collective-permute-start | bytes 196616 | tf_op jit(solution)/shard_map/ppermute | solution.py:65
  18.4 13.9 %collective-permute-start.5 = (bf16[2,64,512]{2,1,0:T(8,128)(2,1)S(1)}, bf16[2,64,512]{2,1,0:T(8,128)(2,1)S(1)}, u32[]{:S(2)}, u32[]{:S(2)}) collective-permute-start(bf16[2,64,512]{2,1,0:T(8,128)(2,1)S(1)} %shard_map.80.refs_0_), channel_id=1, source_target_pairs={{0,8},{2,10},{4,12},{6,14},{8,0},{10,2},{12,4},{14,6},{1,9},{3,11}... | collective-permute-start | bytes 393224 | tf_op jit(solution)/shard_map/ppermute | solution.py:65
  21.6 3.7 %collective-permute-start.10 = (bf16[2,32,512]{2,1,0:T(8,128)(2,1)S(1)}, bf16[2,32,512]{2,1,0:T(8,128)(2,1)S(1)}, u32[]{:S(2)}, u32[]{:S(2)}) collective-permute-start(bf16[2,32,512]{2,1,0:T(8,128)(2,1)S(1)} %shard_map.82.refs_2_), channel_id=1, source_target_pairs={{0,1},{1,0},{2,3},{3,2},{4,5},{5,4},{6,7},{7,6},{8,9},{9,8},{10,11... | collective-permute-start | bytes 196616 | tf_op jit(solution)/shard_map/ppermute | solution.py:65
  21.7 10.6 %collective-permute-start.9 = (bf16[2,32,512]{2,1,0:T(8,128)(2,1)S(1)}, bf16[2,32,512]{2,1,0:T(8,128)(2,1)S(1)}, u32[]{:S(2)}, u32[]{:S(2)}) collective-permute-start(bf16[2,32,512]{2,1,0:T(8,128)(2,1)S(1)} %shard_map.82.refs_2_), channel_id=1, source_target_pairs={{0,8},{2,10},{4,12},{6,14},{8,0},{10,2},{12,4},{14,6},{1,9},{3,11}... | collective-permute-start | bytes 196616 | tf_op jit(solution)/shard_map/ppermute | solution.py:65
  23.9 9.1 %collective-permute-start.8 = (bf16[2,32,512]{2,1,0:T(8,128)(2,1)S(1)}, bf16[2,32,512]{2,1,0:T(8,128)(2,1)S(1)}, u32[]{:S(2)}, u32[]{:S(2)}) collective-permute-start(bf16[2,32,512]{2,1,0:T(8,128)(2,1)S(1)} %shard_map.81.refs_1_), channel_id=1, source_target_pairs={{0,8},{2,10},{4,12},{6,14},{8,0},{10,2},{12,4},{14,6},{1,9},{3,11}... | collective-permute-start | bytes 196616 | tf_op jit(solution)/shard_map/ppermute | solution.py:65
  32.3 1.3 %collective-permute-start.11 = (bf16[2,32,512]{2,1,0:T(8,128)(2,1)S(1)}, bf16[2,32,512]{2,1,0:T(8,128)(2,1)S(1)}, u32[]{:S(2)}, u32[]{:S(2)}) collective-permute-start(bf16[2,32,512]{2,1,0:T(8,128)(2,1)S(1)} %shard_map.84), channel_id=1, source_target_pairs={{0,1},{1,0},{2,3},{3,2},{4,5},{5,4},{6,7},{7,6},{8,9},{9,8},{10,11... | collective-permute-start | bytes 196616 | tf_op jit(solution)/shard_map/ppermute | solution.py:65

commit v5 on v2

v5 whole, which is shorter than its diff:
```python
import functools

import jax
import jax.numpy as jnp
from jax import lax
from jax.experimental import pallas as pl
from jax.experimental.pallas import tpu as pltpu
from jax.sharding import PartitionSpec as P

HALO = 32
LANES = 128
ROWS = 8
STEP = 16
KERNEL_VMEM = 8 << 20
AFTER = {"m0i": "own1a", "own1b": "m1o", "copy2": "own2"}
WORK = {"m1i": 3000000000}
VMEM = pl.BlockSpec(memory_space=pltpu.VMEM)
like = jax.ShapeDtypeStruct
f32, bf16 = jnp.float32, jnp.bfloat16


def run(name, kernel, outs, args, scratch=(), token=None, flops=0):
    tokens = [] if token is None else [token]

    def without_token(*refs):
        kernel(*refs[: len(args)], *refs[len(args) + len(tokens) :])

    return pl.pallas_call(
        without_token,
        out_shape=outs,
        in_specs=[VMEM] * len(args) + [pl.BlockSpec(memory_space=pl.ANY)] * len(tokens),
        out_specs=[VMEM] * len(outs),
        scratch_shapes=scratch,
        name=name,
        compiler_params=pltpu.CompilerParams(vmem_limit_bytes=KERNEL_VMEM),
        cost_estimate=pl.CostEstimate(flops=flops, bytes_accessed=0, transcendentals=0),
    )(*args, *tokens)


def from_partner(value, axis, mask):
    pairs = [(source, source ^ mask) for source in range(lax.axis_size(axis))]
    return lax.ppermute(value, axis, pairs)


def first_bin(span, near, far):
    return pl.multiple_of(jnp.where(lax.axis_index("range") == 0, near, span - far), STEP)


def own_half(level):
    return lax.axis_index("aper") >> level & 1


def turn(image, turned, edge):
    span = turned.shape[1]
    for part in range(image.shape[0]):
        turned[part] = image[part].T
    edge[...] = turned[:, pl.ds(first_bin(span, span - HALO, span), HALO), :]


def halves_kernel(matrix, halves):
    angles = matrix.shape[1]
    for half in range(halves.shape[0]):
        halves[half] = matrix[half * angles : (half + 1) * angles, :].T


def edge_kernel(value, edge):
    width = value.shape[1]
    edge[...] = value[:, pl.ds(first_bin(width, width - HALO, width), HALO), :]


def copy_kernel(source, target):
    target[...] = source[...]


def tables_kernel(span, first_level, off, idx, base, slope, table, shift_ref, taps_ref, phase_ref):
    angles = off.shape[2] // 2
    start = lax.axis_index("range") * span
    taps_count = table.shape[0]
    columns = [jnp.broadcast_to(table[:, k : k + 1], (taps_count, LANES)) for k in range(table.shape[1])]

    def tile(at, carry):
        here, j = at // (angles // LANES), lax.rem(at, angles // LANES)
        level = here + first_level
        half = lax.axis_index("aper") >> level & 1
        lane = pl.ds(pl.multiple_of(half * angles + j * LANES, LANES), LANES)
        for order in range(2):
            role = half if order == 0 else 1 - half

            def row(ref):
                both = ref[level, :, lane]
                return jnp.broadcast_to(jnp.where(role == 0, both[0:1], both[1:2]), (ROWS, LANES))

            shift = row(off) + (HALO - 3)
            shift_ref[here, order, j] = shift
            which = row(idx)
            taps = jnp.zeros((taps_count, LANES), f32)
            for k, column in enumerate(columns):
                taps = jnp.where(which == k, column, taps)
            odd = shift & 1
            zero = jnp.zeros((ROWS, LANES), f32)
            rows = [jnp.broadcast_to(taps[t : t + 1], (ROWS, LANES)) for t in range(taps_count)]
            for t in range(taps_count + 1):
                even_tap = rows[t] if t < taps_count else zero
                odd_tap = rows[t - 1] if t > 0 else zero
                taps_ref[here, order, j, t] = jnp.where(odd == 1, odd_tap, even_tap)
            s = row(slope)
            ramp = lax.broadcasted_iota(jnp.int32, (ROWS, LANES), 0)
            near = row(base) + s * (ramp + start).astype(f32)
            c0, s0 = jnp.cos(near), jnp.sin(near)
            steps = span // ROWS
            far_at = lax.broadcasted_iota(jnp.int32, (steps, LANES), 0) * ROWS
            far = jnp.broadcast_to(s[0:1], (steps, LANES)) * far_at.astype(f32)
            c1, s1 = jnp.cos(far), jnp.sin(far)
            for u in range(steps):
                cu, su = c1[u : u + 1], s1[u : u + 1]
                bins = pl.ds(u * ROWS, ROWS)
                phase_ref[here, order, 0, j, bins, :] = c0 * cu - s0 * su
                phase_ref[here, order, 1, j, bins, :] = s0 * cu + c0 * su
        return carry

    lax.fori_loop(0, shift_ref.shape[0] * (angles // LANES), tile, 0)


def interpolate(level, span, pieces, halves, slab):
    rows = jnp.concatenate([ref[part] for ref, _, _ in pieces for part in range(ref.shape[0])], 0)
    inter = jnp.dot(rows, halves[own_half(level)], preferred_element_type=f32).astype(bf16).astype(f32)
    at = 0
    for ref, near, far in pieces:
        place = pl.ds(pl.multiple_of(first_bin(span, near, far) + HALO, STEP), far - near)
        for part in range(ref.shape[0]):
            for j in range(inter.shape[1] // LANES):
                slab[part, j, place, :] = inter[at : at + far - near, j * LANES : (j + 1) * LANES]
            at += far - near
    place = pl.ds(pl.multiple_of(first_bin(span, -HALO, 0) + HALO, HALO), HALO)
    slab[:, :, place, :] = jnp.zeros((slab.shape[0], slab.shape[1], HALO, LANES), f32)


def pick(shift, bit, a, b):
    count = a.shape[0]
    mask = jnp.broadcast_to((shift >> bit & 1 == 1)[None], (count // ROWS, ROWS, LANES))
    return jnp.where(mask.reshape(count, LANES), a, b)


def shift_filter(slab, part, j, start, shift, taps, tmp, count):
    v = slab[part, j, pl.ds(start, count + 64), :]
    v = jnp.concatenate([pick(shift, 5, v[32 : count + 64], v[: count + 32]), v[count + 32 : count + 40]], 0)
    v = pick(shift, 4, v[16 : count + 40], v[: count + 24])
    v = pick(shift, 3, v[8 : count + 24], v[: count + 16])
    tmp[0, 0 : count + 16] = v
    v = pick(shift, 2, tmp[0, 4 : count + 20], v)
    tmp[1, 0 : count + 16] = v
    v = pick(shift, 1, tmp[1, 2 : count + 18], v)
    tmp[2, 0 : count + 16] = v
    total = None
    for t in range(taps.shape[0]):
        tap = jnp.broadcast_to(taps[t][None], (count // ROWS, ROWS, LANES)).reshape(count, LANES)
        term = tap * (v[:count] if t == 0 else tmp[2, t : t + count])
        total = term if total is None else total + term
    return total


def terms(slab, j, start, count, at, order, tables, tmp):
    shift_ref, taps_ref, phase_ref = tables
    shift, taps = shift_ref[at, order, j], taps_ref[at, order, j]
    re = shift_filter(slab, 0, j, start, shift, taps, tmp.at[0], count)
    im = shift_filter(slab, 1, j, start, shift, taps, tmp.at[1], count)
    c = phase_ref[at, order, 0, j, pl.ds(start, count), :]
    s = phase_ref[at, order, 1, j, pl.ds(start, count), :]
    return re * c - im * s, re * s + im * c


def own_kernel(level, at, span, stretches, near, far, *refs):
    pieces = [(ref, *stretch) for ref, stretch in zip(refs, stretches)]
    halves, *tables, acc, slab, tmp = refs[len(stretches) :]
    interpolate(level, span, pieces, halves, slab)
    start = first_bin(span, near, far)

    def tile(j, carry):
        acc[0, j], acc[1, j] = terms(slab, j, start, far - near, at, 0, tables, tmp)
        return carry

    lax.fori_loop(0, acc.shape[1], tile, 0)


def merge_kernel(level, at, span, stretches, near, far, held, final, *refs):
    pieces = [(ref, *stretch) for ref, stretch in zip(refs, stretches)]
    halves, acc, *tables = refs[len(stretches) : len(stretches) + 5]
    refs = refs[len(stretches) + 5 :]
    start, count = first_bin(span, near, far), far - near
    if final:
        ready, out, slab, tmp, merged = refs
        merged[:, pl.ds(first_bin(span, 0, near), near), :] = ready[...]
        into = start
    else:
        merged, slab, tmp = refs
        into = 0
    interpolate(level, span, pieces, halves, slab)
    acc_rows = pl.ds(pl.multiple_of(start - first_bin(span, *held), STEP), count)

    def tile(j, carry):
        lane = pl.ds(pl.multiple_of(j * LANES, LANES), LANES)
        for part, term in enumerate(terms(slab, j, start, count, at, 1, tables, tmp)):
            merged[part, pl.ds(into, count), lane] = (acc[part, j, acc_rows, :] + term).astype(bf16)
        return carry

    lax.fori_loop(0, acc.shape[1], tile, 0)
    if final:
        for part in range(out.shape[0]):
            out[part] = merged[part].T


def body(images, interp_matrix, offsets, tap_index, tap_table, phase_base, phase_slope):
    parts, angles, span = images.shape[1:]
    levels, roles, parent = offsets.shape
    tiles = angles // LANES
    taps_count = tap_table.shape[1]
    beyond = (span, span + HALO)
    edge_out = like((parts, HALO, angles), bf16)
    turned_outs = [like((parts, span, angles), bf16), edge_out]

    def work(count):
        return [pltpu.VMEM((parts, tiles, span + 2 * HALO, LANES), f32), pltpu.VMEM((parts, 3, count + 24, LANES), f32)]

    done = {}

    def step(name, *args):
        outs = run(name, *args, token=done.get(AFTER.get(name)), flops=WORK.get(name, 0))
        done[name] = outs[0]
        return outs

    def make_tables(name, first_level, count):
        outs = [
            like((count, roles, tiles, ROWS, LANES), jnp.int32),
            like((count, roles, tiles, taps_count + 1, ROWS, LANES), f32),
            like((count, roles, 2, tiles, span, LANES), f32),
        ]
        params = [offsets, tap_index, phase_base, phase_slope, tap_table.T]
        return step(name, functools.partial(tables_kernel, span, first_level), outs, params)

    def own(name, level, pieces, near=0, far=span):
        refs, stretches = zip(*pieces)
        at, tables = (0, first_tables) if level == 0 else (level - 1, later_tables)
        kernel = functools.partial(own_kernel, level, at, span, stretches, near, far)
        return step(name, kernel, [like((parts, tiles, far - near, LANES), f32)], [*refs, halves, *tables], work(far - near))[0]

    def merge(name, level, pieces, near, far, acc, held=(0, span), ready=None):
        refs, stretches = zip(*pieces)
        at, tables = (0, first_tables) if level == 0 else (level - 1, later_tables)
        final = ready is not None
        return step(
            name,
            functools.partial(merge_kernel, level, at, span, stretches, near, far, held, final),
            [like(images.shape[1:] if final else (parts, far - near, angles), bf16)],
            [*refs, halves, acc, *tables] + ([ready] if final else []),
            work(far - near) + ([pltpu.VMEM((parts, span, angles), bf16)] if final else []),
        )[0]

    def swap(value):
        return from_partner(value, "range", 1)

    received = from_partner(images[0], "aper", 1)
    current, edge = step("turn0", turn, turned_outs, [images[0]])
    own_edge = swap(edge)
    (halves,) = step("halves", halves_kernel, [like((2, angles, angles), bf16)], [interp_matrix])
    first_tables = make_tables("tables0", 0, 1)
    acc = own("own0", 0, [(current, (0, span)), (own_edge, beyond)])
    other, other_edge = step("turn1", turn, turned_outs, [received])
    other_edge = swap(other_edge)
    cut, middle, last = 96, 64, span - HALO
    outer = merge("m0o", 0, [(other, (0, span))], 0, cut, acc)

    other_outer = from_partner(outer, "aper", 2)
    later_tables = make_tables("tables12", 1, levels - 1)
    outer_acc = own("own1a", 1, [(outer, (0, cut))], 0, middle)
    inner = merge("m0i", 0, [(other, (0, span)), (other_edge, beyond)], cut, span, acc)
    other_inner = from_partner(inner, "aper", 2)
    own_edge = swap(step("edge1", edge_kernel, [edge_out], [inner])[0])
    other_edge = from_partner(own_edge, "aper", 2)
    new_outer = merge("m1o", 1, [(other_outer, (0, cut))], 0, middle, outer_acc, (0, middle))
    acc = own("own1b", 1, [(outer, (0, cut)), (inner, (cut, span)), (own_edge, beyond)], middle, span)
    pieces = [(other_outer, (0, cut)), (other_inner, (cut, span)), (other_edge, beyond)]
    edge = merge("m1e", 1, pieces, last, span, acc, (middle, span))
    inner = merge("m1i", 1, pieces, middle, last, acc, (middle, span))
    outer = new_outer

    other_outer = from_partner(outer, "aper", 4)
    other_edge = from_partner(edge, "aper", 4)
    other_inner = from_partner(inner, "aper", 4)
    acc = own("own2", 2, [(outer, (0, middle)), (inner, (middle, last)), (edge, (last, span)), (swap(edge), beyond)])
    pieces = [(other_outer, (0, middle)), (other_inner, (middle, last)), (other_edge, (last, span))]
    pieces += [(swap(step("copy2", copy_kernel, [edge_out], [other_edge])[0]), beyond)]
    first = middle - HALO
    ready = merge("f1", 2, [(other_outer, (0, middle))], 0, first, acc)
    return merge("f2", 2, pieces, first, span, acc, ready=ready)[None]


def solution(mesh):
    return jax.shard_map(
        body,
        mesh=mesh,
        in_specs=(P(("scene", "aper"), None, None, "range"), P(), P(), P(), P(), P(), P()),
        out_specs=P(("scene", "aper"), None, None, "range"),
        check_vma=False,
    )
```

time: 38.9 us -> 34.7 us (0.89)
  waiting for transfers between devices: 17.8 us -> 8.51 us
  starting transfers between devices: 8.89 us -> 12.6 us
  Pallas kernels: 9.19 us -> 11 us
  local copies, waits for them, and re-layouts: 2.65 us -> 2.22 us
    ppermute x11 -> x12, waiting for transfers between devices: 17.8 us -> 8.51 us  [from_partner(): return lax.ppermute(value, axis, pairs)]
    ppermute x11 -> x12, starting transfers between devices: 8.89 us -> 12.6 us  [from_partner(): return lax.ppermute(value, axis, pairs)]
    pallas_call x11 -> x18, Pallas kernels: 9.19 us -> 11 us  [run(): pl.pallas_call(without_token, out_shape=outs, in_specs=[VMEM] * len(args)...]
    unnamed x14, local copies, waits for them, and re-layouts: 2.64 us -> 2.22 us
  transfers between devices with their start and end apart: 11 -> 12, of which waited for: 4 -> 5; matrix products, arithmetic and copies ran while one was open for 0% -> 0% of each run, Pallas kernels for 17% -> 24%
where the time goes in v5:
time: 34.7 us; the launch traced here: 34.6 us
  starting transfers between devices  12.6 us (36%)
  Pallas kernels  11 us (32%)
  waiting for transfers between devices  8.51 us (25%)
  local copies, waits for them, and re-layouts  2.22 us (6%)
    ppermute x12, starting transfers between devices, from_partner(): return lax.ppermute(value, axis, pairs)  12.6 us
    pallas_call x18, Pallas kernels, run(): pl.pallas_call(without_token, out_shape=outs, in_specs=[VMEM] * len(args)...  11 us
    ppermute x12, waiting for transfers between devices, from_partner(): return lax.ppermute(value, axis, pairs)  8.51 us
    unnamed x14, local copies, waits for them, and re-layouts  2.22 us
  transfers between devices with their start and end apart: 12, of which 5 were waited for; matrix products, arithmetic and copies ran while one was open for 0% of the time, Pallas kernels for 24%

profile of v5, /device:TPU:0, one launch (start us, length us, event | category | flops | bytes accessed | tf_op | source)
XLA Modules:
  0.0 34.6 jit_solution(15881100242479702354)
XLA Ops:
  0.0 2.9 %collective-permute-start = (bf16[2,512,128]{2,1,0:T(8,128)(2,1)}, bf16[2,512,128]{2,1,0:T(8,128)(2,1)S(1)}, u32[]{:S(2)}, u32[]{:S(2)}) collective-permute-start(bf16[2,512,128]{2,1,0:T(8,128)(2,1)} %bitcast.3), channel_id=1, source_target_pairs={{0,2},{2,0},{4,6},{6,4},{8,10},{10,8},{12,14},{14,12},{1,3},{3,1},... | collective-permute-start | bytes 786440 | tf_op jit(solution)/shard_map/ppermute | solution.py:42
  2.9 1.0 %copy-done.1 = bf16[1,2,512,128]{3,2,1,0:T(8,128)(2,1)S(1)} copy-done((bf16[1,2,512,128]{3,2,1,0:T(8,128)(2,1)S(1)}, bf16[1,2,512,128]{3,2,1,0:T(8,128)(2,1)}, u32[]{:S(2)}) %copy-start.1) | copy-done | bytes 262168
  3.9 0.1 turn0.1
  4.1 0.1 collective-permute-start.1
  4.2 0.0 copy-start
  4.2 1.2 %copy-done = bf16[1024,512]{1,0:T(8,128)(2,1)S(1)} copy-done((bf16[1024,512]{1,0:T(8,128)(2,1)S(1)}, bf16[1024,512]{1,0:T(8,128)(2,1)}, u32[]{:S(2)}) %copy-start) | copy-done | bytes 1048600
  5.4 0.3 halves.1.refs_2_.refs_1_.refs_3_.refs_4_
  5.7 0.0 copy-done.2
  5.7 0.0 copy-done.3
  5.7 0.0 copy-done.4
  5.7 0.0 copy-done.5
  5.7 0.0 copy-done.6
  5.8 0.7 %tables0.1 = (s32[1,2,4,8,128]{4,3,2,1,0:T(8,128)S(1)}, f32[1,2,4,9,8,128]{5,4,3,2,1,0:T(8,128)S(1)}, f32[1,2,2,4,128,128]{5,4,3,2,1,0:T(8,128)S(1)}) custom-call(s32[3,2,1024]{2,1,0:T(2,128)S(1)} %copy-done.2, s32[3,2,1024]{2,1,0:T(2,128)S(1)} %copy-done.3, f32[3,2,1024]{2,1,0:T(2,128)S(1)} %copy-done.4, f32[3,2,1024]{2,1,0:T(2,128)S(1)} %copy-done.5, ...), custom_call_target="tpu_custom_call" | custom-call | tf_op jit(solution)/shard_map/tables0/pallas_call | solution.py:28
  6.5 0.0 collective-permute-done.1.refs_1_
  6.5 1.0 %own0.1.refs_2_.refs_3_ = f32[2,4,128,128]{3,2,1,0:T(8,128)S(1)} custom-call(bf16[2,128,512]{2,1,0:T(8,128)(2,1)S(1)} %get-tuple-element.16.refs_0_, bf16[2,32,512]{2,1,0:T(8,128)(2,1)S(1)} %collective-permute-done.1.refs_1_, bf16[2,512,512]{2,1,0:T(8,128)(2,1)S(1)} %halves.1.refs_2_.refs_1_.refs_3_.refs_4_, ...), custom_call_target="tpu_custom_call" | custom-call | tf_op jit(solution)/shard_map/own0/pallas_call | solution.py:28
  7.5 2.0 %collective-permute-done.refs_0_ = bf16[2,512,128]{2,1,0:T(8,128)(2,1)S(1)} collective-permute-done((bf16[2,512,128]{2,1,0:T(8,128)(2,1)}, bf16[2,512,128]{2,1,0:T(8,128)(2,1)S(1)}, u32[]{:S(2)}, u32[]{:S(2)}) %collective-permute-start) | collective-permute-done | bytes 262176 | tf_op jit(solution)/shard_map/ppermute | solution.py:42
  9.5 0.1 turn1.1
  9.6 0.8 %m0o.1.refs_0_ = bf16[2,96,512]{2,1,0:T(8,128)(2,1)S(1)} custom-call(bf16[2,128,512]{2,1,0:T(8,128)(2,1)S(1)} %get-tuple-element.15.refs_0_, bf16[2,512,512]{2,1,0:T(8,128)(2,1)S(1)} %halves.1.refs_2_.refs_1_.refs_3_.refs_4_, f32[2,4,128,128]{3,2,1,0:T(8,128)S(1)} %own0.1.refs_2_.refs_3_, s32[1,2,4,8,128]{4,3,2,1,0:T(8,128)S(1)} %get-tuple-element.18.refs_3_.refs_4_, ...), custom_call_target="tpu_custom_call" | custom-call | tf_op jit(solution)/shard_map/m0o/pallas_call | solution.py:28
  10.4 1.9 %collective-permute-start.2 = (bf16[2,96,512]{2,1,0:T(8,128)(2,1)S(1)}, bf16[2,96,512]{2,1,0:T(8,128)(2,1)S(1)}, u32[]{:S(2)}, u32[]{:S(2)}) collective-permute-start(bf16[2,96,512]{2,1,0:T(8,128)(2,1)S(1)} %m0o.1.refs_0_), channel_id=1, source_target_pairs={{0,4},{2,6},{4,0},{6,2},{8,12},{10,14},{12,8},{14,10},{1,5},{3,7},... | collective-permute-start | bytes 589832 | tf_op jit(solution)/shard_map/ppermute | solution.py:42
  12.3 0.0 collective-permute-start.4
  12.3 1.3 %tables12.1 = (s32[2,2,4,8,128]{4,3,2,1,0:T(8,128)S(1)}, f32[2,2,4,9,8,128]{5,4,3,2,1,0:T(8,128)S(1)}, f32[2,2,2,4,128,128]{5,4,3,2,1,0:T(8,128)S(1)}) custom-call(s32[3,2,1024]{2,1,0:T(2,128)S(1)} %copy-done.2, s32[3,2,1024]{2,1,0:T(2,128)S(1)} %copy-done.3, f32[3,2,1024]{2,1,0:T(2,128)S(1)} %copy-done.4, f32[3,2,1024]{2,1,0:T(2,128)S(1)} %copy-done.5, ...), custom_call_target="tpu_custom_call" | custom-call | tf_op jit(solution)/shard_map/tables12/pallas_call | solution.py:28
  13.7 0.6 %own1a.1.refs_2_.refs_7_ = f32[2,4,64,128]{3,2,1,0:T(8,128)S(1)} custom-call(bf16[2,96,512]{2,1,0:T(8,128)(2,1)S(1)} %m0o.1.refs_0_, bf16[2,512,512]{2,1,0:T(8,128)(2,1)S(1)} %halves.1.refs_2_.refs_1_.refs_3_.refs_4_, s32[2,2,4,8,128]{4,3,2,1,0:T(8,128)S(1)} %get-tuple-element.21.refs_2_.refs_3_.refs_4_.refs_5_.refs_6_, ...), custom_call_target="tpu_custom_call" | custom-call | tf_op jit(solution)/shard_map/own1a/pallas_call | solution.py:28
  14.3 0.0 collective-permute-done.4.refs_1_
  14.3 0.6 %m0i.1.refs_0_.refs_1_ = bf16[2,32,512]{2,1,0:T(8,128)(2,1)S(1)} custom-call(bf16[2,128,512]{2,1,0:T(8,128)(2,1)S(1)} %get-tuple-element.15.refs_0_, bf16[2,32,512]{2,1,0:T(8,128)(2,1)S(1)} %collective-permute-done.4.refs_1_, bf16[2,512,512]{2,1,0:T(8,128)(2,1)S(1)} %halves.1.refs_2_.refs_1_.refs_3_.refs_4_, f32[2,4,128,128]{3,2,1,0:T(8,128)S(1)} %own0.1.refs_2_.refs_3_, ...), custom_call_target="tpu_custom_call" | custom-call | tf_op jit(solution)/shard_map/m0i/pallas_call | solution.py:28
  14.8 0.6 %collective-permute-start.6 = (bf16[2,32,512]{2,1,0:T(8,128)(2,1)S(1)}, bf16[2,32,512]{2,1,0:T(8,128)(2,1)S(1)}, u32[]{:S(2)}, u32[]{:S(2)}) collective-permute-start(bf16[2,32,512]{2,1,0:T(8,128)(2,1)S(1)} %edge1.1), channel_id=1, source_target_pairs={{0,1},{1,0},{2,3},{3,2},{4,5},{5,4},{6,7},{7,6},{8,9},{9,8},{10,11... | collective-permute-start | bytes 196616 | tf_op jit(solution)/shard_map/ppermute | solution.py:42
  15.4 0.2 collective-permute-start.5
  15.6 0.7 %collective-permute-done.6.refs_2_ = bf16[2,32,512]{2,1,0:T(8,128)(2,1)S(1)} collective-permute-done((bf16[2,32,512]{2,1,0:T(8,128)(2,1)S(1)}, bf16[2,32,512]{2,1,0:T(8,128)(2,1)S(1)}, u32[]{:S(2)}, u32[]{:S(2)}) %collective-permute-start.6) | collective-permute-done | bytes 65568 | tf_op jit(solution)/shard_map/ppermute | solution.py:42
  16.3 1.1 %collective-permute-start.7 = (bf16[2,32,512]{2,1,0:T(8,128)(2,1)S(1)}, bf16[2,32,512]{2,1,0:T(8,128)(2,1)S(1)}, u32[]{:S(2)}, u32[]{:S(2)}) collective-permute-start(bf16[2,32,512]{2,1,0:T(8,128)(2,1)S(1)} %collective-permute-done.6.refs_2_), channel_id=1, source_target_pairs={{0,4},{2,6},{4,0},{6,2},{8,12},{10,14},{12,8},{14,10},{1,5},{3,7},... | collective-permute-start | bytes 196616 | tf_op jit(solution)/shard_map/ppermute | solution.py:42
  17.4 0.0 collective-permute-done.2.refs_0_
  17.4 0.6 %m1o.1.refs_7_.refs_0_ = bf16[2,64,512]{2,1,0:T(8,128)(2,1)S(1)} custom-call(bf16[2,96,512]{2,1,0:T(8,128)(2,1)S(1)} %collective-permute-done.2.refs_0_, bf16[2,512,512]{2,1,0:T(8,128)(2,1)S(1)} %halves.1.refs_2_.refs_1_.refs_3_.refs_4_, f32[2,4,64,128]{3,2,1,0:T(8,128)S(1)} %own1a.1.refs_2_.refs_7_, ...), custom_call_target="tpu_custom_call" | custom-call | tf_op jit(solution)/shard_map/m1o/pallas_call | solution.py:28
  18.0 2.7 %collective-permute-start.3 = (bf16[2,64,512]{2,1,0:T(8,128)(2,1)S(1)}, bf16[2,64,512]{2,1,0:T(8,128)(2,1)S(1)}, u32[]{:S(2)}, u32[]{:S(2)}) collective-permute-start(bf16[2,64,512]{2,1,0:T(8,128)(2,1)S(1)} %m1o.1.refs_7_.refs_0_), channel_id=1, source_target_pairs={{0,8},{2,10},{4,12},{6,14},{8,0},{10,2},{12,4},{14,6},{1,9},{3,11}... | collective-permute-start | bytes 393224 | tf_op jit(solution)/shard_map/ppermute | solution.py:42
  20.7 0.6 %own1b.1.refs_4_ = f32[2,4,64,128]{3,2,1,0:T(8,128)S(1)} custom-call(bf16[2,96,512]{2,1,0:T(8,128)(2,1)S(1)} %m0o.1.refs_0_, bf16[2,32,512]{2,1,0:T(8,128)(2,1)S(1)} %m0i.1.refs_0_.refs_1_, bf16[2,32,512]{2,1,0:T(8,128)(2,1)S(1)} %collective-permute-done.6.refs_2_, bf16[2,512,512]{2,1,0:T(8,128)(2,1)S(1)} %halves.1.refs_2_.refs_1_.refs_3_.refs_4_, ...), custom_call_target="tpu_custom_call" | custom-call | tf_op jit(solution)/shard_map/own1b/pallas_call | solution.py:28
  21.4 0.0 collective-permute-done.5.refs_1_
  21.4 0.0 collective-permute-done.7.refs_2_
  21.4 0.6 %m1e.1.refs_2_ = bf16[2,32,512]{2,1,0:T(8,128)(2,1)S(1)} custom-call(bf16[2,96,512]{2,1,0:T(8,128)(2,1)S(1)} %collective-permute-done.2.refs_0_, bf16[2,32,512]{2,1,0:T(8,128)(2,1)S(1)} %collective-permute-done.5.refs_1_, bf16[2,32,512]{2,1,0:T(8,128)(2,1)S(1)} %collective-permute-done.7.refs_2_, ...), custom_call_target="tpu_custom_call" | custom-call | tf_op jit(solution)/shard_map/m1e/pallas_call | solution.py:28
  21.9 0.1 collective-permute-start.10
  22.0 2.8 %collective-permute-start.9 = (bf16[2,32,512]{2,1,0:T(8,128)(2,1)S(1)}, bf16[2,32,512]{2,1,0:T(8,128)(2,1)S(1)}, u32[]{:S(2)}, u32[]{:S(2)}) collective-permute-start(bf16[2,32,512]{2,1,0:T(8,128)(2,1)S(1)} %m1e.1.refs_2_), channel_id=1, source_target_pairs={{0,8},{2,10},{4,12},{6,14},{8,0},{10,2},{12,4},{14,6},{1,9},{3,11}... | collective-permute-start | bytes 196616 | tf_op jit(solution)/shard_map/ppermute | solution.py:42
  24.8 0.5 %m1i.1.refs_1_ = bf16[2,32,512]{2,1,0:T(8,128)(2,1)S(1)} custom-call(bf16[2,96,512]{2,1,0:T(8,128)(2,1)S(1)} %collective-permute-done.2.refs_0_, bf16[2,32,512]{2,1,0:T(8,128)(2,1)S(1)} %collective-permute-done.5.refs_1_, bf16[2,32,512]{2,1,0:T(8,128)(2,1)S(1)} %collective-permute-done.7.refs_2_, ...), custom_call_target="tpu_custom_call" | custom-call | flops 3000000000 | tf_op jit(solution)/shard_map/m1i/pallas_call | solution.py:28
  25.3 0.3 collective-permute-start.8
  25.6 0.0 collective-permute-done.10.refs_3_
  25.6 1.0 %own2.1.refs_1_.refs_2_.refs_5_ = f32[2,4,128,128]{3,2,1,0:T(8,128)S(1)} custom-call(bf16[2,64,512]{2,1,0:T(8,128)(2,1)S(1)} %m1o.1.refs_7_.refs_0_, bf16[2,32,512]{2,1,0:T(8,128)(2,1)S(1)} %m1i.1.refs_1_, bf16[2,32,512]{2,1,0:T(8,128)(2,1)S(1)} %m1e.1.refs_2_, bf16[2,32,512]{2,1,0:T(8,128)(2,1)S(1)} %collective-permute-done.10.refs_3_, ...), custom_call_target="tpu_custom_call" | custom-call | tf_op jit(solution)/shard_map/own2/pallas_call | solution.py:28
  26.6 5.0 %collective-permute-done.9.refs_0_.refs_2_ = bf16[2,32,512]{2,1,0:T(8,128)(2,1)S(1)} collective-permute-done((bf16[2,32,512]{2,1,0:T(8,128)(2,1)S(1)}, bf16[2,32,512]{2,1,0:T(8,128)(2,1)S(1)}, u32[]{:S(2)}, u32[]{:S(2)}) %collective-permute-start.9) | collective-permute-done | bytes 65568 | tf_op jit(solution)/shard_map/ppermute | solution.py:42
  31.7 0.0 collective-permute-start.11
  31.7 0.0 collective-permute-done.3.refs_0_
  31.7 0.5 %f1.1.refs_9_ = bf16[2,32,512]{2,1,0:T(8,128)(2,1)S(1)} custom-call(bf16[2,64,512]{2,1,0:T(8,128)(2,1)S(1)} %collective-permute-done.3.refs_0_, bf16[2,512,512]{2,1,0:T(8,128)(2,1)S(1)} %halves.1.refs_2_.refs_1_.refs_3_.refs_4_, f32[2,4,128,128]{3,2,1,0:T(8,128)S(1)} %own2.1.refs_1_.refs_2_.refs_5_, ...), custom_call_target="tpu_custom_call" | custom-call | tf_op jit(solution)/shard_map/f1/pallas_call | solution.py:28
  32.1 0.3 collective-permute-done.8.refs_1_
  32.4 0.5 %collective-permute-done.11.refs_3_ = bf16[2,32,512]{2,1,0:T(8,128)(2,1)S(1)} collective-permute-done((bf16[2,32,512]{2,1,0:T(8,128)(2,1)S(1)}, bf16[2,32,512]{2,1,0:T(8,128)(2,1)S(1)}, u32[]{:S(2)}, u32[]{:S(2)}) %collective-permute-start.11) | collective-permute-done | bytes 65568 | tf_op jit(solution)/shard_map/ppermute | solution.py:42
  32.9 1.7 %f2.1 = bf16[2,512,128]{2,1,0:T(8,128)(2,1)} custom-call(bf16[2,64,512]{2,1,0:T(8,128)(2,1)S(1)} %collective-permute-done.3.refs_0_, bf16[2,32,512]{2,1,0:T(8,128)(2,1)S(1)} %collective-permute-done.8.refs_1_, bf16[2,32,512]{2,1,0:T(8,128)(2,1)S(1)} %collective-permute-done.9.refs_0_.refs_2_, bf16[2,32,512]{2,1,0:T(8,128)(2,1)S(1)} %collective-permute-done.11.refs_3_, ...), custom_call_target="tpu_custom_call" | custom-call | tf_op jit(solution)/shard_map/f2/pallas_call | solution.py:28
  (8 shorter events, 0.0 us)
Async XLA Ops:
  0.0 9.5 %collective-permute-start = (bf16[2,512,128]{2,1,0:T(8,128)(2,1)}, bf16[2,512,128]{2,1,0:T(8,128)(2,1)S(1)}, u32[]{:S(2)}, u32[]{:S(2)}) collective-permute-start(bf16[2,512,128]{2,1,0:T(8,128)(2,1)} %bitcast.3), channel_id=1, source_target_pairs={{0,2},{2,0},{4,6},{6,4},{8,10},{10,8},{12,14},{14,12},{1,3},{3,1},... | collective-permute-start | bytes 786440 | tf_op jit(solution)/shard_map/ppermute | solution.py:42
  2.9 1.0 %copy-start.1 = (bf16[1,2,512,128]{3,2,1,0:T(8,128)(2,1)S(1)}, bf16[1,2,512,128]{3,2,1,0:T(8,128)(2,1)}, u32[]{:S(2)}) copy-start(bf16[1,2,512,128]{3,2,1,0:T(8,128)(2,1)} %param.7) | copy-start | bytes 786436
  3.9 1.8 %copy-start.2 = (s32[3,2,1024]{2,1,0:T(2,128)S(1)}, s32[3,2,1024]{2,1,0:T(2,128)}, u32[]{:S(2)}) copy-start(s32[3,2,1024]{2,1,0:T(2,128)} %refs_0_.5) | copy-start | bytes 73732
  3.9 1.8 %copy-start.3 = (s32[3,2,1024]{2,1,0:T(2,128)S(1)}, s32[3,2,1024]{2,1,0:T(2,128)}, u32[]{:S(2)}) copy-start(s32[3,2,1024]{2,1,0:T(2,128)} %refs_1_.3) | copy-start | bytes 73732
  3.9 1.8 %copy-start.4 = (f32[3,2,1024]{2,1,0:T(2,128)S(1)}, f32[3,2,1024]{2,1,0:T(2,128)}, u32[]{:S(2)}) copy-start(f32[3,2,1024]{2,1,0:T(2,128)} %refs_2_.3) | copy-start | bytes 73732
  3.9 1.8 %copy-start.5 = (f32[3,2,1024]{2,1,0:T(2,128)S(1)}, f32[3,2,1024]{2,1,0:T(2,128)}, u32[]{:S(2)}) copy-start(f32[3,2,1024]{2,1,0:T(2,128)} %refs_3_.3) | copy-start | bytes 73732
  3.9 1.8 %copy-start.6 = (f32[16,8]{0,1:T(8,128)S(1)}, f32[16,8]{0,1:T(8,128)}, u32[]{:S(2)}) copy-start(f32[16,8]{0,1:T(8,128)} %param.11) | copy-start | bytes 1540
  4.1 2.4 %collective-permute-start.1 = (bf16[2,32,512]{2,1,0:T(8,128)(2,1)S(1)}, bf16[2,32,512]{2,1,0:T(8,128)(2,1)S(1)}, u32[]{:S(2)}, u32[]{:S(2)}) collective-permute-start(bf16[2,32,512]{2,1,0:T(8,128)(2,1)S(1)} %get-tuple-element.17), channel_id=1, source_target_pairs={{0,1},{1,0},{2,3},{3,2},{4,5},{5,4},{6,7},{7,6},{8,9},{9,8},{10,11... | collective-permute-start | bytes 196616 | tf_op jit(solution)/shard_map/ppermute | solution.py:42
  4.2 1.2 %copy-start = (bf16[1024,512]{1,0:T(8,128)(2,1)S(1)}, bf16[1024,512]{1,0:T(8,128)(2,1)}, u32[]{:S(2)}) copy-start(bf16[1024,512]{1,0:T(8,128)(2,1)} %refs_0_.3) | copy-start | bytes 3145732
  10.4 7.0 %collective-permute-start.2 = (bf16[2,96,512]{2,1,0:T(8,128)(2,1)S(1)}, bf16[2,96,512]{2,1,0:T(8,128)(2,1)S(1)}, u32[]{:S(2)}, u32[]{:S(2)}) collective-permute-start(bf16[2,96,512]{2,1,0:T(8,128)(2,1)S(1)} %m0o.1.refs_0_), channel_id=1, source_target_pairs={{0,4},{2,6},{4,0},{6,2},{8,12},{10,14},{12,8},{14,10},{1,5},{3,7},... | collective-permute-start | bytes 589832 | tf_op jit(solution)/shard_map/ppermute | solution.py:42
  12.3 2.0 %collective-permute-start.4 = (bf16[2,32,512]{2,1,0:T(8,128)(2,1)S(1)}, bf16[2,32,512]{2,1,0:T(8,128)(2,1)S(1)}, u32[]{:S(2)}, u32[]{:S(2)}) collective-permute-start(bf16[2,32,512]{2,1,0:T(8,128)(2,1)S(1)} %get-tuple-element.24), channel_id=1, source_target_pairs={{0,1},{1,0},{2,3},{3,2},{4,5},{5,4},{6,7},{7,6},{8,9},{9,8},{10,11... | collective-permute-start | bytes 196616 | tf_op jit(solution)/shard_map/ppermute | solution.py:42
  14.8 1.5 %collective-permute-start.6 = (bf16[2,32,512]{2,1,0:T(8,128)(2,1)S(1)}, bf16[2,32,512]{2,1,0:T(8,128)(2,1)S(1)}, u32[]{:S(2)}, u32[]{:S(2)}) collective-permute-start(bf16[2,32,512]{2,1,0:T(8,128)(2,1)S(1)} %edge1.1), channel_id=1, source_target_pairs={{0,1},{1,0},{2,3},{3,2},{4,5},{5,4},{6,7},{7,6},{8,9},{9,8},{10,11... | collective-permute-start | bytes 196616 | tf_op jit(solution)/shard_map/ppermute | solution.py:42
  15.4 6.0 %collective-permute-start.5 = (bf16[2,32,512]{2,1,0:T(8,128)(2,1)S(1)}, bf16[2,32,512]{2,1,0:T(8,128)(2,1)S(1)}, u32[]{:S(2)}, u32[]{:S(2)}) collective-permute-start(bf16[2,32,512]{2,1,0:T(8,128)(2,1)S(1)} %m0i.1.refs_0_.refs_1_), channel_id=1, source_target_pairs={{0,4},{2,6},{4,0},{6,2},{8,12},{10,14},{12,8},{14,10},{1,5},{3,7},... | collective-permute-start | bytes 196616 | tf_op jit(solution)/shard_map/ppermute | solution.py:42
  16.3 5.1 %collective-permute-start.7 = (bf16[2,32,512]{2,1,0:T(8,128)(2,1)S(1)}, bf16[2,32,512]{2,1,0:T(8,128)(2,1)S(1)}, u32[]{:S(2)}, u32[]{:S(2)}) collective-permute-start(bf16[2,32,512]{2,1,0:T(8,128)(2,1)S(1)} %collective-permute-done.6.refs_2_), channel_id=1, source_target_pairs={{0,4},{2,6},{4,0},{6,2},{8,12},{10,14},{12,8},{14,10},{1,5},{3,7},... | collective-permute-start | bytes 196616 | tf_op jit(solution)/shard_map/ppermute | solution.py:42
  18.0 13.6 %collective-permute-start.3 = (bf16[2,64,512]{2,1,0:T(8,128)(2,1)S(1)}, bf16[2,64,512]{2,1,0:T(8,128)(2,1)S(1)}, u32[]{:S(2)}, u32[]{:S(2)}) collective-permute-start(bf16[2,64,512]{2,1,0:T(8,128)(2,1)S(1)} %m1o.1.refs_7_.refs_0_), channel_id=1, source_target_pairs={{0,8},{2,10},{4,12},{6,14},{8,0},{10,2},{12,4},{14,6},{1,9},{3,11}... | collective-permute-start | bytes 393224 | tf_op jit(solution)/shard_map/ppermute | solution.py:42
  21.9 3.7 %collective-permute-start.10 = (bf16[2,32,512]{2,1,0:T(8,128)(2,1)S(1)}, bf16[2,32,512]{2,1,0:T(8,128)(2,1)S(1)}, u32[]{:S(2)}, u32[]{:S(2)}) collective-permute-start(bf16[2,32,512]{2,1,0:T(8,128)(2,1)S(1)} %m1e.1.refs_2_), channel_id=1, source_target_pairs={{0,1},{1,0},{2,3},{3,2},{4,5},{5,4},{6,7},{7,6},{8,9},{9,8},{10,11... | collective-permute-start | bytes 196616 | tf_op jit(solution)/shard_map/ppermute | solution.py:42
  22.0 9.6 %collective-permute-start.9 = (bf16[2,32,512]{2,1,0:T(8,128)(2,1)S(1)}, bf16[2,32,512]{2,1,0:T(8,128)(2,1)S(1)}, u32[]{:S(2)}, u32[]{:S(2)}) collective-permute-start(bf16[2,32,512]{2,1,0:T(8,128)(2,1)S(1)} %m1e.1.refs_2_), channel_id=1, source_target_pairs={{0,8},{2,10},{4,12},{6,14},{8,0},{10,2},{12,4},{14,6},{1,9},{3,11}... | collective-permute-start | bytes 196616 | tf_op jit(solution)/shard_map/ppermute | solution.py:42
  25.3 7.1 %collective-permute-start.8 = (bf16[2,32,512]{2,1,0:T(8,128)(2,1)S(1)}, bf16[2,32,512]{2,1,0:T(8,128)(2,1)S(1)}, u32[]{:S(2)}, u32[]{:S(2)}) collective-permute-start(bf16[2,32,512]{2,1,0:T(8,128)(2,1)S(1)} %m1i.1.refs_1_), channel_id=1, source_target_pairs={{0,8},{2,10},{4,12},{6,14},{8,0},{10,2},{12,4},{14,6},{1,9},{3,11}... | collective-permute-start | bytes 196616 | tf_op jit(solution)/shard_map/ppermute | solution.py:42
  31.7 1.3 %collective-permute-start.11 = (bf16[2,32,512]{2,1,0:T(8,128)(2,1)S(1)}, bf16[2,32,512]{2,1,0:T(8,128)(2,1)S(1)}, u32[]{:S(2)}, u32[]{:S(2)}) collective-permute-start(bf16[2,32,512]{2,1,0:T(8,128)(2,1)S(1)} %copy2.1), channel_id=1, source_target_pairs={{0,1},{1,0},{2,3},{3,2},{4,5},{5,4},{6,7},{7,6},{8,9},{9,8},{10,11... | collective-permute-start | bytes 196616 | tf_op jit(solution)/shard_map/ppermute | solution.py:42

commit v6 on v5

--- a/solution.py
+++ b/solution.py
@@ -12,8 +12,8 @@
 ROWS = 8
 STEP = 16
 KERNEL_VMEM = 8 << 20
-AFTER = {"m0i": "own1a", "own1b": "m1o", "copy2": "own2"}
-WORK = {"m1i": 3000000000}
+AFTER = {"m0i": "m0o", "own1b": "m1o", "copy2": "own2", "copy1": "m1o", "edge1": "m0i"}
+WORK = {"m1i": 3000000000, "m0o": 0, "m1o": 3000000000, "own1b": 3000000000}
 VMEM = pl.BlockSpec(memory_space=pltpu.VMEM)
 like = jax.ShapeDtypeStruct
 f32, bf16 = jnp.float32, jnp.bfloat16
@@ -275,9 +275,9 @@
     inner = merge("m0i", 0, [(other, (0, span)), (other_edge, beyond)], cut, span, acc)
     other_inner = from_partner(inner, "aper", 2)
     own_edge = swap(step("edge1", edge_kernel, [edge_out], [inner])[0])
-    other_edge = from_partner(own_edge, "aper", 2)
     new_outer = merge("m1o", 1, [(other_outer, (0, cut))], 0, middle, outer_acc, (0, middle))
     acc = own("own1b", 1, [(outer, (0, cut)), (inner, (cut, span)), (own_edge, beyond)], middle, span)
+    other_edge = swap(step("copy1", edge_kernel, [edge_out], [other_inner])[0])
     pieces = [(other_outer, (0, cut)), (other_inner, (cut, span)), (other_edge, beyond)]
     edge = merge("m1e", 1, pieces, last, span, acc, (middle, span))
     inner = merge("m1i", 1, pieces, middle, last, acc, (middle, span))

time: 34.7 us -> 33.2 us (0.957)
  starting transfers between devices: 12.6 us -> 11.4 us
  waiting for transfers between devices: 8.51 us -> 8.14 us
    ppermute x12, starting transfers between devices: 12.6 us -> 11.4 us  [from_partner(): return lax.ppermute(value, axis, pairs)]
    ppermute x12, waiting for transfers between devices: 8.51 us -> 8.14 us  [from_partner(): return lax.ppermute(value, axis, pairs)]
    pallas_call x18 -> x19, Pallas kernels: 11 us -> 11 us  [run(): pl.pallas_call(without_token, out_shape=outs, in_specs=[VMEM] * len(args)...]
  transfers between devices with their start and end apart: 12 -> 12, of which waited for: 5 -> 6; matrix products, arithmetic and copies ran while one was open for 0% -> 0% of each run, Pallas kernels for 24% -> 25%
where the time goes in v6:
time: 33.2 us; the launch traced here: 33.1 us
  starting transfers between devices  11.4 us (34%)
  Pallas kernels  11 us (33%)
  waiting for transfers between devices  8.14 us (25%)
  local copies, waits for them, and re-layouts  2.22 us (7%)
    ppermute x12, starting transfers between devices, from_partner(): return lax.ppermute(value, axis, pairs)  11.4 us
    pallas_call x19, Pallas kernels, run(): pl.pallas_call(without_token, out_shape=outs, in_specs=[VMEM] * len(args)...  11 us
    ppermute x12, waiting for transfers between devices, from_partner(): return lax.ppermute(value, axis, pairs)  8.14 us
    unnamed x14, local copies, waits for them, and re-layouts  2.22 us
  transfers between devices with their start and end apart: 12, of which 6 were waited for; matrix products, arithmetic and copies ran while one was open for 0% of the time, Pallas kernels for 25%

profile of v6, /device:TPU:0, one launch (start us, length us, event | category | flops | bytes accessed | tf_op | source)
XLA Modules:
  0.0 33.1 jit_solution(68727551215364319)
XLA Ops:
  0.0 2.9 %collective-permute-start = (bf16[2,512,128]{2,1,0:T(8,128)(2,1)}, bf16[2,512,128]{2,1,0:T(8,128)(2,1)S(1)}, u32[]{:S(2)}, u32[]{:S(2)}) collective-permute-start(bf16[2,512,128]{2,1,0:T(8,128)(2,1)} %bitcast.3), channel_id=1, source_target_pairs={{0,2},{2,0},{4,6},{6,4},{8,10},{10,8},{12,14},{14,12},{1,3},{3,1},... | collective-permute-start | bytes 786440 | tf_op jit(solution)/shard_map/ppermute | solution.py:42
  2.9 1.0 %copy-done.1 = bf16[1,2,512,128]{3,2,1,0:T(8,128)(2,1)S(1)} copy-done((bf16[1,2,512,128]{3,2,1,0:T(8,128)(2,1)S(1)}, bf16[1,2,512,128]{3,2,1,0:T(8,128)(2,1)}, u32[]{:S(2)}) %copy-start.1) | copy-done | bytes 262168
  3.9 0.0 copy-start.6
  3.9 0.1 turn0.1
  4.1 0.1 collective-permute-start.1
  4.2 0.0 copy-start
  4.2 1.2 %copy-done = bf16[1024,512]{1,0:T(8,128)(2,1)S(1)} copy-done((bf16[1024,512]{1,0:T(8,128)(2,1)S(1)}, bf16[1024,512]{1,0:T(8,128)(2,1)}, u32[]{:S(2)}) %copy-start) | copy-done | bytes 1048600
  5.4 0.3 halves.1.refs_2_.refs_1_.refs_3_.refs_4_
  5.7 0.0 copy-done.2
  5.7 0.0 copy-done.3
  5.7 0.0 copy-done.4
  5.7 0.0 copy-done.5
  5.8 0.7 %tables0.1 = (s32[1,2,4,8,128]{4,3,2,1,0:T(8,128)S(1)}, f32[1,2,4,9,8,128]{5,4,3,2,1,0:T(8,128)S(1)}, f32[1,2,2,4,128,128]{5,4,3,2,1,0:T(8,128)S(1)}) custom-call(s32[3,2,1024]{2,1,0:T(2,128)S(1)} %copy-done.2, s32[3,2,1024]{2,1,0:T(2,128)S(1)} %copy-done.3, f32[3,2,1024]{2,1,0:T(2,128)S(1)} %copy-done.4, f32[3,2,1024]{2,1,0:T(2,128)S(1)} %copy-done.5, ...), custom_call_target="tpu_custom_call" | custom-call | tf_op jit(solution)/shard_map/tables0/pallas_call | solution.py:28
  6.5 0.0 collective-permute-done.1.refs_1_
  6.5 1.0 %own0.1.refs_2_.refs_3_ = f32[2,4,128,128]{3,2,1,0:T(8,128)S(1)} custom-call(bf16[2,128,512]{2,1,0:T(8,128)(2,1)S(1)} %get-tuple-element.16.refs_0_, bf16[2,32,512]{2,1,0:T(8,128)(2,1)S(1)} %collective-permute-done.1.refs_1_, bf16[2,512,512]{2,1,0:T(8,128)(2,1)S(1)} %halves.1.refs_2_.refs_1_.refs_3_.refs_4_, ...), custom_call_target="tpu_custom_call" | custom-call | tf_op jit(solution)/shard_map/own0/pallas_call | solution.py:28
  7.5 2.0 %collective-permute-done.refs_0_ = bf16[2,512,128]{2,1,0:T(8,128)(2,1)S(1)} collective-permute-done((bf16[2,512,128]{2,1,0:T(8,128)(2,1)}, bf16[2,512,128]{2,1,0:T(8,128)(2,1)S(1)}, u32[]{:S(2)}, u32[]{:S(2)}) %collective-permute-start) | collective-permute-done | bytes 262176 | tf_op jit(solution)/shard_map/ppermute | solution.py:42
  9.5 0.1 turn1.1
  9.6 0.8 %m0o.1.refs_0_.refs_7_ = bf16[2,96,512]{2,1,0:T(8,128)(2,1)S(1)} custom-call(bf16[2,128,512]{2,1,0:T(8,128)(2,1)S(1)} %get-tuple-element.15.refs_0_, bf16[2,512,512]{2,1,0:T(8,128)(2,1)S(1)} %halves.1.refs_2_.refs_1_.refs_3_.refs_4_, f32[2,4,128,128]{3,2,1,0:T(8,128)S(1)} %own0.1.refs_2_.refs_3_, s32[1,2,4,8,128]{4,3,2,1,0:T(8,128)S(1)} %get-tuple-element.18.refs_3_.refs_4_, ...), custom_call_target="tpu_custom_call" | custom-call | tf_op jit(solution)/shard_map/m0o/pallas_call | solution.py:28
  10.4 1.9 %collective-permute-start.2 = (bf16[2,96,512]{2,1,0:T(8,128)(2,1)S(1)}, bf16[2,96,512]{2,1,0:T(8,128)(2,1)S(1)}, u32[]{:S(2)}, u32[]{:S(2)}) collective-permute-start(bf16[2,96,512]{2,1,0:T(8,128)(2,1)S(1)} %m0o.1.refs_0_.refs_7_), channel_id=1, source_target_pairs={{0,4},{2,6},{4,0},{6,2},{8,12},{10,14},{12,8},{14,10},{1,5},{3,7},... | collective-permute-start | bytes 589832 | tf_op jit(solution)/shard_map/ppermute | solution.py:42
  12.3 0.0 collective-permute-start.4
  12.3 1.3 %tables12.1 = (s32[2,2,4,8,128]{4,3,2,1,0:T(8,128)S(1)}, f32[2,2,4,9,8,128]{5,4,3,2,1,0:T(8,128)S(1)}, f32[2,2,2,4,128,128]{5,4,3,2,1,0:T(8,128)S(1)}) custom-call(s32[3,2,1024]{2,1,0:T(2,128)S(1)} %copy-done.2, s32[3,2,1024]{2,1,0:T(2,128)S(1)} %copy-done.3, f32[3,2,1024]{2,1,0:T(2,128)S(1)} %copy-done.4, f32[3,2,1024]{2,1,0:T(2,128)S(1)} %copy-done.5, ...), custom_call_target="tpu_custom_call" | custom-call | tf_op jit(solution)/shard_map/tables12/pallas_call | solution.py:28
  13.7 0.6 %own1a.1.refs_2_ = f32[2,4,64,128]{3,2,1,0:T(8,128)S(1)} custom-call(bf16[2,96,512]{2,1,0:T(8,128)(2,1)S(1)} %m0o.1.refs_0_.refs_7_, bf16[2,512,512]{2,1,0:T(8,128)(2,1)S(1)} %halves.1.refs_2_.refs_1_.refs_3_.refs_4_, s32[2,2,4,8,128]{4,3,2,1,0:T(8,128)S(1)} %get-tuple-element.21.refs_2_.refs_3_.refs_4_.refs_5_.refs_6_, ...), custom_call_target="tpu_custom_call" | custom-call | tf_op jit(solution)/shard_map/own1a/pallas_call | solution.py:28
  14.3 0.0 collective-permute-done.4.refs_1_
  14.3 0.6 %m0i.1.refs_0_.refs_1_ = bf16[2,32,512]{2,1,0:T(8,128)(2,1)S(1)} custom-call(bf16[2,128,512]{2,1,0:T(8,128)(2,1)S(1)} %get-tuple-element.15.refs_0_, bf16[2,32,512]{2,1,0:T(8,128)(2,1)S(1)} %collective-permute-done.4.refs_1_, bf16[2,512,512]{2,1,0:T(8,128)(2,1)S(1)} %halves.1.refs_2_.refs_1_.refs_3_.refs_4_, f32[2,4,128,128]{3,2,1,0:T(8,128)S(1)} %own0.1.refs_2_.refs_3_, ...), custom_call_target="tpu_custom_call" | custom-call | tf_op jit(solution)/shard_map/m0i/pallas_call | solution.py:28
  14.8 0.3 collective-permute-start.5
  15.1 0.4 %collective-permute-start.7 = (bf16[2,32,512]{2,1,0:T(8,128)(2,1)S(1)}, bf16[2,32,512]{2,1,0:T(8,128)(2,1)S(1)}, u32[]{:S(2)}, u32[]{:S(2)}) collective-permute-start(bf16[2,32,512]{2,1,0:T(8,128)(2,1)S(1)} %edge1.1), channel_id=1, source_target_pairs={{0,1},{1,0},{2,3},{3,2},{4,5},{5,4},{6,7},{7,6},{8,9},{9,8},{10,11... | collective-permute-start | bytes 196616 | tf_op jit(solution)/shard_map/ppermute | solution.py:42
  15.5 1.1 %collective-permute-done.2.refs_0_ = bf16[2,96,512]{2,1,0:T(8,128)(2,1)S(1)} collective-permute-done((bf16[2,96,512]{2,1,0:T(8,128)(2,1)S(1)}, bf16[2,96,512]{2,1,0:T(8,128)(2,1)S(1)}, u32[]{:S(2)}, u32[]{:S(2)}) %collective-permute-start.2) | collective-permute-done | bytes 196640 | tf_op jit(solution)/shard_map/ppermute | solution.py:42
  16.6 0.6 %m1o.1.refs_1_.refs_7_.refs_0_ = bf16[2,64,512]{2,1,0:T(8,128)(2,1)S(1)} custom-call(bf16[2,96,512]{2,1,0:T(8,128)(2,1)S(1)} %collective-permute-done.2.refs_0_, bf16[2,512,512]{2,1,0:T(8,128)(2,1)S(1)} %halves.1.refs_2_.refs_1_.refs_3_.refs_4_, f32[2,4,64,128]{3,2,1,0:T(8,128)S(1)} %own1a.1.refs_2_, ...), custom_call_target="tpu_custom_call" | custom-call | flops 3000000000 | tf_op jit(solution)/shard_map/m1o/pallas_call | solution.py:28
  17.2 2.6 %collective-permute-start.3 = (bf16[2,64,512]{2,1,0:T(8,128)(2,1)S(1)}, bf16[2,64,512]{2,1,0:T(8,128)(2,1)S(1)}, u32[]{:S(2)}, u32[]{:S(2)}) collective-permute-start(bf16[2,64,512]{2,1,0:T(8,128)(2,1)S(1)} %m1o.1.refs_1_.refs_7_.refs_0_), channel_id=1, source_target_pairs={{0,8},{2,10},{4,12},{6,14},{8,0},{10,2},{12,4},{14,6},{1,9},{3,11}... | collective-permute-start | bytes 393224 | tf_op jit(solution)/shard_map/ppermute | solution.py:42
  19.7 0.0 collective-permute-done.5.refs_0_.refs_1_
  19.8 0.1 collective-permute-start.6
  19.8 0.0 collective-permute-done.7.refs_2_
  19.8 0.7 %own1b.1.refs_4_ = f32[2,4,64,128]{3,2,1,0:T(8,128)S(1)} custom-call(bf16[2,96,512]{2,1,0:T(8,128)(2,1)S(1)} %m0o.1.refs_0_.refs_7_, bf16[2,32,512]{2,1,0:T(8,128)(2,1)S(1)} %m0i.1.refs_0_.refs_1_, bf16[2,32,512]{2,1,0:T(8,128)(2,1)S(1)} %collective-permute-done.7.refs_2_, bf16[2,512,512]{2,1,0:T(8,128)(2,1)S(1)} %halves.1.refs_2_.refs_1_.refs_3_.refs_4_, ...), custom_call_target="tpu_custom_call" | custom-call | flops 3000000000 | tf_op jit(solution)/shard_map/own1b/pallas_call | solution.py:28
  20.5 0.6 %collective-permute-done.6.refs_2_ = bf16[2,32,512]{2,1,0:T(8,128)(2,1)S(1)} collective-permute-done((bf16[2,32,512]{2,1,0:T(8,128)(2,1)S(1)}, bf16[2,32,512]{2,1,0:T(8,128)(2,1)S(1)}, u32[]{:S(2)}, u32[]{:S(2)}) %collective-permute-start.6) | collective-permute-done | bytes 65568 | tf_op jit(solution)/shard_map/ppermute | solution.py:42
  21.1 0.5 %m1e.1.refs_2_ = bf16[2,32,512]{2,1,0:T(8,128)(2,1)S(1)} custom-call(bf16[2,96,512]{2,1,0:T(8,128)(2,1)S(1)} %collective-permute-done.2.refs_0_, bf16[2,32,512]{2,1,0:T(8,128)(2,1)S(1)} %collective-permute-done.5.refs_0_.refs_1_, bf16[2,32,512]{2,1,0:T(8,128)(2,1)S(1)} %collective-permute-done.6.refs_2_, ...), custom_call_target="tpu_custom_call" | custom-call | tf_op jit(solution)/shard_map/m1e/pallas_call | solution.py:28
  21.6 0.2 collective-permute-start.10
  21.8 2.6 %collective-permute-start.9 = (bf16[2,32,512]{2,1,0:T(8,128)(2,1)S(1)}, bf16[2,32,512]{2,1,0:T(8,128)(2,1)S(1)}, u32[]{:S(2)}, u32[]{:S(2)}) collective-permute-start(bf16[2,32,512]{2,1,0:T(8,128)(2,1)S(1)} %m1e.1.refs_2_), channel_id=1, source_target_pairs={{0,8},{2,10},{4,12},{6,14},{8,0},{10,2},{12,4},{14,6},{1,9},{3,11}... | collective-permute-start | bytes 196616 | tf_op jit(solution)/shard_map/ppermute | solution.py:42
  24.4 0.5 %m1i.1.refs_1_ = bf16[2,32,512]{2,1,0:T(8,128)(2,1)S(1)} custom-call(bf16[2,96,512]{2,1,0:T(8,128)(2,1)S(1)} %collective-permute-done.2.refs_0_, bf16[2,32,512]{2,1,0:T(8,128)(2,1)S(1)} %collective-permute-done.5.refs_0_.refs_1_, bf16[2,32,512]{2,1,0:T(8,128)(2,1)S(1)} %collective-permute-done.6.refs_2_, ...), custom_call_target="tpu_custom_call" | custom-call | flops 3000000000 | tf_op jit(solution)/shard_map/m1i/pallas_call | solution.py:28
  25.0 0.4 %collective-permute-start.8 = (bf16[2,32,512]{2,1,0:T(8,128)(2,1)S(1)}, bf16[2,32,512]{2,1,0:T(8,128)(2,1)S(1)}, u32[]{:S(2)}, u32[]{:S(2)}) collective-permute-start(bf16[2,32,512]{2,1,0:T(8,128)(2,1)S(1)} %m1i.1.refs_1_), channel_id=1, source_target_pairs={{0,8},{2,10},{4,12},{6,14},{8,0},{10,2},{12,4},{14,6},{1,9},{3,11}... | collective-permute-start | bytes 196616 | tf_op jit(solution)/shard_map/ppermute | solution.py:42
  25.4 0.0 collective-permute-done.10.refs_3_
  25.4 1.0 %own2.1.refs_1_.refs_2_.refs_5_ = f32[2,4,128,128]{3,2,1,0:T(8,128)S(1)} custom-call(bf16[2,64,512]{2,1,0:T(8,128)(2,1)S(1)} %m1o.1.refs_1_.refs_7_.refs_0_, bf16[2,32,512]{2,1,0:T(8,128)(2,1)S(1)} %m1i.1.refs_1_, bf16[2,32,512]{2,1,0:T(8,128)(2,1)S(1)} %m1e.1.refs_2_, bf16[2,32,512]{2,1,0:T(8,128)(2,1)S(1)} %collective-permute-done.10.refs_3_, ...), custom_call_target="tpu_custom_call" | custom-call | tf_op jit(solution)/shard_map/own2/pallas_call | solution.py:28
  26.4 3.8 %collective-permute-done.9.refs_0_.refs_2_ = bf16[2,32,512]{2,1,0:T(8,128)(2,1)S(1)} collective-permute-done((bf16[2,32,512]{2,1,0:T(8,128)(2,1)S(1)}, bf16[2,32,512]{2,1,0:T(8,128)(2,1)S(1)}, u32[]{:S(2)}, u32[]{:S(2)}) %collective-permute-start.9) | collective-permute-done | bytes 65568 | tf_op jit(solution)/shard_map/ppermute | solution.py:42
  30.1 0.0 collective-permute-start.11
  30.1 0.0 collective-permute-done.3.refs_0_
  30.2 0.5 %f1.1.refs_9_ = bf16[2,32,512]{2,1,0:T(8,128)(2,1)S(1)} custom-call(bf16[2,64,512]{2,1,0:T(8,128)(2,1)S(1)} %collective-permute-done.3.refs_0_, bf16[2,512,512]{2,1,0:T(8,128)(2,1)S(1)} %halves.1.refs_2_.refs_1_.refs_3_.refs_4_, f32[2,4,128,128]{3,2,1,0:T(8,128)S(1)} %own2.1.refs_1_.refs_2_.refs_5_, ...), custom_call_target="tpu_custom_call" | custom-call | tf_op jit(solution)/shard_map/f1/pallas_call | solution.py:28
  30.6 0.7 %collective-permute-done.8.refs_1_ = bf16[2,32,512]{2,1,0:T(8,128)(2,1)S(1)} collective-permute-done((bf16[2,32,512]{2,1,0:T(8,128)(2,1)S(1)}, bf16[2,32,512]{2,1,0:T(8,128)(2,1)S(1)}, u32[]{:S(2)}, u32[]{:S(2)}) %collective-permute-start.8) | collective-permute-done | bytes 65568 | tf_op jit(solution)/shard_map/ppermute | solution.py:42
  31.3 0.1 collective-permute-done.11.refs_3_
  31.4 1.7 %f2.1 = bf16[2,512,128]{2,1,0:T(8,128)(2,1)} custom-call(bf16[2,64,512]{2,1,0:T(8,128)(2,1)S(1)} %collective-permute-done.3.refs_0_, bf16[2,32,512]{2,1,0:T(8,128)(2,1)S(1)} %collective-permute-done.8.refs_1_, bf16[2,32,512]{2,1,0:T(8,128)(2,1)S(1)} %collective-permute-done.9.refs_0_.refs_2_, bf16[2,32,512]{2,1,0:T(8,128)(2,1)S(1)} %collective-permute-done.11.refs_3_, ...), custom_call_target="tpu_custom_call" | custom-call | tf_op jit(solution)/shard_map/f2/pallas_call | solution.py:28
  (9 shorter events, 0.0 us)
Async XLA Ops:
  0.0 9.5 %collective-permute-start = (bf16[2,512,128]{2,1,0:T(8,128)(2,1)}, bf16[2,512,128]{2,1,0:T(8,128)(2,1)S(1)}, u32[]{:S(2)}, u32[]{:S(2)}) collective-permute-start(bf16[2,512,128]{2,1,0:T(8,128)(2,1)} %bitcast.3), channel_id=1, source_target_pairs={{0,2},{2,0},{4,6},{6,4},{8,10},{10,8},{12,14},{14,12},{1,3},{3,1},... | collective-permute-start | bytes 786440 | tf_op jit(solution)/shard_map/ppermute | solution.py:42
  2.9 1.0 %copy-start.1 = (bf16[1,2,512,128]{3,2,1,0:T(8,128)(2,1)S(1)}, bf16[1,2,512,128]{3,2,1,0:T(8,128)(2,1)}, u32[]{:S(2)}) copy-start(bf16[1,2,512,128]{3,2,1,0:T(8,128)(2,1)} %param.7) | copy-start | bytes 786436
  3.9 1.8 %copy-start.2 = (s32[3,2,1024]{2,1,0:T(2,128)S(1)}, s32[3,2,1024]{2,1,0:T(2,128)}, u32[]{:S(2)}) copy-start(s32[3,2,1024]{2,1,0:T(2,128)} %refs_0_.5) | copy-start | bytes 73732
  3.9 1.8 %copy-start.3 = (s32[3,2,1024]{2,1,0:T(2,128)S(1)}, s32[3,2,1024]{2,1,0:T(2,128)}, u32[]{:S(2)}) copy-start(s32[3,2,1024]{2,1,0:T(2,128)} %refs_1_.3) | copy-start | bytes 73732
  3.9 1.8 %copy-start.4 = (f32[3,2,1024]{2,1,0:T(2,128)S(1)}, f32[3,2,1024]{2,1,0:T(2,128)}, u32[]{:S(2)}) copy-start(f32[3,2,1024]{2,1,0:T(2,128)} %refs_2_.3) | copy-start | bytes 73732
  3.9 1.8 %copy-start.5 = (f32[3,2,1024]{2,1,0:T(2,128)S(1)}, f32[3,2,1024]{2,1,0:T(2,128)}, u32[]{:S(2)}) copy-start(f32[3,2,1024]{2,1,0:T(2,128)} %refs_3_.3) | copy-start | bytes 73732
  3.9 1.8 %copy-start.6 = (f32[16,8]{0,1:T(8,128)S(1)}, f32[16,8]{0,1:T(8,128)}, u32[]{:S(2)}) copy-start(f32[16,8]{0,1:T(8,128)} %param.11) | copy-start | bytes 1540
  4.1 2.4 %collective-permute-start.1 = (bf16[2,32,512]{2,1,0:T(8,128)(2,1)S(1)}, bf16[2,32,512]{2,1,0:T(8,128)(2,1)S(1)}, u32[]{:S(2)}, u32[]{:S(2)}) collective-permute-start(bf16[2,32,512]{2,1,0:T(8,128)(2,1)S(1)} %get-tuple-element.17), channel_id=1, source_target_pairs={{0,1},{1,0},{2,3},{3,2},{4,5},{5,4},{6,7},{7,6},{8,9},{9,8},{10,11... | collective-permute-start | bytes 196616 | tf_op jit(solution)/shard_map/ppermute | solution.py:42
  4.2 1.2 %copy-start = (bf16[1024,512]{1,0:T(8,128)(2,1)S(1)}, bf16[1024,512]{1,0:T(8,128)(2,1)}, u32[]{:S(2)}) copy-start(bf16[1024,512]{1,0:T(8,128)(2,1)} %refs_0_.3) | copy-start | bytes 3145732
  10.4 6.2 %collective-permute-start.2 = (bf16[2,96,512]{2,1,0:T(8,128)(2,1)S(1)}, bf16[2,96,512]{2,1,0:T(8,128)(2,1)S(1)}, u32[]{:S(2)}, u32[]{:S(2)}) collective-permute-start(bf16[2,96,512]{2,1,0:T(8,128)(2,1)S(1)} %m0o.1.refs_0_.refs_7_), channel_id=1, source_target_pairs={{0,4},{2,6},{4,0},{6,2},{8,12},{10,14},{12,8},{14,10},{1,5},{3,7},... | collective-permute-start | bytes 589832 | tf_op jit(solution)/shard_map/ppermute | solution.py:42
  12.3 2.0 %collective-permute-start.4 = (bf16[2,32,512]{2,1,0:T(8,128)(2,1)S(1)}, bf16[2,32,512]{2,1,0:T(8,128)(2,1)S(1)}, u32[]{:S(2)}, u32[]{:S(2)}) collective-permute-start(bf16[2,32,512]{2,1,0:T(8,128)(2,1)S(1)} %get-tuple-element.24), channel_id=1, source_target_pairs={{0,1},{1,0},{2,3},{3,2},{4,5},{5,4},{6,7},{7,6},{8,9},{9,8},{10,11... | collective-permute-start | bytes 196616 | tf_op jit(solution)/shard_map/ppermute | solution.py:42
  14.8 4.9 %collective-permute-start.5 = (bf16[2,32,512]{2,1,0:T(8,128)(2,1)S(1)}, bf16[2,32,512]{2,1,0:T(8,128)(2,1)S(1)}, u32[]{:S(2)}, u32[]{:S(2)}) collective-permute-start(bf16[2,32,512]{2,1,0:T(8,128)(2,1)S(1)} %m0i.1.refs_0_.refs_1_), channel_id=1, source_target_pairs={{0,4},{2,6},{4,0},{6,2},{8,12},{10,14},{12,8},{14,10},{1,5},{3,7},... | collective-permute-start | bytes 196616 | tf_op jit(solution)/shard_map/ppermute | solution.py:42
  15.1 4.7 %collective-permute-start.7 = (bf16[2,32,512]{2,1,0:T(8,128)(2,1)S(1)}, bf16[2,32,512]{2,1,0:T(8,128)(2,1)S(1)}, u32[]{:S(2)}, u32[]{:S(2)}) collective-permute-start(bf16[2,32,512]{2,1,0:T(8,128)(2,1)S(1)} %edge1.1), channel_id=1, source_target_pairs={{0,1},{1,0},{2,3},{3,2},{4,5},{5,4},{6,7},{7,6},{8,9},{9,8},{10,11... | collective-permute-start | bytes 196616 | tf_op jit(solution)/shard_map/ppermute | solution.py:42
  17.2 13.0 %collective-permute-start.3 = (bf16[2,64,512]{2,1,0:T(8,128)(2,1)S(1)}, bf16[2,64,512]{2,1,0:T(8,128)(2,1)S(1)}, u32[]{:S(2)}, u32[]{:S(2)}) collective-permute-start(bf16[2,64,512]{2,1,0:T(8,128)(2,1)S(1)} %m1o.1.refs_1_.refs_7_.refs_0_), channel_id=1, source_target_pairs={{0,8},{2,10},{4,12},{6,14},{8,0},{10,2},{12,4},{14,6},{1,9},{3,11}... | collective-permute-start | bytes 393224 | tf_op jit(solution)/shard_map/ppermute | solution.py:42
  19.8 1.3 %collective-permute-start.6 = (bf16[2,32,512]{2,1,0:T(8,128)(2,1)S(1)}, bf16[2,32,512]{2,1,0:T(8,128)(2,1)S(1)}, u32[]{:S(2)}, u32[]{:S(2)}) collective-permute-start(bf16[2,32,512]{2,1,0:T(8,128)(2,1)S(1)} %copy1.1), channel_id=1, source_target_pairs={{0,1},{1,0},{2,3},{3,2},{4,5},{5,4},{6,7},{7,6},{8,9},{9,8},{10,11... | collective-permute-start | bytes 196616 | tf_op jit(solution)/shard_map/ppermute | solution.py:42
  21.6 3.8 %collective-permute-start.10 = (bf16[2,32,512]{2,1,0:T(8,128)(2,1)S(1)}, bf16[2,32,512]{2,1,0:T(8,128)(2,1)S(1)}, u32[]{:S(2)}, u32[]{:S(2)}) collective-permute-start(bf16[2,32,512]{2,1,0:T(8,128)(2,1)S(1)} %m1e.1.refs_2_), channel_id=1, source_target_pairs={{0,1},{1,0},{2,3},{3,2},{4,5},{5,4},{6,7},{7,6},{8,9},{9,8},{10,11... | collective-permute-start | bytes 196616 | tf_op jit(solution)/shard_map/ppermute | solution.py:42
  21.8 8.3 %collective-permute-start.9 = (bf16[2,32,512]{2,1,0:T(8,128)(2,1)S(1)}, bf16[2,32,512]{2,1,0:T(8,128)(2,1)S(1)}, u32[]{:S(2)}, u32[]{:S(2)}) collective-permute-start(bf16[2,32,512]{2,1,0:T(8,128)(2,1)S(1)} %m1e.1.refs_2_), channel_id=1, source_target_pairs={{0,8},{2,10},{4,12},{6,14},{8,0},{10,2},{12,4},{14,6},{1,9},{3,11}... | collective-permute-start | bytes 196616 | tf_op jit(solution)/shard_map/ppermute | solution.py:42
  25.0 6.3 %collective-permute-start.8 = (bf16[2,32,512]{2,1,0:T(8,128)(2,1)S(1)}, bf16[2,32,512]{2,1,0:T(8,128)(2,1)S(1)}, u32[]{:S(2)}, u32[]{:S(2)}) collective-permute-start(bf16[2,32,512]{2,1,0:T(8,128)(2,1)S(1)} %m1i.1.refs_1_), channel_id=1, source_target_pairs={{0,8},{2,10},{4,12},{6,14},{8,0},{10,2},{12,4},{14,6},{1,9},{3,11}... | collective-permute-start | bytes 196616 | tf_op jit(solution)/shard_map/ppermute | solution.py:42
  30.1 1.3 %collective-permute-start.11 = (bf16[2,32,512]{2,1,0:T(8,128)(2,1)S(1)}, bf16[2,32,512]{2,1,0:T(8,128)(2,1)S(1)}, u32[]{:S(2)}, u32[]{:S(2)}) collective-permute-start(bf16[2,32,512]{2,1,0:T(8,128)(2,1)S(1)} %copy2.1), channel_id=1, source_target_pairs={{0,1},{1,0},{2,3},{3,2},{4,5},{5,4},{6,7},{7,6},{8,9},{9,8},{10,11... | collective-permute-start | bytes 196616 | tf_op jit(solution)/shard_map/ppermute | solution.py:42

commit v7 on v6

--- a/solution.py
+++ b/solution.py
@@ -12,14 +12,24 @@
 ROWS = 8
 STEP = 16
 KERNEL_VMEM = 8 << 20
-AFTER = {"m0i": "m0o", "own1b": "m1o", "copy2": "own2", "copy1": "m1o", "edge1": "m0i"}
-WORK = {"m1i": 3000000000, "m0o": 0, "m1o": 3000000000, "own1b": 3000000000}
+AFTER = {
+    "m0i": "m0o",
+    "own1b": "m1o",
+    "copy2": "own2",
+    "copy1": "m1o",
+    "edge1": "m0i",
+    "later": "m1e",
+    "own1a": "tables12",
+    "tables12": "own0",
+    "turn1": "tables12",
+}
+WORK = {"m1o": 3000000000, "own1b": 3000000000, "m1i": 3000000000}
 VMEM = pl.BlockSpec(memory_space=pltpu.VMEM)
 like = jax.ShapeDtypeStruct
 f32, bf16 = jnp.float32, jnp.bfloat16
 
 
-def run(name, kernel, outs, args, scratch=(), token=None, flops=0):
+def run(name, kernel, outs, args, scratch=(), aliases=None, token=None, flops=0):
     tokens = [] if token is None else [token]
 
     def without_token(*refs):
@@ -31,6 +41,7 @@
         in_specs=[VMEM] * len(args) + [pl.BlockSpec(memory_space=pl.ANY)] * len(tokens),
         out_specs=[VMEM] * len(outs),
         scratch_shapes=scratch,
+        input_output_aliases=aliases or {},
         name=name,
         compiler_params=pltpu.CompilerParams(vmem_limit_bytes=KERNEL_VMEM),
         cost_estimate=pl.CostEstimate(flops=flops, bytes_accessed=0, transcendentals=0),
@@ -44,6 +55,10 @@
 
 def first_bin(span, near, far):
     return pl.multiple_of(jnp.where(lax.axis_index("range") == 0, near, span - far), STEP)
+
+
+def trimmed(stretch, near, far):
+    return max(stretch[0], near - HALO), min(stretch[1], far + HALO)
 
 
 def own_half(level):
@@ -122,10 +137,14 @@
 
 
 def interpolate(level, span, pieces, halves, slab):
-    rows = jnp.concatenate([ref[part] for ref, _, _ in pieces for part in range(ref.shape[0])], 0)
+    rows = []
+    for ref, held, used in pieces:
+        skip = pl.multiple_of(first_bin(span, *used) - first_bin(span, *held), STEP)
+        rows += [ref[part, pl.ds(skip, used[1] - used[0]), :] for part in range(ref.shape[0])]
+    rows = jnp.concatenate(rows, 0)
     inter = jnp.dot(rows, halves[own_half(level)], preferred_element_type=f32).astype(bf16).astype(f32)
     at = 0
-    for ref, near, far in pieces:
+    for ref, _, (near, far) in pieces:
         place = pl.ds(pl.multiple_of(first_bin(span, near, far) + HALO, STEP), far - near)
         for part in range(ref.shape[0]):
             for j in range(inter.shape[1] // LANES):
@@ -170,7 +189,7 @@
 
 
 def own_kernel(level, at, span, stretches, near, far, *refs):
-    pieces = [(ref, *stretch) for ref, stretch in zip(refs, stretches)]
+    pieces = [(ref, held, trimmed(held, near, far)) for ref, held in zip(refs, stretches)]
     halves, *tables, acc, slab, tmp = refs[len(stretches) :]
     interpolate(level, span, pieces, halves, slab)
     start = first_bin(span, near, far)
@@ -182,13 +201,13 @@
     lax.fori_loop(0, acc.shape[1], tile, 0)
 
 
-def merge_kernel(level, at, span, stretches, near, far, held, final, *refs):
-    pieces = [(ref, *stretch) for ref, stretch in zip(refs, stretches)]
+def merge_kernel(level, at, span, stretches, near, far, held, mode, *refs):
+    pieces = [(ref, got, got if mode == "early" else trimmed(got, near, far)) for ref, got in zip(refs, stretches)]
     halves, acc, *tables = refs[len(stretches) : len(stretches) + 5]
     refs = refs[len(stretches) + 5 :]
     start, count = first_bin(span, near, far), far - near
-    if final:
-        ready, out, slab, tmp, merged = refs
+    if mode == "last":
+        ready, _, out, slab, tmp, merged = refs
         merged[:, pl.ds(first_bin(span, 0, near), near), :] = ready[...]
         into = start
     else:
@@ -204,7 +223,7 @@
         return carry
 
     lax.fori_loop(0, acc.shape[1], tile, 0)
-    if final:
+    if mode == "last":
         for part in range(out.shape[0]):
             out[part] = merged[part].T
 
@@ -243,17 +262,20 @@
         kernel = functools.partial(own_kernel, level, at, span, stretches, near, far)
         return step(name, kernel, [like((parts, tiles, far - near, LANES), f32)], [*refs, halves, *tables], work(far - near))[0]
 
-    def merge(name, level, pieces, near, far, acc, held=(0, span), ready=None):
+    def merge(name, level, pieces, near, far, acc, held=(0, span), mode="", ready=()):
         refs, stretches = zip(*pieces)
         at, tables = (0, first_tables) if level == 0 else (level - 1, later_tables)
-        final = ready is not None
-        return step(
-            name,
-            functools.partial(merge_kernel, level, at, span, stretches, near, far, held, final),
-            [like(images.shape[1:] if final else (parts, far - near, angles), bf16)],
-            [*refs, halves, acc, *tables] + ([ready] if final else []),
-            work(far - near) + ([pltpu.VMEM((parts, span, angles), bf16)] if final else []),
-        )[0]
+        args = [*refs, halves, acc, *tables, *ready]
+        outs = [like(images.shape[1:] if mode == "last" else (parts, far - near, angles), bf16)]
+        slab, tmp = work(far - near)
+        if mode:
+            outs.append(like((parts, tiles, span + 2 * HALO, LANES), f32))
+        scratch = ([] if mode else [slab]) + [tmp]
+        if mode == "last":
+            scratch.append(pltpu.VMEM((parts, span, angles), bf16))
+        kernel = functools.partial(merge_kernel, level, at, span, stretches, near, far, held, mode)
+        result = step(name, kernel, outs, args, scratch, {len(args) - 1: 1} if mode == "last" else None)
+        return result if mode == "early" else result[0]
 
     def swap(value):
         return from_partner(value, "range", 1)
@@ -279,19 +301,20 @@
     acc = own("own1b", 1, [(outer, (0, cut)), (inner, (cut, span)), (own_edge, beyond)], middle, span)
     other_edge = swap(step("copy1", edge_kernel, [edge_out], [other_inner])[0])
     pieces = [(other_outer, (0, cut)), (other_inner, (cut, span)), (other_edge, beyond)]
+    inner = merge("m1i", 1, pieces[:2], middle, last, acc, (middle, span))
     edge = merge("m1e", 1, pieces, last, span, acc, (middle, span))
-    inner = merge("m1i", 1, pieces, middle, last, acc, (middle, span))
+    (inner,) = step("later", copy_kernel, [like(inner.shape, bf16)], [inner])
     outer = new_outer
 
     other_outer = from_partner(outer, "aper", 4)
     other_edge = from_partner(edge, "aper", 4)
     other_inner = from_partner(inner, "aper", 4)
     acc = own("own2", 2, [(outer, (0, middle)), (inner, (middle, last)), (edge, (last, span)), (swap(edge), beyond)])
-    pieces = [(other_outer, (0, middle)), (other_inner, (middle, last)), (other_edge, (last, span))]
-    pieces += [(swap(step("copy2", copy_kernel, [edge_out], [other_edge])[0]), beyond)]
+    beyond_edge = swap(step("copy2", copy_kernel, [edge_out], [other_edge])[0])
     first = middle - HALO
-    ready = merge("f1", 2, [(other_outer, (0, middle))], 0, first, acc)
-    return merge("f2", 2, pieces, first, span, acc, ready=ready)[None]
+    ready = merge("f1", 2, [(other_outer, (0, middle)), (other_edge, (last, span))], 0, first, acc, mode="early")
+    pieces = [(other_inner, (middle, last)), (beyond_edge, beyond)]
+    return merge("f2", 2, pieces, first, span, acc, mode="last", ready=ready)[None]
 
 
 def solution(mesh):

time: 33.2 us -> 33.1 us (level)
    pallas_call x19 -> x20, Pallas kernels: 11 us -> 10.7 us  [run(): pl.pallas_call(without_token, out_shape=outs, in_specs=[VMEM] * len(args)...]
where the time goes in v7:
time: 33.1 us; the launch traced here: 32.9 us
  starting transfers between devices  11.4 us (34%)
  Pallas kernels  10.7 us (32%)
  waiting for transfers between devices  8.26 us (25%)
  local copies, waits for them, and re-layouts  2.22 us (7%)
    ppermute x12, starting transfers between devices, from_partner(): return lax.ppermute(value, axis, pairs)  11.4 us
    pallas_call x20, Pallas kernels, run(): pl.pallas_call(without_token, out_shape=outs, in_specs=[VMEM] * len(args)...  10.7 us
    ppermute x12, waiting for transfers between devices, from_partner(): return lax.ppermute(value, axis, pairs)  8.26 us
    unnamed x14, local copies, waits for them, and re-layouts  2.22 us
  transfers between devices with their start and end apart: 12, of which 6 were waited for; matrix products, arithmetic and copies ran while one was open for 0% of the time, Pallas kernels for 25%

profile of v7, /device:TPU:0, one launch (start us, length us, event | category | flops | bytes accessed | tf_op | source)
XLA Modules:
  0.0 32.9 jit_solution(16902061752419077927)
XLA Ops:
  0.0 2.9 %collective-permute-start = (bf16[2,512,128]{2,1,0:T(8,128)(2,1)}, bf16[2,512,128]{2,1,0:T(8,128)(2,1)S(1)}, u32[]{:S(2)}, u32[]{:S(2)}) collective-permute-start(bf16[2,512,128]{2,1,0:T(8,128)(2,1)} %bitcast.3), channel_id=1, source_target_pairs={{0,2},{2,0},{4,6},{6,4},{8,10},{10,8},{12,14},{14,12},{1,3},{3,1},... | collective-permute-start | bytes 786440 | tf_op jit(solution)/shard_map/ppermute | solution.py:53
  2.9 1.0 %copy-done.1 = bf16[1,2,512,128]{3,2,1,0:T(8,128)(2,1)S(1)} copy-done((bf16[1,2,512,128]{3,2,1,0:T(8,128)(2,1)S(1)}, bf16[1,2,512,128]{3,2,1,0:T(8,128)(2,1)}, u32[]{:S(2)}) %copy-start.1) | copy-done | bytes 262168
  3.9 0.0 copy-start.6
  3.9 0.1 turn0.1
  4.1 0.1 collective-permute-start.1
  4.2 0.0 copy-start
  4.2 1.2 %copy-done = bf16[1024,512]{1,0:T(8,128)(2,1)S(1)} copy-done((bf16[1024,512]{1,0:T(8,128)(2,1)S(1)}, bf16[1024,512]{1,0:T(8,128)(2,1)}, u32[]{:S(2)}) %copy-start) | copy-done | bytes 1048600
  5.4 0.3 halves.1.refs_2_.refs_1_.refs_3_.refs_4_
  5.7 0.0 copy-done.2
  5.7 0.0 copy-done.3
  5.7 0.0 copy-done.4
  5.7 0.0 copy-done.5
  5.8 0.7 %tables0.1 = (s32[1,2,4,8,128]{4,3,2,1,0:T(8,128)S(1)}, f32[1,2,4,9,8,128]{5,4,3,2,1,0:T(8,128)S(1)}, f32[1,2,2,4,128,128]{5,4,3,2,1,0:T(8,128)S(1)}) custom-call(s32[3,2,1024]{2,1,0:T(2,128)S(1)} %copy-done.2, s32[3,2,1024]{2,1,0:T(2,128)S(1)} %copy-done.3, f32[3,2,1024]{2,1,0:T(2,128)S(1)} %copy-done.4, f32[3,2,1024]{2,1,0:T(2,128)S(1)} %copy-done.5, ...), custom_call_target="tpu_custom_call" | custom-call | tf_op jit(solution)/shard_map/tables0/pallas_call | solution.py:38
  6.5 0.0 collective-permute-done.1.refs_1_
  6.5 1.0 %own0.1.refs_2_.refs_3_.refs_5_ = f32[2,4,128,128]{3,2,1,0:T(8,128)S(1)} custom-call(bf16[2,128,512]{2,1,0:T(8,128)(2,1)S(1)} %get-tuple-element.19.refs_0_, bf16[2,32,512]{2,1,0:T(8,128)(2,1)S(1)} %collective-permute-done.1.refs_1_, bf16[2,512,512]{2,1,0:T(8,128)(2,1)S(1)} %halves.1.refs_2_.refs_1_.refs_3_.refs_4_, ...), custom_call_target="tpu_custom_call" | custom-call | tf_op jit(solution)/shard_map/own0/pallas_call | solution.py:38
  7.5 2.0 %collective-permute-done.refs_0_ = bf16[2,512,128]{2,1,0:T(8,128)(2,1)S(1)} collective-permute-done((bf16[2,512,128]{2,1,0:T(8,128)(2,1)}, bf16[2,512,128]{2,1,0:T(8,128)(2,1)S(1)}, u32[]{:S(2)}, u32[]{:S(2)}) %collective-permute-start) | collective-permute-done | bytes 262176 | tf_op jit(solution)/shard_map/ppermute | solution.py:53
  9.5 0.1 turn1.1
  9.6 0.8 %m0o.1.refs_7_.refs_0_ = bf16[2,96,512]{2,1,0:T(8,128)(2,1)S(1)} custom-call(bf16[2,128,512]{2,1,0:T(8,128)(2,1)S(1)} %get-tuple-element.18.refs_0_, bf16[2,512,512]{2,1,0:T(8,128)(2,1)S(1)} %halves.1.refs_2_.refs_1_.refs_3_.refs_4_, f32[2,4,128,128]{3,2,1,0:T(8,128)S(1)} %own0.1.refs_2_.refs_3_.refs_5_, ...), custom_call_target="tpu_custom_call" | custom-call | tf_op jit(solution)/shard_map/m0o/pallas_call | solution.py:38
  10.4 1.9 %collective-permute-start.2 = (bf16[2,96,512]{2,1,0:T(8,128)(2,1)S(1)}, bf16[2,96,512]{2,1,0:T(8,128)(2,1)S(1)}, u32[]{:S(2)}, u32[]{:S(2)}) collective-permute-start(bf16[2,96,512]{2,1,0:T(8,128)(2,1)S(1)} %m0o.1.refs_7_.refs_0_), channel_id=1, source_target_pairs={{0,4},{2,6},{4,0},{6,2},{8,12},{10,14},{12,8},{14,10},{1,5},{3,7},... | collective-permute-start | bytes 589832 | tf_op jit(solution)/shard_map/ppermute | solution.py:53
  12.3 0.0 collective-permute-start.3
  12.3 1.3 %tables12.1 = (s32[2,2,4,8,128]{4,3,2,1,0:T(8,128)S(1)}, f32[2,2,4,9,8,128]{5,4,3,2,1,0:T(8,128)S(1)}, f32[2,2,2,4,128,128]{5,4,3,2,1,0:T(8,128)S(1)}) custom-call(s32[3,2,1024]{2,1,0:T(2,128)S(1)} %copy-done.2, s32[3,2,1024]{2,1,0:T(2,128)S(1)} %copy-done.3, f32[3,2,1024]{2,1,0:T(2,128)S(1)} %copy-done.4, f32[3,2,1024]{2,1,0:T(2,128)S(1)} %copy-done.5, ...), custom_call_target="tpu_custom_call" | custom-call | tf_op jit(solution)/shard_map/tables12/pallas_call | solution.py:38
  13.7 0.6 %own1a.1.refs_2_ = f32[2,4,64,128]{3,2,1,0:T(8,128)S(1)} custom-call(bf16[2,96,512]{2,1,0:T(8,128)(2,1)S(1)} %m0o.1.refs_7_.refs_0_, bf16[2,512,512]{2,1,0:T(8,128)(2,1)S(1)} %halves.1.refs_2_.refs_1_.refs_3_.refs_4_, s32[2,2,4,8,128]{4,3,2,1,0:T(8,128)S(1)} %get-tuple-element.25.refs_2_.refs_5_.refs_3_.refs_4_, ...), custom_call_target="tpu_custom_call" | custom-call | tf_op jit(solution)/shard_map/own1a/pallas_call | solution.py:38
  14.3 0.0 collective-permute-done.3.refs_1_
  14.3 0.5 %m0i.1.refs_0_.refs_1_ = bf16[2,32,512]{2,1,0:T(8,128)(2,1)S(1)} custom-call(bf16[2,128,512]{2,1,0:T(8,128)(2,1)S(1)} %get-tuple-element.18.refs_0_, bf16[2,32,512]{2,1,0:T(8,128)(2,1)S(1)} %collective-permute-done.3.refs_1_, bf16[2,512,512]{2,1,0:T(8,128)(2,1)S(1)} %halves.1.refs_2_.refs_1_.refs_3_.refs_4_, ...), custom_call_target="tpu_custom_call" | custom-call | tf_op jit(solution)/shard_map/m0i/pallas_call | solution.py:38
  14.8 0.3 collective-permute-start.4
  15.0 0.4 %collective-permute-start.5 = (bf16[2,32,512]{2,1,0:T(8,128)(2,1)S(1)}, bf16[2,32,512]{2,1,0:T(8,128)(2,1)S(1)}, u32[]{:S(2)}, u32[]{:S(2)}) collective-permute-start(bf16[2,32,512]{2,1,0:T(8,128)(2,1)S(1)} %edge1.1), channel_id=1, source_target_pairs={{0,1},{1,0},{2,3},{3,2},{4,5},{5,4},{6,7},{7,6},{8,9},{9,8},{10,11... | collective-permute-start | bytes 196616 | tf_op jit(solution)/shard_map/ppermute | solution.py:53
  15.4 1.1 %collective-permute-done.2.refs_0_ = bf16[2,96,512]{2,1,0:T(8,128)(2,1)S(1)} collective-permute-done((bf16[2,96,512]{2,1,0:T(8,128)(2,1)S(1)}, bf16[2,96,512]{2,1,0:T(8,128)(2,1)S(1)}, u32[]{:S(2)}, u32[]{:S(2)}) %collective-permute-start.2) | collective-permute-done | bytes 196640 | tf_op jit(solution)/shard_map/ppermute | solution.py:53
  16.6 0.6 %m1o.1.refs_7_.refs_1_.refs_0_ = bf16[2,64,512]{2,1,0:T(8,128)(2,1)S(1)} custom-call(bf16[2,96,512]{2,1,0:T(8,128)(2,1)S(1)} %collective-permute-done.2.refs_0_, bf16[2,512,512]{2,1,0:T(8,128)(2,1)S(1)} %halves.1.refs_2_.refs_1_.refs_3_.refs_4_, f32[2,4,64,128]{3,2,1,0:T(8,128)S(1)} %own1a.1.refs_2_, ...), custom_call_target="tpu_custom_call" | custom-call | flops 3000000000 | tf_op jit(solution)/shard_map/m1o/pallas_call | solution.py:38
  17.2 2.6 %collective-permute-start.11 = (bf16[2,64,512]{2,1,0:T(8,128)(2,1)S(1)}, bf16[2,64,512]{2,1,0:T(8,128)(2,1)S(1)}, u32[]{:S(2)}, u32[]{:S(2)}) collective-permute-start(bf16[2,64,512]{2,1,0:T(8,128)(2,1)S(1)} %m1o.1.refs_7_.refs_1_.refs_0_), channel_id=1, source_target_pairs={{0,8},{2,10},{4,12},{6,14},{8,0},{10,2},{12,4},{14,6},{1,9},{3,11}... | collective-permute-start | bytes 393224 | tf_op jit(solution)/shard_map/ppermute | solution.py:53
  19.7 0.0 collective-permute-done.4.refs_1_.refs_0_
  19.8 0.1 collective-permute-start.6
  19.8 0.0 collective-permute-done.5.refs_2_
  19.8 0.6 %own1b.1.refs_3_.refs_4_ = f32[2,4,64,128]{3,2,1,0:T(8,128)S(1)} custom-call(bf16[2,96,512]{2,1,0:T(8,128)(2,1)S(1)} %m0o.1.refs_7_.refs_0_, bf16[2,32,512]{2,1,0:T(8,128)(2,1)S(1)} %m0i.1.refs_0_.refs_1_, bf16[2,32,512]{2,1,0:T(8,128)(2,1)S(1)} %collective-permute-done.5.refs_2_, bf16[2,512,512]{2,1,0:T(8,128)(2,1)S(1)} %halves.1.refs_2_.refs_1_.refs_3_.refs_4_, ...), custom_call_target="tpu_custom_call" | custom-call | flops 3000000000 | tf_op jit(solution)/shard_map/own1b/pallas_call | solution.py:38
  20.5 0.6 %collective-permute-done.6.refs_2_ = bf16[2,32,512]{2,1,0:T(8,128)(2,1)S(1)} collective-permute-done((bf16[2,32,512]{2,1,0:T(8,128)(2,1)S(1)}, bf16[2,32,512]{2,1,0:T(8,128)(2,1)S(1)}, u32[]{:S(2)}, u32[]{:S(2)}) %collective-permute-start.6) | collective-permute-done | bytes 65568 | tf_op jit(solution)/shard_map/ppermute | solution.py:53
  21.1 0.5 %m1e.1.refs_1_.refs_2_ = bf16[2,32,512]{2,1,0:T(8,128)(2,1)S(1)} custom-call(bf16[2,96,512]{2,1,0:T(8,128)(2,1)S(1)} %collective-permute-done.2.refs_0_, bf16[2,32,512]{2,1,0:T(8,128)(2,1)S(1)} %collective-permute-done.4.refs_1_.refs_0_, bf16[2,32,512]{2,1,0:T(8,128)(2,1)S(1)} %collective-permute-done.6.refs_2_, ...), custom_call_target="tpu_custom_call" | custom-call | tf_op jit(solution)/shard_map/m1e/pallas_call | solution.py:38
  21.6 0.2 collective-permute-start.9
  21.8 2.5 %collective-permute-start.8 = (bf16[2,32,512]{2,1,0:T(8,128)(2,1)S(1)}, bf16[2,32,512]{2,1,0:T(8,128)(2,1)S(1)}, u32[]{:S(2)}, u32[]{:S(2)}) collective-permute-start(bf16[2,32,512]{2,1,0:T(8,128)(2,1)S(1)} %m1e.1.refs_1_.refs_2_), channel_id=1, source_target_pairs={{0,8},{2,10},{4,12},{6,14},{8,0},{10,2},{12,4},{14,6},{1,9},{3,11}... | collective-permute-start | bytes 196616 | tf_op jit(solution)/shard_map/ppermute | solution.py:53
  24.3 0.5 %m1i.1.refs_0_ = bf16[2,32,512]{2,1,0:T(8,128)(2,1)S(1)} custom-call(bf16[2,96,512]{2,1,0:T(8,128)(2,1)S(1)} %collective-permute-done.2.refs_0_, bf16[2,32,512]{2,1,0:T(8,128)(2,1)S(1)} %collective-permute-done.4.refs_1_.refs_0_, bf16[2,512,512]{2,1,0:T(8,128)(2,1)S(1)} %halves.1.refs_2_.refs_1_.refs_3_.refs_4_, f32[2,4,64,128]{3,2,1,0:T(8,128)S(1)} %own1b.1.refs_3_.refs_4_, ...), custom_call_target="tpu_custom_call" | custom-call | flops 3000000000 | tf_op jit(solution)/shard_map/m1i/pallas_call | solution.py:38
  24.8 0.5 %collective-permute-start.7 = (bf16[2,32,512]{2,1,0:T(8,128)(2,1)S(1)}, bf16[2,32,512]{2,1,0:T(8,128)(2,1)S(1)}, u32[]{:S(2)}, u32[]{:S(2)}) collective-permute-start(bf16[2,32,512]{2,1,0:T(8,128)(2,1)S(1)} %later.1.refs_1_), channel_id=1, source_target_pairs={{0,8},{2,10},{4,12},{6,14},{8,0},{10,2},{12,4},{14,6},{1,9},{3,11}... | collective-permute-start | bytes 196616 | tf_op jit(solution)/shard_map/ppermute | solution.py:53
  25.3 0.0 collective-permute-done.9.refs_3_
  25.3 1.0 %own2.1.refs_1_.refs_3_ = f32[2,4,128,128]{3,2,1,0:T(8,128)S(1)} custom-call(bf16[2,64,512]{2,1,0:T(8,128)(2,1)S(1)} %m1o.1.refs_7_.refs_1_.refs_0_, bf16[2,32,512]{2,1,0:T(8,128)(2,1)S(1)} %later.1.refs_1_, bf16[2,32,512]{2,1,0:T(8,128)(2,1)S(1)} %m1e.1.refs_1_.refs_2_, bf16[2,32,512]{2,1,0:T(8,128)(2,1)S(1)} %collective-permute-done.9.refs_3_, ...), custom_call_target="tpu_custom_call" | custom-call | tf_op jit(solution)/shard_map/own2/pallas_call | solution.py:38
  26.3 3.8 %collective-permute-done.8.refs_0_.refs_1_ = bf16[2,32,512]{2,1,0:T(8,128)(2,1)S(1)} collective-permute-done((bf16[2,32,512]{2,1,0:T(8,128)(2,1)S(1)}, bf16[2,32,512]{2,1,0:T(8,128)(2,1)S(1)}, u32[]{:S(2)}, u32[]{:S(2)}) %collective-permute-start.8) | collective-permute-done | bytes 65568 | tf_op jit(solution)/shard_map/ppermute | solution.py:53
  30.1 0.0 collective-permute-start.10
  30.1 0.0 collective-permute-done.11.refs_0_
  30.1 0.5 %f1.1 = (bf16[2,32,512]{2,1,0:T(8,128)(2,1)S(1)}, f32[2,4,192,128]{3,2,1,0:T(8,128)S(1)}) custom-call(bf16[2,64,512]{2,1,0:T(8,128)(2,1)S(1)} %collective-permute-done.11.refs_0_, bf16[2,32,512]{2,1,0:T(8,128)(2,1)S(1)} %collective-permute-done.8.refs_0_.refs_1_, bf16[2,512,512]{2,1,0:T(8,128)(2,1)S(1)} %halves.1.refs_2_.refs_1_.refs_3_.refs_4_, ...), custom_call_target="tpu_custom_call" | custom-call | tf_op jit(solution)/shard_map/f1/pallas_call | solution.py:38
  30.6 0.7 %collective-permute-done.7.refs_0_ = bf16[2,32,512]{2,1,0:T(8,128)(2,1)S(1)} collective-permute-done((bf16[2,32,512]{2,1,0:T(8,128)(2,1)S(1)}, bf16[2,32,512]{2,1,0:T(8,128)(2,1)S(1)}, u32[]{:S(2)}, u32[]{:S(2)}) %collective-permute-start.7) | collective-permute-done | bytes 65568 | tf_op jit(solution)/shard_map/ppermute | solution.py:53
  31.2 0.1 collective-permute-done.10.refs_1_
  31.3 1.6 %f2.1 = (bf16[2,512,128]{2,1,0:T(8,128)(2,1)}, f32[2,4,192,128]{3,2,1,0:T(8,128)S(1)}) custom-call(bf16[2,32,512]{2,1,0:T(8,128)(2,1)S(1)} %collective-permute-done.7.refs_0_, bf16[2,32,512]{2,1,0:T(8,128)(2,1)S(1)} %collective-permute-done.10.refs_1_, ...), custom_call_target="tpu_custom_call", output_to_operand_aliasing={{1}: (8, {})} | custom-call | tf_op jit(solution)/shard_map/f2/pallas_call | solution.py:38
  (10 shorter events, 0.0 us)
Async XLA Ops:
  0.0 9.5 %collective-permute-start = (bf16[2,512,128]{2,1,0:T(8,128)(2,1)}, bf16[2,512,128]{2,1,0:T(8,128)(2,1)S(1)}, u32[]{:S(2)}, u32[]{:S(2)}) collective-permute-start(bf16[2,512,128]{2,1,0:T(8,128)(2,1)} %bitcast.3), channel_id=1, source_target_pairs={{0,2},{2,0},{4,6},{6,4},{8,10},{10,8},{12,14},{14,12},{1,3},{3,1},... | collective-permute-start | bytes 786440 | tf_op jit(solution)/shard_map/ppermute | solution.py:53
  2.9 1.0 %copy-start.1 = (bf16[1,2,512,128]{3,2,1,0:T(8,128)(2,1)S(1)}, bf16[1,2,512,128]{3,2,1,0:T(8,128)(2,1)}, u32[]{:S(2)}) copy-start(bf16[1,2,512,128]{3,2,1,0:T(8,128)(2,1)} %param.7) | copy-start | bytes 786436
  3.9 1.8 %copy-start.2 = (s32[3,2,1024]{2,1,0:T(2,128)S(1)}, s32[3,2,1024]{2,1,0:T(2,128)}, u32[]{:S(2)}) copy-start(s32[3,2,1024]{2,1,0:T(2,128)} %refs_0_.5) | copy-start | bytes 73732
  3.9 1.8 %copy-start.3 = (s32[3,2,1024]{2,1,0:T(2,128)S(1)}, s32[3,2,1024]{2,1,0:T(2,128)}, u32[]{:S(2)}) copy-start(s32[3,2,1024]{2,1,0:T(2,128)} %refs_1_.3) | copy-start | bytes 73732
  3.9 1.8 %copy-start.4 = (f32[3,2,1024]{2,1,0:T(2,128)S(1)}, f32[3,2,1024]{2,1,0:T(2,128)}, u32[]{:S(2)}) copy-start(f32[3,2,1024]{2,1,0:T(2,128)} %refs_2_.3) | copy-start | bytes 73732
  3.9 1.8 %copy-start.5 = (f32[3,2,1024]{2,1,0:T(2,128)S(1)}, f32[3,2,1024]{2,1,0:T(2,128)}, u32[]{:S(2)}) copy-start(f32[3,2,1024]{2,1,0:T(2,128)} %refs_3_.3) | copy-start | bytes 73732
  3.9 1.8 %copy-start.6 = (f32[16,8]{0,1:T(8,128)S(1)}, f32[16,8]{0,1:T(8,128)}, u32[]{:S(2)}) copy-start(f32[16,8]{0,1:T(8,128)} %param.11) | copy-start | bytes 1540
  4.1 2.4 %collective-permute-start.1 = (bf16[2,32,512]{2,1,0:T(8,128)(2,1)S(1)}, bf16[2,32,512]{2,1,0:T(8,128)(2,1)S(1)}, u32[]{:S(2)}, u32[]{:S(2)}) collective-permute-start(bf16[2,32,512]{2,1,0:T(8,128)(2,1)S(1)} %get-tuple-element.20), channel_id=1, source_target_pairs={{0,1},{1,0},{2,3},{3,2},{4,5},{5,4},{6,7},{7,6},{8,9},{9,8},{10,11... | collective-permute-start | bytes 196616 | tf_op jit(solution)/shard_map/ppermute | solution.py:53
  4.2 1.2 %copy-start = (bf16[1024,512]{1,0:T(8,128)(2,1)S(1)}, bf16[1024,512]{1,0:T(8,128)(2,1)}, u32[]{:S(2)}) copy-start(bf16[1024,512]{1,0:T(8,128)(2,1)} %refs_0_.3) | copy-start | bytes 3145732
  10.4 6.2 %collective-permute-start.2 = (bf16[2,96,512]{2,1,0:T(8,128)(2,1)S(1)}, bf16[2,96,512]{2,1,0:T(8,128)(2,1)S(1)}, u32[]{:S(2)}, u32[]{:S(2)}) collective-permute-start(bf16[2,96,512]{2,1,0:T(8,128)(2,1)S(1)} %m0o.1.refs_7_.refs_0_), channel_id=1, source_target_pairs={{0,4},{2,6},{4,0},{6,2},{8,12},{10,14},{12,8},{14,10},{1,5},{3,7},... | collective-permute-start | bytes 589832 | tf_op jit(solution)/shard_map/ppermute | solution.py:53
  12.3 2.0 %collective-permute-start.3 = (bf16[2,32,512]{2,1,0:T(8,128)(2,1)S(1)}, bf16[2,32,512]{2,1,0:T(8,128)(2,1)S(1)}, u32[]{:S(2)}, u32[]{:S(2)}) collective-permute-start(bf16[2,32,512]{2,1,0:T(8,128)(2,1)S(1)} %get-tuple-element.24), channel_id=1, source_target_pairs={{0,1},{1,0},{2,3},{3,2},{4,5},{5,4},{6,7},{7,6},{8,9},{9,8},{10,11... | collective-permute-start | bytes 196616 | tf_op jit(solution)/shard_map/ppermute | solution.py:53
  14.8 5.0 %collective-permute-start.4 = (bf16[2,32,512]{2,1,0:T(8,128)(2,1)S(1)}, bf16[2,32,512]{2,1,0:T(8,128)(2,1)S(1)}, u32[]{:S(2)}, u32[]{:S(2)}) collective-permute-start(bf16[2,32,512]{2,1,0:T(8,128)(2,1)S(1)} %m0i.1.refs_0_.refs_1_), channel_id=1, source_target_pairs={{0,4},{2,6},{4,0},{6,2},{8,12},{10,14},{12,8},{14,10},{1,5},{3,7},... | collective-permute-start | bytes 196616 | tf_op jit(solution)/shard_map/ppermute | solution.py:53
  15.0 4.8 %collective-permute-start.5 = (bf16[2,32,512]{2,1,0:T(8,128)(2,1)S(1)}, bf16[2,32,512]{2,1,0:T(8,128)(2,1)S(1)}, u32[]{:S(2)}, u32[]{:S(2)}) collective-permute-start(bf16[2,32,512]{2,1,0:T(8,128)(2,1)S(1)} %edge1.1), channel_id=1, source_target_pairs={{0,1},{1,0},{2,3},{3,2},{4,5},{5,4},{6,7},{7,6},{8,9},{9,8},{10,11... | collective-permute-start | bytes 196616 | tf_op jit(solution)/shard_map/ppermute | solution.py:53
  17.2 12.9 %collective-permute-start.11 = (bf16[2,64,512]{2,1,0:T(8,128)(2,1)S(1)}, bf16[2,64,512]{2,1,0:T(8,128)(2,1)S(1)}, u32[]{:S(2)}, u32[]{:S(2)}) collective-permute-start(bf16[2,64,512]{2,1,0:T(8,128)(2,1)S(1)} %m1o.1.refs_7_.refs_1_.refs_0_), channel_id=1, source_target_pairs={{0,8},{2,10},{4,12},{6,14},{8,0},{10,2},{12,4},{14,6},{1,9},{3,11}... | collective-permute-start | bytes 393224 | tf_op jit(solution)/shard_map/ppermute | solution.py:53
  19.8 1.3 %collective-permute-start.6 = (bf16[2,32,512]{2,1,0:T(8,128)(2,1)S(1)}, bf16[2,32,512]{2,1,0:T(8,128)(2,1)S(1)}, u32[]{:S(2)}, u32[]{:S(2)}) collective-permute-start(bf16[2,32,512]{2,1,0:T(8,128)(2,1)S(1)} %copy1.1), channel_id=1, source_target_pairs={{0,1},{1,0},{2,3},{3,2},{4,5},{5,4},{6,7},{7,6},{8,9},{9,8},{10,11... | collective-permute-start | bytes 196616 | tf_op jit(solution)/shard_map/ppermute | solution.py:53
  21.6 3.7 %collective-permute-start.9 = (bf16[2,32,512]{2,1,0:T(8,128)(2,1)S(1)}, bf16[2,32,512]{2,1,0:T(8,128)(2,1)S(1)}, u32[]{:S(2)}, u32[]{:S(2)}) collective-permute-start(bf16[2,32,512]{2,1,0:T(8,128)(2,1)S(1)} %m1e.1.refs_1_.refs_2_), channel_id=1, source_target_pairs={{0,1},{1,0},{2,3},{3,2},{4,5},{5,4},{6,7},{7,6},{8,9},{9,8},{10,11... | collective-permute-start | bytes 196616 | tf_op jit(solution)/shard_map/ppermute | solution.py:53
  21.8 8.3 %collective-permute-start.8 = (bf16[2,32,512]{2,1,0:T(8,128)(2,1)S(1)}, bf16[2,32,512]{2,1,0:T(8,128)(2,1)S(1)}, u32[]{:S(2)}, u32[]{:S(2)}) collective-permute-start(bf16[2,32,512]{2,1,0:T(8,128)(2,1)S(1)} %m1e.1.refs_1_.refs_2_), channel_id=1, source_target_pairs={{0,8},{2,10},{4,12},{6,14},{8,0},{10,2},{12,4},{14,6},{1,9},{3,11}... | collective-permute-start | bytes 196616 | tf_op jit(solution)/shard_map/ppermute | solution.py:53
  24.8 6.5 %collective-permute-start.7 = (bf16[2,32,512]{2,1,0:T(8,128)(2,1)S(1)}, bf16[2,32,512]{2,1,0:T(8,128)(2,1)S(1)}, u32[]{:S(2)}, u32[]{:S(2)}) collective-permute-start(bf16[2,32,512]{2,1,0:T(8,128)(2,1)S(1)} %later.1.refs_1_), channel_id=1, source_target_pairs={{0,8},{2,10},{4,12},{6,14},{8,0},{10,2},{12,4},{14,6},{1,9},{3,11}... | collective-permute-start | bytes 196616 | tf_op jit(solution)/shard_map/ppermute | solution.py:53
  30.1 1.3 %collective-permute-start.10 = (bf16[2,32,512]{2,1,0:T(8,128)(2,1)S(1)}, bf16[2,32,512]{2,1,0:T(8,128)(2,1)S(1)}, u32[]{:S(2)}, u32[]{:S(2)}) collective-permute-start(bf16[2,32,512]{2,1,0:T(8,128)(2,1)S(1)} %copy2.1), channel_id=1, source_target_pairs={{0,1},{1,0},{2,3},{3,2},{4,5},{5,4},{6,7},{7,6},{8,9},{9,8},{10,11... | collective-permute-start | bytes 196616 | tf_op jit(solution)/shard_map/ppermute | solution.py:53
